TPU v7x, 32 devices: a whole 2x2x4 slice. The times are simulated.
32 devices in a mesh: batch: 2 (over x), row: 4 (over z), col: 4 (over y, core).
Axes of the slice: x: 2, y: 2, z: 4, core: 2. Of those that a mesh axis runs over, the one named last changes fastest.
Arguments:
- low_map: bfloat16 [8, 64, 64, 64], P('batch', 'row', 'col')
- skip_map: bfloat16 [8, 128, 128, 64], P('batch', 'row', 'col')
- conv_first: bfloat16 [3, 3, 64, 64], replicated, may hold values from -0.25 to 0.25
- gain_first: float32 [64], replicated, may hold values from 0.5 to 1.5
- shift_first: float32 [64], replicated, may hold values from -0.5 to 0.5
- conv_second: bfloat16 [3, 3, 64, 64], replicated, may hold values from -0.25 to 0.25
- gain_second: float32 [64], replicated, may hold values from 0.5 to 1.5
- shift_second: float32 [64], replicated, may hold values from -0.5 to 0.5
- head_conv: bfloat16 [3, 3, 64, 768], replicated, may hold values from -0.25 to 0.25
- head_bias: float32 [768], replicated, may hold values from -3 to 3
- heat_weight: bfloat16 [256, 80], replicated, may hold values from -0.375 to 0.375
- heat_bias: float32 [80], replicated, may hold values from -3 to -1.4
- box_weight: bfloat16 [2, 256, 2], replicated, may hold values from -0.375 to 0.375
- box_bias: float32 [2, 2], replicated, may hold values from -3 to 3
- heat_target: bfloat16 [8, 128, 128, 80], P('batch', 'row', 'col'), as said below
- box_target: float32 [8, 128, 4], P('batch'), may hold values from -6 to 6
- obj_index: int32 [8, 128], P('batch'), may hold values from 0 to 16383, as said below
- obj_count: int32 [8], P('batch'), may hold values from 0 to 128, as said below
Outputs:
- heat_map: float32 [8, 128, 128, 80], P('batch', 'row', 'col')
- box_map: float32 [8, 128, 128, 4], P('batch', 'row', 'col')
- grad_low: float32 [8, 64, 64, 64], P('batch', 'row', 'col')
- grad_skip: float32 [8, 128, 128, 64], P('batch', 'row', 'col')
- grad_conv_first: float32 [3, 3, 64, 64], replicated
- grad_gain_first: float32 [64], replicated
- grad_shift_first: float32 [64], replicated
- grad_conv_second: float32 [3, 3, 64, 64], replicated
- grad_gain_second: float32 [64], replicated
- grad_shift_second: float32 [64], replicated
- grad_head_conv: float32 [3, 3, 64, 768], replicated
- grad_head_bias: float32 [768], replicated
- grad_heat_weight: float32 [256, 80], replicated
- grad_heat_bias: float32 [80], replicated
- grad_box_weight: float32 [2, 256, 2], replicated
- grad_box_bias: float32 [2, 2], replicated
Inputs may be any that keep to these rules, and one draw needn't show every extreme that they name: `obj_index`: for image b the first obj_count[b] entries are distinct cells row * 128 + column; the other entries are 0. `obj_count`: some image has 128 objects and some other image has none. `heat_target`: at least one entry equals 1; every other entry is below 0.96.
All inputs are finite; a program needn't handle non-finite values.
Results may differ from a plain program's by a relative error of at most 0.015.
Values may be sent and summed in bfloat16 or wider, within the bound.
A program may use at most 128 MiB of HBM per device.

v0:
```python
import jax
import jax.numpy as jnp
from jax import lax
from jax.sharding import PartitionSpec as P

EPSILON = 1e-05


def extended(block, sides, width):
    for axis, dim in sides:
        count = lax.axis_size(axis)
        forward = [(i, i + 1) for i in range(count - 1)]
        backward = [(target, source) for source, target in forward]
        low = lax.ppermute(
            lax.slice_in_dim(block, block.shape[dim] - width, None, axis=dim), axis, forward
        )
        high = lax.ppermute(lax.slice_in_dim(block, 0, width, axis=dim), axis, backward)
        block = jnp.concatenate([low, block, high], axis=dim)
    return block


def silu_slope(values):
    logistic = jax.nn.sigmoid(values)
    return logistic * (1.0 + values * (1.0 - logistic))


def patches(padded, height, breadth):
    pieces = []
    for row_tap in range(3):
        for col_tap in range(3):
            pieces.append(padded[:, row_tap : row_tap + height, col_tap : col_tap + breadth, :])
    return jnp.concatenate(pieces, axis=-1)


def convolve(padded, kernel, height, breadth):
    matrix = kernel.reshape(-1, kernel.shape[-1])
    return jnp.dot(patches(padded, height, breadth), matrix, preferred_element_type=jnp.float32)


def transpose_conv(padded_grad, kernel, height, breadth):
    result = None
    for row_tap in range(3):
        for col_tap in range(3):
            window = padded_grad[
                :, 2 - row_tap : 2 - row_tap + height, 2 - col_tap : 2 - col_tap + breadth, :
            ]
            term = jnp.dot(window, kernel[row_tap, col_tap].T, preferred_element_type=jnp.float32)
            result = term if result is None else result + term
    return result


def kernel_grad(padded, grad_out, height, breadth, target_shape):
    product = jnp.einsum(
        "brqk,brqo->ko",
        patches(padded, height, breadth),
        grad_out,
        preferred_element_type=jnp.float32,
    )
    return product.reshape(target_shape)


def upsample(padded, axis):
    length = padded.shape[axis] - 2
    before = lax.slice_in_dim(padded, 0, length, axis=axis)
    middle = lax.slice_in_dim(padded, 1, length + 1, axis=axis)
    behind = lax.slice_in_dim(padded, 2, length + 2, axis=axis)
    even_rows = 0.75 * middle + 0.25 * before
    odd_rows = 0.75 * middle + 0.25 * behind
    stacked = jnp.stack([even_rows, odd_rows], axis=axis + 1)
    new_shape = list(middle.shape)
    new_shape[axis] = 2 * length
    return stacked.reshape(new_shape)


def narrow(padded, axis):
    length = padded.shape[axis] - 2
    inner = lax.slice_in_dim(padded, 1, length + 1, axis=axis)
    pair_shape = list(inner.shape)
    pair_shape[axis] = length // 2
    pair_shape.insert(axis + 1, 2)
    paired = jnp.sum(inner.reshape(pair_shape), axis=axis + 1)
    before = lax.slice_in_dim(padded, 0, length, stride=2, axis=axis)
    behind = lax.slice_in_dim(padded, 3, length + 2, stride=2, axis=axis)
    return 0.75 * paired + 0.25 * (before + behind)


def local(
    low_map,
    skip_map,
    conv_first,
    gain_first,
    shift_first,
    conv_second,
    gain_second,
    shift_second,
    head_conv,
    head_bias,
    heat_weight,
    heat_bias,
    box_weight,
    box_bias,
    heat_target,
    box_target,
    obj_index,
    obj_count,
):
    images = low_map.shape[0]
    low_height = low_map.shape[1]
    low_breadth = low_map.shape[2]
    height = skip_map.shape[1]
    breadth = skip_map.shape[2]
    row_place = lax.axis_index("row")
    col_place = lax.axis_index("col")
    low_rows_all = low_height * lax.axis_size("row")
    low_cols_all = low_breadth * lax.axis_size("col")
    cells_low = float(images * lax.axis_size("batch") * low_rows_all * low_cols_all)
    cells_high = 4.0 * cells_low
    reduce_axes = (0, 1, 2)
    low_padded = extended(low_map, (("row", 1), ("col", 2)), 2)
    y_cycle = convolve(low_padded, conv_first, low_height + 2, low_breadth + 2)
    y_one = y_cycle[:, 1:-1, 1:-1, :]
    positive_local = jnp.sum((heat_target == 1.0).astype(jnp.float32))
    leading = jnp.logical_and(row_place == 0, col_place == 0)
    object_local = jnp.where(leading, jnp.sum(obj_count).astype(jnp.float32), 0.0)
    first_sum, first_square, totals = lax.psum(
        (
            jnp.sum(y_one, axis=reduce_axes),
            jnp.sum(y_one * y_one, axis=reduce_axes),
            jnp.stack([positive_local, object_local]),
        ),
        ("batch", "row", "col"),
    )
    mean_one = first_sum / cells_low
    scale_one = lax.rsqrt(first_square / cells_low - mean_one * mean_one + EPSILON)
    normed_cycle = (y_cycle - mean_one) * scale_one
    z_cycle = normed_cycle * gain_first + shift_first
    cycle_rows = row_place * low_height - 1 + jnp.arange(low_height + 2)
    cycle_cols = col_place * low_breadth - 1 + jnp.arange(low_breadth + 2)
    inside = jnp.logical_and(
        jnp.logical_and(cycle_rows >= 0, cycle_rows < low_rows_all)[:, None],
        jnp.logical_and(cycle_cols >= 0, cycle_cols < low_cols_all)[None, :],
    )
    act_one = jnp.where(inside[None, :, :, None], jax.nn.silu(z_cycle), 0.0).astype(jnp.bfloat16)
    up_map = upsample(upsample(act_one.astype(jnp.float32), 1), 2)
    merged = (up_map + skip_map.astype(jnp.float32)).astype(jnp.bfloat16)
    merged_padded = extended(merged, (("row", 1), ("col", 2)), 1)
    y_two = convolve(merged_padded, conv_second, height, breadth)
    second_sum, second_square = lax.psum(
        (jnp.sum(y_two, axis=reduce_axes), jnp.sum(y_two * y_two, axis=reduce_axes)),
        ("batch", "row", "col"),
    )
    mean_two = second_sum / cells_high
    scale_two = lax.rsqrt(second_square / cells_high - mean_two * mean_two + EPSILON)
    normed_two = (y_two - mean_two) * scale_two
    z_two = normed_two * gain_second + shift_second
    feature = jax.nn.silu(z_two).astype(jnp.bfloat16)
    feature_padded = extended(feature, (("row", 1), ("col", 2)), 1)
    feature_patches = patches(feature_padded, height, breadth)
    head_matrix = head_conv.reshape(-1, head_conv.shape[-1])
    hidden = jnp.dot(feature_patches, head_matrix, preferred_element_type=jnp.float32) + head_bias
    active = jax.nn.silu(hidden).astype(jnp.bfloat16)
    units = heat_weight.shape[0]
    heat_units = active[..., :units]
    size_units = active[..., units : 2 * units]
    offset_units = active[..., 2 * units :]
    logit = jnp.dot(heat_units, heat_weight, preferred_element_type=jnp.float32) + heat_bias
    size_out = jnp.dot(size_units, box_weight[0], preferred_element_type=jnp.float32) + box_bias[0]
    offset_out = (
        jnp.dot(offset_units, box_weight[1], preferred_element_type=jnp.float32) + box_bias[1]
    )
    box_out = jnp.concatenate([size_out, offset_out], axis=-1)
    slot_total = obj_index.shape[1]
    map_side = height * lax.axis_size("row")
    obj_rows = obj_index // map_side - row_place * height
    obj_cols = obj_index % map_side - col_place * breadth
    present = jnp.arange(slot_total)[None, :] < obj_count[:, None]
    in_tile = jnp.logical_and(
        jnp.logical_and(obj_rows >= 0, obj_rows < height),
        jnp.logical_and(obj_cols >= 0, obj_cols < breadth),
    )
    hit = jnp.logical_and(present, in_tile)
    spot = obj_rows * breadth + obj_cols
    picker = jnp.logical_and(
        spot[..., None] == jnp.arange(height * breadth), hit[..., None]
    ).astype(jnp.float32)
    hit_weight = hit.astype(jnp.float32)[..., None]
    target = heat_target.astype(jnp.float32)
    positive = heat_target == 1.0
    positives = totals[0]
    objects = totals[1]

    def local_loss(logit_in, box_in):
        chance = jax.nn.sigmoid(logit_in)
        focal_term = jnp.where(
            positive,
            (1.0 - chance) ** 2 * jax.nn.softplus(-logit_in),
            (1.0 - target) ** 4 * chance**2 * jax.nn.softplus(logit_in),
        )
        picked = jnp.einsum(
            "bkp,bpc->bkc",
            picker,
            box_in.reshape(images, height * breadth, 4),
            precision=lax.Precision.HIGHEST,
        )
        distance = (jnp.sqrt((picked - box_target) ** 2 + 1.0) - 1.0) * hit_weight
        return jnp.sum(focal_term) / positives + (
            0.1 * jnp.sum(distance[..., :2]) + jnp.sum(distance[..., 2:])
        ) / (2.0 * objects)

    loss_value, pullback = jax.vjp(local_loss, logit, box_out)
    grad_logit, grad_box = pullback(jnp.ones_like(loss_value))
    logit_low = grad_logit.astype(jnp.bfloat16)
    box_low = grad_box.astype(jnp.bfloat16)
    heat_w_grad = jnp.einsum(
        "brqh,brqc->hc", heat_units, logit_low, preferred_element_type=jnp.float32
    )
    heat_b_grad = jnp.sum(logit_low.astype(jnp.float32), axis=reduce_axes)
    box_w_grad = jnp.stack(
        [
            jnp.einsum(
                "brqh,brqc->hc", size_units, box_low[..., :2], preferred_element_type=jnp.float32
            ),
            jnp.einsum(
                "brqh,brqc->hc", offset_units, box_low[..., 2:], preferred_element_type=jnp.float32
            ),
        ]
    )
    box_b_grad = jnp.stack(
        [
            jnp.sum(box_low[..., :2].astype(jnp.float32), axis=reduce_axes),
            jnp.sum(box_low[..., 2:].astype(jnp.float32), axis=reduce_axes),
        ]
    )
    grad_active = jnp.concatenate(
        [
            jnp.dot(logit_low, heat_weight.T, preferred_element_type=jnp.float32),
            jnp.dot(box_low[..., :2], box_weight[0].T, preferred_element_type=jnp.float32),
            jnp.dot(box_low[..., 2:], box_weight[1].T, preferred_element_type=jnp.float32),
        ],
        axis=-1,
    )
    grad_hidden = (grad_active * silu_slope(hidden)).astype(jnp.bfloat16)
    head_w_grad = jnp.einsum(
        "brqk,brqo->ko", feature_patches, grad_hidden, preferred_element_type=jnp.float32
    ).reshape(head_conv.shape)
    head_b_grad = jnp.sum(grad_hidden.astype(jnp.float32), axis=reduce_axes)
    hidden_padded = extended(grad_hidden, (("row", 1), ("col", 2)), 1)
    grad_feature = transpose_conv(hidden_padded, head_conv, height, breadth)
    grad_z_two = grad_feature * silu_slope(z_two)
    shift_two_grad, gain_two_grad = lax.psum(
        (jnp.sum(grad_z_two, axis=reduce_axes), jnp.sum(grad_z_two * normed_two, axis=reduce_axes)),
        ("batch", "row", "col"),
    )
    grad_y_two = (
        gain_second
        * scale_two
        * (grad_z_two - shift_two_grad / cells_high - normed_two * gain_two_grad / cells_high)
    ).astype(jnp.bfloat16)
    conv_two_grad = kernel_grad(merged_padded, grad_y_two, height, breadth, conv_second.shape)
    grad_two_padded = extended(grad_y_two, (("row", 1), ("col", 2)), 1)
    grad_merged = transpose_conv(grad_two_padded, conv_second, height, breadth)
    up_padded = extended(grad_merged.astype(jnp.bfloat16), (("row", 1), ("col", 2)), 1).astype(
        jnp.float32
    )
    grad_act_one = narrow(narrow(up_padded, 1), 2)
    grad_z_one = grad_act_one * silu_slope(z_cycle[:, 1:-1, 1:-1, :])
    normed_one = normed_cycle[:, 1:-1, 1:-1, :]
    shift_one_grad, gain_one_grad = lax.psum(
        (jnp.sum(grad_z_one, axis=reduce_axes), jnp.sum(grad_z_one * normed_one, axis=reduce_axes)),
        ("batch", "row", "col"),
    )
    grad_y_one = (
        gain_first
        * scale_one
        * (grad_z_one - shift_one_grad / cells_low - normed_one * gain_one_grad / cells_low)
    ).astype(jnp.bfloat16)
    conv_one_grad = kernel_grad(
        low_padded[:, 1:-1, 1:-1, :], grad_y_one, low_height, low_breadth, conv_first.shape
    )
    grad_one_padded = extended(grad_y_one, (("row", 1), ("col", 2)), 1)
    grad_low = transpose_conv(grad_one_padded, conv_first, low_height, low_breadth)
    summed = lax.psum(
        (
            conv_one_grad,
            conv_two_grad,
            head_w_grad,
            head_b_grad,
            heat_w_grad,
            heat_b_grad,
            box_w_grad,
            box_b_grad,
        ),
        ("batch", "row", "col"),
    )
    return (
        jax.nn.sigmoid(logit),
        box_out,
        grad_low,
        grad_merged,
        summed[0],
        gain_one_grad,
        shift_one_grad,
        summed[1],
        gain_two_grad,
        shift_two_grad,
        summed[2],
        summed[3],
        summed[4],
        summed[5],
        summed[6],
        summed[7],
    )


def solution(mesh):
    return jax.shard_map(
        local,
        mesh=mesh,
        in_specs=(
            P("batch", "row", "col", None),
            P("batch", "row", "col", None),
            P(),
            P(),
            P(),
            P(),
            P(),
            P(),
            P(),
            P(),
            P(),
            P(),
            P(),
            P(),
            P("batch", "row", "col", None),
            P("batch", None, None),
            P("batch", None),
            P("batch"),
        ),
        out_specs=(
            P("batch", "row", "col", None),
            P("batch", "row", "col", None),
            P("batch", "row", "col", None),
            P("batch", "row", "col", None),
            P(),
            P(),
            P(),
            P(),
            P(),
            P(),
            P(),
            P(),
            P(),
            P(),
            P(),
            P(),
        ),
        check_vma=False,
    )
```

profile of v0, /device:TPU:0, one launch (start us, length us, event | category | flops | bytes accessed | tf_op | source)
XLA Modules:
  0.0 607.4 jit_solution(1820912576200839581)
XLA Ops:
  9.3 5.6 collective-permute-start
  33.6 4.2 concatenate.157
  39.7 42.6 %all-reduce.5 = (f32[64]{0:T(128)S(1)}, f32[64]{0:T(128)S(1)}) all-reduce(f32[64]{0:T(128)S(1)} %get-tuple-element.29, f32[64]{0:T(128)S(1)} %get-tuple-element.28), channel_id=1, replica_groups=mesh['batch'=2,'row'=4,'col'=4] {'batch','row','col'}, use_global_device_ids=true, to_apply=%region_3.4 | all-reduce | flops 128 | bytes 1024 | tf_op jit(solution)/shard_map/psum | solution.py:125
  93.8 3.6 concatenate.191
  98.9 3.3 collective-permute-start.6
  108.6 11.8 %concatenate.163 = bf16[4,32,32,576]{3,2,1,0:T(8,128)(2,1)} concatenate(bf16[4,32,32,64]{3,2,1,0:T(8,128)(2,1)} %get-tuple-element.79, bf16[4,32,32,64]{3,2,1,0:T(8,128)(2,1)S(1)} %get-tuple-element.105, bf16[4,32,32,64]{3,2,1,0:T(8,128)(2,1)} %get-tuple-element.76, bf16[4,32,32,64]{3,2,1,0:T(8,128)(2,1)} %get-tuple-element.78, bf16[4,32,32,64]{3,2,1,0:T(8,128)(2,1)S(1)} %add_convert_fusion, ...), dimensions={3} | concatenate | bytes 9437184 | tf_op jit(solution)/shard_map/concatenate | solution.py:32
  120.4 4.1 fusion.256
  124.5 43.0 %all-reduce.4 = (f32[64]{0:T(128)S(1)}, f32[64]{0:T(128)S(1)}, f32[2]{0:T(128)S(1)}) all-reduce(f32[64]{0:T(128)S(1)} %get-tuple-element.27, f32[64]{0:T(128)S(1)} %get-tuple-element.26, f32[2]{0:T(128)S(1)} %copy-done.36), channel_id=1, replica_groups=mesh['batch'=2,'row'=4,'col'=4] {'batch','row','col'}, use_global_device_ids=true, to_apply=%region_7.8 | all-reduce | flops 130 | bytes 1040 | tf_op jit(solution)/shard_map/psum | solution.py:148
  168.8 3.7 collective-permute-start.8
  179.8 3.6 collective-permute-start.10
  190.1 11.9 %concatenate.169 = bf16[4,32,32,576]{3,2,1,0:T(8,128)(2,1)} concatenate(bf16[4,32,32,64]{3,2,1,0:T(8,128)(2,1)} %get-tuple-element.73, bf16[4,32,32,64]{3,2,1,0:T(8,128)(2,1)} %get-tuple-element.101, bf16[4,32,32,64]{3,2,1,0:T(8,128)(2,1)} %get-tuple-element.70, bf16[4,32,32,64]{3,2,1,0:T(8,128)(2,1)} %get-tuple-element.72, bf16[4,32,32,64]{3,2,1,0:T(8,128)(2,1)S(1)} %multiply_convert_fusion.2, ...), dimensions={3} | concatenate | bytes 9437184 | tf_op jit(solution)/shard_map/concatenate | solution.py:32
  202.0 11.2 %multiply_convert_fusion = (bf16[4,32,32,768]{3,2,1,0:T(8,128)(2,1)S(1)}, f32[4,32,32,768]{3,2,1,0:T(8,128)}) fusion(f32[768]{0:T(1024)S(1)} %copy-done.19, bf16[4,32,32,576]{3,2,1,0:T(8,128)(2,1)} %concatenate.169, bf16[576,768,1,1]{1,0,3,2:T(8,128)(2,1)} %bitcast.319), kind=kOutput, calls=%fused_computation.3 | convolution fusion | flops 3642753024 | bytes 24480768 | tf_op jit(solution)/shard_map/dot_general | solution.py:160
  225.8 8.9 %convert_reduce_fusion.1 = (f32[80]{0:T(128)}, bf16[4,32,32,80]{3,2,1,0:T(8,128)(2,1)S(1)}, f32[4,32,32,80]{3,2,1,0:T(8,128)}) fusion(f32[80]{0:T(128)S(1)} %copy-done.34, f32[]{:T(128)} %bitcast.25, bf16[4,32,32,80]{3,2,1,0:T(8,128)(2,1)S(1)} %copy-done.8, bf16[256,80]{0,1:T(8,128)(2,1)S(1)} %copy-done, bf16[4,32,32,768]{3,2,1,0:T(8,128)(2,1)} %copy-done.38), kind=kOutput, calls=%fused_computation.66 | convolution fusion | flops 187432880 | bytes 4760704 | tf_op jit(solution)/shard_map/dot_general | solution.py:166
  238.1 8.1 %convert_reduce_fusion = (f32[768]{0:T(1024)S(1)}, bf16[4,32,32,768]{3,2,1,0:T(8,128)(2,1)S(1)}) fusion(f32[4,32,32,768]{3,2,1,0:T(8,128)} %get-tuple-element.156, f32[768]{0:T(1024)S(1)} %copy-done.19, f32[4,32,32,256]{3,2,1,0:T(8,128)S(1)} %fusion.228, f32[4,32,32,256]{3,2,1,0:T(8,128)S(1)} %fusion.231, f32[4,32,32,256]{3,2,1,0:T(8,128)S(1)} %fusion.173), kind=kLoop, calls=%fused_computation.2 | loop fusion | flops 44039424 | bytes 31463424 | tf_op jit(solution)/shard_map/reduce_sum | solution.py:246
  246.2 5.1 fusion.283
  254.4 4.6 collective-permute-start.12
  274.4 4.9 maximum_maximum_fusion
  282.5 3.2 fusion.17
  295.2 8.2 %fusion.255 = (f32[64]{0:T(128)S(1)}, f32[64]{0:T(128)S(1)}, f32[4,32,32,64]{3,2,1,0:T(8,128)}) fusion(f32[64]{0:T(128)S(1)} %get-tuple-element.147, f32[4,32,32,64]{3,2,1,0:T(8,128)S(1)} %get-tuple-element.154, f32[64]{0:T(128)S(1)} %get-tuple-element.150, f32[64]{0:T(128)S(1)} %copy-done.32, f32[64]{0:T(128)S(1)} %copy-done.25, ...), kind=kOutput, calls=%fused_computation.373 | convolution fusion | flops 408682368 | bytes 26315264 | tf_op jit(solution)/shard_map/dot_general | solution.py:47
  303.3 43.1 %all-reduce.3 = (f32[64]{0:T(128)S(1)}, f32[64]{0:T(128)S(1)}) all-reduce(f32[64]{0:T(128)S(1)} %get-tuple-element.25, f32[64]{0:T(128)S(1)} %get-tuple-element.24), channel_id=1, replica_groups=mesh['batch'=2,'row'=4,'col'=4] {'batch','row','col'}, use_global_device_ids=true, to_apply=%region_14.16 | all-reduce | flops 128 | bytes 1024 | tf_op jit(solution)/shard_map/psum | solution.py:250
  350.0 4.5 collective-permute-start.16
  359.8 3.5 collective-permute-done.18
  368.7 4.2 collective-permute-start.20
  374.5 4.2 collective-permute-done.21
  378.9 3.5 collective-permute-start.22
  388.7 3.2 reduce_sum.152
  394.5 5.3 slice.602
  399.8 5.0 slice.601
  408.5 39.7 %all-reduce.2 = (f32[64]{0:T(128)S(1)}, f32[64]{0:T(128)S(1)}, f32[768]{0:T(1024)}, f32[80]{0:T(128)}, f32[2,256,2]{1,2,0:T(2,128)}, /*index=5*/f32[2,2]{1,0:T(2,128)}) all-reduce(f32[64]{0:T(128)S(1)} %get-tuple-element.31, f32[64]{0:T(128)S(1)} %get-tuple-element.30, ...), channel_id=1, replica_groups=mesh['batch'=2,'row'=4,'col'=4] {'batch','row','col'}, use_global_device_ids=true, to_apply=%region_20.22 | all-reduce | flops 2004 | bytes 16032 | tf_op jit(solution)/shard_map/psum | solution.py:268
  449.6 3.9 collective-permute-start.24
  455.1 4.1 collective-permute-done.25
  466.9 126.7 %all-reduce.9.cloned.1.call-done = (f32[3,3,64,64]{3,2,1,0:T(8,128)}, f32[3,3,64,64]{3,2,1,0:T(8,128)}, f32[3,3,64,768]{3,2,1,0:T(8,128)}, f32[256,80]{0,1:T(8,128)}) async-done(((f32[3,3,64,64]{3,2,1,0:T(8,128)}, f32[3,3,64,64]{3,2,1,0:T(8,128)}, f32[3,3,64,768]{3,2,1,0:T(8,128)}, f32[256,80]{0,1:T(8,128)}), (f32[3,3,64,64]{3,2,1,0:T(8,128)}, f32[3,3,64,64]{3,2,1,0:T(8,128)}, f32[3,3,64,768]{3,2,1,0:T(8,128)}, ...) | async-done | bytes 2146320 | tf_op jit(solution)/shard_map/psum | solution.py:282
  (249 shorter events, 147.8 us)
Async XLA Ops:
  7.2 218.1 %copy-start = (bf16[256,80]{0,1:T(8,128)(2,1)S(1)}, bf16[256,80]{0,1:T(8,128)(2,1)}, u32[]{:S(2)}) copy-start(bf16[256,80]{0,1:T(8,128)(2,1)} %param.29) | copy-start | bytes 122884
  7.2 586.3 %all-reduce.9.cloned.1.call-start = ((), (), s32[]{:S(2)}) async-start(), calls=%async_computation | async-start | bytes 4882432 | tf_op jit(solution)/shard_map/psum | solution.py:282
  8.0 15.2 %collective-permute-start.1 = (bf16[4,2,16,64]{3,2,1,0:T(8,128)(2,1)S(1)}, bf16[4,2,16,64]{3,2,1,0:T(8,128)(2,1)S(1)}, u32[]{:S(2)}, u32[]{:S(2)}) collective-permute-start(bf16[4,2,16,64]{3,2,1,0:T(8,128)(2,1)S(1)} %get-tuple-element.142), channel_id=1, source_target_pairs={{4,0},{8,4},{12,8},{5,1},{9,5},{13,9},{6,2},{10,6},{14,10},{7,3},{... | collective-permute-start | bytes 49160 | tf_op jit(solution)/shard_map/ppermute | solution.py:17
  9.3 13.9 %collective-permute-start = (bf16[4,2,16,64]{3,2,1,0:T(8,128)(2,1)S(1)}, bf16[4,2,16,64]{3,2,1,0:T(8,128)(2,1)S(1)}, u32[]{:S(2)}, u32[]{:S(2)}) collective-permute-start(bf16[4,2,16,64]{3,2,1,0:T(8,128)(2,1)S(1)} %get-tuple-element.143), channel_id=1, source_target_pairs={{0,4},{4,8},{8,12},{1,5},{5,9},{9,13},{2,6},{6,10},{10,14},{3,7},{... | collective-permute-start | bytes 49160 | tf_op jit(solution)/shard_map/ppermute | solution.py:14
  25.5 5.6 collective-permute-start.3
  26.8 4.3 collective-permute-start.2
  88.9 8.5 %collective-permute-start.4 = (bf16[4,1,32,64]{3,2,1,0:T(8,128)(2,1)S(1)}, bf16[4,1,32,64]{3,2,1,0:T(8,128)(2,1)S(1)}, u32[]{:S(2)}, u32[]{:S(2)}) collective-permute-start(bf16[4,1,32,64]{3,2,1,0:T(8,128)(2,1)S(1)} %get-tuple-element.106), channel_id=1, source_target_pairs={{0,4},{4,8},{8,12},{1,5},{5,9},{9,13},{2,6},{6,10},{10,14},{3,7},{... | collective-permute-start | bytes 49160 | tf_op jit(solution)/shard_map/ppermute | solution.py:14
  91.2 6.2 %collective-permute-start.5 = (bf16[4,1,32,64]{3,2,1,0:T(8,128)(2,1)S(1)}, bf16[4,1,32,64]{3,2,1,0:T(8,128)(2,1)S(1)}, u32[]{:S(2)}, u32[]{:S(2)}) collective-permute-start(bf16[4,1,32,64]{3,2,1,0:T(8,128)(2,1)S(1)} %get-tuple-element.107), channel_id=1, source_target_pairs={{4,0},{8,4},{12,8},{5,1},{9,5},{13,9},{6,2},{10,6},{14,10},{7,3},{... | collective-permute-start | bytes 49160 | tf_op jit(solution)/shard_map/ppermute | solution.py:17
  97.6 5.7 collective-permute-start.7
  98.9 4.4 collective-permute-start.6
  120.4 47.7 %copy-start.25 = (f32[64]{0:T(128)S(1)}, f32[64]{0:T(128)}, u32[]{:S(2)}) copy-start(f32[64]{0:T(128)} %param.25) | copy-start | bytes 772
  120.4 47.7 %copy-start.32 = (f32[64]{0:T(128)S(1)}, f32[64]{0:T(128)}, u32[]{:S(2)}) copy-start(f32[64]{0:T(128)} %param.26) | copy-start | bytes 772
  168.8 6.5 %collective-permute-start.8 = (bf16[4,1,32,64]{3,2,1,0:T(8,128)(2,1)S(1)}, bf16[4,1,32,64]{3,2,1,0:T(8,128)(2,1)S(1)}, u32[]{:S(2)}, u32[]{:S(2)}) collective-permute-start(bf16[4,1,32,64]{3,2,1,0:T(8,128)(2,1)S(1)} %get-tuple-element.102), channel_id=1, source_target_pairs={{0,4},{4,8},{8,12},{1,5},{5,9},{9,13},{2,6},{6,10},{10,14},{3,7},{... | collective-permute-start | bytes 49160 | tf_op jit(solution)/shard_map/ppermute | solution.py:14
  172.5 5.8 collective-permute-start.9
  178.5 6.4 %collective-permute-start.11 = (bf16[4,34,1,64]{3,2,1,0:T(2,128)(2,1)S(1)}, bf16[4,34,1,64]{3,2,1,0:T(2,128)(2,1)S(1)}, u32[]{:S(2)}, u32[]{:S(2)}) collective-permute-start(bf16[4,34,1,64]{3,2,1,0:T(2,128)(2,1)S(1)} %get-tuple-element.90), channel_id=1, source_target_pairs={{1,0},{2,1},{3,2},{5,4},{6,5},{7,6},{9,8},{10,9},{11,10},{13,12},{... | collective-permute-start | bytes 52232 | tf_op jit(solution)/shard_map/ppermute | solution.py:17
  179.8 5.1 collective-permute-start.10
  253.1 8.7 %collective-permute-start.13 = (bf16[4,1,32,768]{3,2,1,0:T(8,128)(2,1)S(1)}, bf16[4,1,32,768]{3,2,1,0:T(8,128)(2,1)S(1)}, u32[]{:S(2)}, u32[]{:S(2)}) collective-permute-start(bf16[4,1,32,768]{3,2,1,0:T(8,128)(2,1)S(1)} %get-tuple-element.66), channel_id=1, source_target_pairs={{4,0},{8,4},{12,8},{5,1},{9,5},{13,9},{6,2},{10,6},{14,10},{7,3},{... | collective-permute-start | bytes 589832 | tf_op jit(solution)/shard_map/ppermute | solution.py:17
  254.4 9.2 %collective-permute-start.12 = (bf16[4,1,32,768]{3,2,1,0:T(8,128)(2,1)S(1)}, bf16[4,1,32,768]{3,2,1,0:T(8,128)(2,1)S(1)}, u32[]{:S(2)}, u32[]{:S(2)}) collective-permute-start(bf16[4,1,32,768]{3,2,1,0:T(8,128)(2,1)S(1)} %get-tuple-element.67), channel_id=1, source_target_pairs={{0,4},{4,8},{8,12},{1,5},{5,9},{9,13},{2,6},{6,10},{10,14},{3,7},{... | collective-permute-start | bytes 589832 | tf_op jit(solution)/shard_map/ppermute | solution.py:14
  264.3 10.1 %collective-permute-start.15 = (bf16[4,34,1,768]{3,2,1,0:T(2,128)(2,1)S(1)}, bf16[4,34,1,768]{3,2,1,0:T(2,128)(2,1)S(1)}, u32[]{:S(2)}, u32[]{:S(2)}) collective-permute-start(bf16[4,34,1,768]{3,2,1,0:T(2,128)(2,1)S(1)} %get-tuple-element.64), channel_id=1, source_target_pairs={{0,1},{1,2},{2,3},{4,5},{5,6},{6,7},{8,9},{9,10},{10,11},{12,13},{... | collective-permute-start | bytes 626696 | tf_op jit(solution)/shard_map/ppermute | solution.py:14
  267.0 7.4 %collective-permute-start.14 = (bf16[4,34,1,768]{3,2,1,0:T(2,128)(2,1)S(1)}, bf16[4,34,1,768]{3,2,1,0:T(2,128)(2,1)S(1)}, u32[]{:S(2)}, u32[]{:S(2)}) collective-permute-start(bf16[4,34,1,768]{3,2,1,0:T(2,128)(2,1)S(1)} %get-tuple-element.65), channel_id=1, source_target_pairs={{1,0},{2,1},{3,2},{5,4},{6,5},{7,6},{9,8},{10,9},{11,10},{13,12},{... | collective-permute-start | bytes 626696 | tf_op jit(solution)/shard_map/ppermute | solution.py:17
  348.7 6.3 %collective-permute-start.17 = (bf16[4,1,32,64]{3,2,1,0:T(8,128)(2,1)S(1)}, bf16[4,1,32,64]{3,2,1,0:T(8,128)(2,1)S(1)}, u32[]{:S(2)}, u32[]{:S(2)}) collective-permute-start(bf16[4,1,32,64]{3,2,1,0:T(8,128)(2,1)S(1)} %get-tuple-element.98), channel_id=1, source_target_pairs={{4,0},{8,4},{12,8},{5,1},{9,5},{13,9},{6,2},{10,6},{14,10},{7,3},{... | collective-permute-start | bytes 49160 | tf_op jit(solution)/shard_map/ppermute | solution.py:17
  350.0 6.1 %collective-permute-start.16 = (bf16[4,1,32,64]{3,2,1,0:T(8,128)(2,1)S(1)}, bf16[4,1,32,64]{3,2,1,0:T(8,128)(2,1)S(1)}, u32[]{:S(2)}, u32[]{:S(2)}) collective-permute-start(bf16[4,1,32,64]{3,2,1,0:T(8,128)(2,1)S(1)} %get-tuple-element.99), channel_id=1, source_target_pairs={{0,4},{4,8},{8,12},{1,5},{5,9},{9,13},{2,6},{6,10},{10,14},{3,7},{... | collective-permute-start | bytes 49160 | tf_op jit(solution)/shard_map/ppermute | solution.py:14
  356.3 3.5 collective-permute-start.19
  357.6 5.7 collective-permute-start.18
  368.7 5.8 collective-permute-start.20
  373.0 5.8 collective-permute-start.21
  378.9 7.1 %collective-permute-start.22 = (bf16[4,34,1,64]{3,2,1,0:T(2,128)(2,1)S(1)}, bf16[4,34,1,64]{3,2,1,0:T(2,128)(2,1)S(1)}, u32[]{:S(2)}, u32[]{:S(2)}) collective-permute-start(bf16[4,34,1,64]{3,2,1,0:T(2,128)(2,1)S(1)} %get-tuple-element.82), channel_id=1, source_target_pairs={{0,1},{1,2},{2,3},{4,5},{5,6},{6,7},{8,9},{9,10},{10,11},{12,13},{... | collective-permute-start | bytes 52232 | tf_op jit(solution)/shard_map/ppermute | solution.py:14
  382.4 4.0 collective-permute-start.23
  449.6 5.5 collective-permute-start.24
  453.6 5.6 collective-permute-start.25
  459.3 4.8 collective-permute-start.26
  460.6 3.9 collective-permute-start.27
  (40 other events, 318.8 us)
Sparse Core Ops, SparseCore 0:
  455.2 138.2 all-reduce.8
where the time goes:
time: 618 us; the launch traced here: 607 us
  blocking collectives  168 us (27%)
  waiting for transfers between devices  148 us (24%)
  matrix products  88.9 us (14%)
  starting transfers between devices  67.2 us (11%)
  local copies, waits for them, and re-layouts  65.8 us (11%)
  other arithmetic  51.5 us (8%)
  between operations  17.5 us (3%)
    psum x1, waiting for transfers between devices, local(): lax.psum((conv_one_grad, conv_two_grad, head_w_grad, head_b_grad, heat_w_...  127 us
    ppermute x14, starting transfers between devices, extended(): lax.ppermute(lax.slice_in_dim(block, block.shape[dim] - width, None, axis...  49.1 us
    psum x1, blocking collectives, local(): lax.psum((jnp.sum(grad_z_two, axis=reduce_axes), jnp.sum(grad_z_two * nor...  43.1 us
    psum x1, blocking collectives, local(): lax.psum((jnp.sum(y_two, axis=reduce_axes), jnp.sum(y_two * y_two, axis=r...  43 us
    psum x1, blocking collectives, local(): lax.psum((jnp.sum(y_one, axis=reduce_axes), jnp.sum(y_one * y_one, axis=r...  42.6 us
    dot_general x27, matrix products, transpose_conv(): jnp.dot(window, kernel[row_tap, col_tap].T, preferred_element_type=jnp.fl...  40.4 us
    psum x1, blocking collectives, local(): lax.psum((jnp.sum(grad_z_one, axis=reduce_axes), jnp.sum(grad_z_one * nor...  39.7 us
    concatenate x4, local copies, waits for them, and re-layouts, patches(): return jnp.concatenate(pieces, axis=-1)  31.4 us
  transfers between devices with their start and end apart: 29, of which 11 were waited for; matrix products, arithmetic and copies ran while one was open for 5% of the time, Pallas kernels for 0%

commit v1 on v0

v1 whole, which is shorter than its diff:
```python
import functools

import jax
import jax.numpy as jnp
from jax import lax
from jax.experimental import pallas as pl
from jax.experimental.pallas import tpu as pltpu
from jax.sharding import PartitionSpec as P

EPSILON = 1e-05
F32 = jnp.float32
BF16 = jnp.bfloat16
KEEP = (((1,), (1,)), ((), ()))
LEFT = (((0,), (0,)), ((), ()))
MIB = 1024 * 1024


def dot(left, right):
    return jnp.dot(left, right, preferred_element_type=F32)


def dot_keep(left, right):
    return lax.dot_general(left, right, KEEP, preferred_element_type=F32)


def dot_left(left, right):
    return lax.dot_general(left, right, LEFT, preferred_element_type=F32)


def three_parts(values):
    high = values.astype(BF16)
    rest = values - high.astype(F32)
    mid = rest.astype(BF16)
    return high, mid, (rest - mid.astype(F32)).astype(BF16)


def tile_count(devices):
    return -(-230 // (2 * devices)) * 2 * devices


def heads_body(
    chunks,
    map_side,
    y_two_ref,
    target_ref,
    spot_ref,
    goal_ref,
    stat_ref,
    conv_ref,
    bias_ref,
    heat_w_ref,
    heat_b_ref,
    box_w_ref,
    box_b_ref,
    heat_out,
    box_out,
    spread_out,
    load_out,
    small_out,
    feat_s,
    taps_ref,
    kernel_s,
    back_s,
    box_s,
    goal_s,
    wide_s,
    grad_s,
    heat_grad_s,
    box_grad_s,
    heat_sum_s,
    box_sum_s,
):
    image = pl.program_id(0)
    chunk = pl.program_id(1)
    rows, breadth = target_ref.shape[1], target_ref.shape[2]
    cells = rows * breadth
    units = 256

    @pl.when(jnp.logical_and(image == 0, chunk == 0))
    def _():
        for tap in range(3):
            kernel_s[tap, 0:192, :] = (0.5 * conv_ref[tap].astype(F32)).astype(BF16)
            kernel_s[tap, 192:256, :] = jnp.zeros((64, 768), BF16)
        parts = three_parts(0.5 * bias_ref[...].reshape(1, 768))
        which = lax.broadcasted_iota(jnp.int32, (16, 768), 0)
        filled = jnp.zeros((16, 768), F32)
        for place in range(3):
            filled = jnp.where(which == place, parts[place].astype(F32), filled)
        kernel_s[1, 192:208, :] = filled.astype(BF16)
        for tap in range(3):
            for block in range(3):
                span = slice(256 * block, 256 * block + 256)
                back_s[span, 256 * tap : 256 * tap + 256] = (
                    kernel_s[tap, :, span].astype(F32).T.astype(BF16)
                )
        empty = jnp.zeros((2, 256), F32)
        for part in range(2):
            pieces = [empty, empty]
            pieces[part] = box_w_ref[part].astype(F32)
            box_s[part] = jnp.concatenate(pieces, axis=0).astype(BF16)
        grad_s[...] = jnp.zeros_like(grad_s)
        heat_grad_s[...] = jnp.zeros_like(heat_grad_s)
        box_grad_s[...] = jnp.zeros_like(box_grad_s)
        heat_sum_s[...] = jnp.zeros_like(heat_sum_s)
        box_sum_s[...] = jnp.zeros_like(box_sum_s)

    @pl.when(chunk == 0)
    def _():
        wide_s[...] = jnp.zeros_like(wide_s)
        ext, wide = taps_ref.shape[0], breadth + 16
        normed = (y_two_ref[0, 1 : ext + 1] - stat_ref[2:3, :]) * stat_ref[3:4, :]
        feature, _ = silu_parts(normed * stat_ref[8:9, :] + stat_ref[9:10, :])
        column = lax.broadcasted_iota(jnp.int32, (wide, 128), 0)
        keep = jnp.where(column < 8, stat_ref[12:13, :], 1.0)
        keep = jnp.where(column >= 8 + breadth, stat_ref[13:14, :], keep)
        feat_s[0:PAD, :] = jnp.zeros((PAD, 128), F32)
        feat_s[PAD : PAD + ext * wide, :] = (feature * keep).reshape(ext * wide, 128)
        feat_s[PAD + ext * wide :, :] = jnp.zeros((PAD, 128), F32)
        for line, row in ((PAD, 10), (PAD + (ext - 1) * wide, 11)):
            feat_s[line : line + wide, :] = feat_s[line : line + wide, :] * stat_ref[row : row + 1]
        pairs = tap_pairs(feat_s, PAD, ext * wide, 1.0)
        taps_ref[...] = pairs.reshape(ext, wide, 256)[:, 8 : 8 + breadth].astype(BF16)
        for place, part in enumerate(three_parts(goal_ref[0])):
            goal_s[place] = part

    first = chunk * rows
    taps = jnp.concatenate(
        [taps_ref[pl.ds(first + tap, rows)].reshape(cells, 256) for tap in range(3)], axis=1
    )
    active, slope = [], []
    for block in range(3):
        weight = kernel_s[:, :, block * units : (block + 1) * units].reshape(768, units)
        hidden = dot(taps, weight)
        turn = jnp.tanh(hidden)
        above = 1.0 + turn
        product = hidden * above
        active.append(product.astype(BF16))
        slope.append(above + product * (1.0 - turn))

    logit = dot_keep(active[0], heat_w_ref[...]) + heat_b_ref[...]
    decay = jnp.exp(-jnp.abs(logit))
    large = 1.0 / (1.0 + decay)
    small = decay * large
    above = logit >= 0.0
    chance = jnp.where(above, large, small)
    heat_out[0] = chance.reshape(rows, breadth, 80)
    target = target_ref[0].reshape(cells, 80).astype(F32)
    positive = target == 1.0
    side = jnp.where(positive, jnp.where(above, small, large), chance)
    value = jnp.where(positive, -logit, logit)
    soft = jnp.maximum(value, 0.0) + jnp.log(1.0 + decay)
    slant = side * side * (2.0 * (1.0 - side) * soft + side)
    gap = 1.0 - target
    gap = gap * gap
    weighting = jnp.where(positive, -1.0, gap * gap) * stat_ref[4:5, 0:80]
    logit_grad = weighting * slant
    logit_low = logit_grad.astype(BF16)

    box_bias = jnp.concatenate([box_b_ref[0:1, :], box_b_ref[1:2, :]], axis=1)
    boxes = dot_keep(active[1], box_s[0]) + dot_keep(active[2], box_s[1]) + box_bias
    box_out[0] = jnp.swapaxes(boxes.reshape(rows, breadth, 4), 1, 2)
    shape = (rows, breadth, 128)
    cell = (first + lax.broadcasted_iota(jnp.int32, shape, 0)) * map_side
    cell = (cell + lax.broadcasted_iota(jnp.int32, shape, 1)).reshape(cells, 128)
    chosen = (cell == spot_ref[pl.ds(image, 1), :]).astype(F32).astype(BF16)
    goals = dot_keep(chosen, goal_s[0]) + dot_keep(chosen, goal_s[1])
    goals = goals + dot_keep(chosen, goal_s[2])
    hit = dot(chosen, jnp.ones((128, 4), BF16))
    miss = boxes - goals
    lane = lax.broadcasted_iota(jnp.int32, (1, 4), 1)
    factor = jnp.where(lane < 2, 0.1, 1.0) * stat_ref[5:6, 0:4]
    box_grad = hit * factor * miss * lax.rsqrt(miss * miss + 1.0)
    box_low = box_grad.astype(BF16)

    heat_sum_s[...] += jnp.sum(logit_low.astype(F32).reshape(cells // 8, 8, 80), axis=0)
    box_sum_s[...] += jnp.sum(box_low.astype(F32).reshape(cells // 8, 8, 4), axis=0)
    heat_grad_s[...] += dot_left(logit_low, active[0])
    for part in range(2):
        box_grad_s[part] += dot_left(box_low, active[1 + part])

    back = [
        dot(logit_low, heat_w_ref[...]),
        dot(box_low, box_s[0]),
        dot(box_low, box_s[1]),
    ]
    grad_hidden = jnp.concatenate(
        [(back[block] * slope[block]).astype(BF16) for block in range(3)], axis=1
    )
    spread = []
    for tap in range(3):
        part = dot(grad_hidden, back_s[:, 256 * tap : 256 * tap + 256])
        spread.append(part.reshape(rows, breadth, 256))
    inner = slice(16, 16 + breadth)
    wide_s[pl.ds(first, 1), inner, :] += spread[0][0:1]
    wide_s[pl.ds(first + 1, 1), inner, :] += spread[0][1:2] + spread[1][0:1]
    wide_s[pl.ds(first + 2, rows - 2), inner, :] = (
        spread[0][2:] + spread[1][1:-1] + spread[2][:-2]
    )
    wide_s[pl.ds(first + rows, 1), inner, :] = spread[1][-1:] + spread[2][-2:-1]
    wide_s[pl.ds(first + rows + 1, 1), inner, :] = spread[2][-1:]
    for tap in range(3):
        grad_s[tap] += dot_left(taps[:, 256 * tap : 256 * tap + 256], grad_hidden)

    @pl.when(chunk == chunks - 1)
    def _():
        reach = breadth + 16
        centre = pltpu.roll(wide_s[:, 8 : 8 + reach, 0:128], 64, 2)
        total = wide_s[:, 9 : 9 + reach, 0:128] + centre + wide_s[:, 7 : 7 + reach, 128:256]
        lanes = lax.broadcasted_iota(jnp.int32, total.shape, 2)
        spread_out[0] = jnp.where(lanes < 64, total, pltpu.roll(total, 64, 2))

    @pl.when(jnp.logical_and(image == pl.num_programs(0) - 1, chunk == chunks - 1))
    def _():
        for column in range(6):
            span = slice(128 * column, 128 * column + 128)
            for tap in range(3):
                start = 36 * column + 12 * tap
                load_out[start : start + 12] = (
                    (0.5 * grad_s[tap, 0:192, span]).reshape(12, 16, 128).astype(BF16)
                )
            small_out[column : column + 1, :] = 0.5 * grad_s[1, 192:193, span]
        for half in range(2):
            span = slice(128 * half, 128 * half + 128)
            start = 216 + 5 * half
            load_out[start : start + 5] = heat_grad_s[:, span].reshape(5, 16, 128).astype(BF16)
            for part in range(2):
                padded = jnp.concatenate(
                    [box_grad_s[part, :, span], jnp.zeros((12, 128), F32)], axis=0
                )
                load_out[226 + 2 * part + half] = padded.astype(BF16)
        load_out[230:] = jnp.zeros((load_out.shape[0] - 230, 16, 128), BF16)
        small_out[6:8, :] = jnp.zeros((2, 128), F32)
        small_out[6:7, 0:80] = jnp.sum(heat_sum_s[...], axis=0, keepdims=True)
        small_out[7:8, 0:4] = jnp.sum(box_sum_s[...], axis=0, keepdims=True)


def heads(
    taps, target, spot, goal, stats, conv, bias, heat_w, heat_b, box_w, box_b, devices
):
    images, height, breadth, classes = target.shape
    rows = height
    chunks = height // rows
    tiles = tile_count(devices)
    whole = lambda *shape: pl.BlockSpec(shape, lambda b, c: (0,) * len(shape))
    cells = images * height * breadth
    return pl.pallas_call(
        functools.partial(heads_body, chunks, breadth * lax.axis_size("col")),
        grid=(images, chunks),
        in_specs=[
            pl.BlockSpec((1, height + 4, breadth + 16, 128), lambda b, c: (b, 0, 0, 0)),
            pl.BlockSpec((1, rows, breadth, classes), lambda b, c: (b, c, 0, 0)),
            whole(8, 128),
            pl.BlockSpec((1, 4, 128), lambda b, c: (b, 0, 0)),
            whole(24, 128),
            whole(3, 192, 768),
            whole(768),
            whole(80, 256),
            whole(1, 80),
            whole(2, 2, 256),
            whole(2, 2),
        ],
        out_specs=[
            pl.BlockSpec((1, rows, breadth, classes), lambda b, c: (b, c, 0, 0)),
            pl.BlockSpec((1, rows, 4, breadth), lambda b, c: (b, c, 0, 0)),
            pl.BlockSpec((1, height + 2, breadth + 16, 128), lambda b, c: (b, 0, 0, 0)),
            whole(tiles, 16, 128),
            whole(8, 128),
        ],
        out_shape=[
            jax.ShapeDtypeStruct((images, height, breadth, classes), F32),
            jax.ShapeDtypeStruct((images, height, 4, breadth), F32),
            jax.ShapeDtypeStruct((images, height + 2, breadth + 16, 128), F32),
            jax.ShapeDtypeStruct((tiles, 16, 128), BF16),
            jax.ShapeDtypeStruct((8, 128), F32),
        ],
        scratch_shapes=[
            pltpu.VMEM((2 * PAD + (height + 2) * (breadth + 16), 128), F32),
            pltpu.VMEM((height + 2, breadth, 256), BF16),
            pltpu.VMEM((3, 256, 768), BF16),
            pltpu.VMEM((768, 768), BF16),
            pltpu.VMEM((2, 4, 256), BF16),
            pltpu.VMEM((3, 4, 128), BF16),
            pltpu.VMEM((height + 2, breadth + 32, 256), F32),
            pltpu.VMEM((3, 256, 768), F32),
            pltpu.VMEM((80, 256), F32),
            pltpu.VMEM((2, 4, 256), F32),
            pltpu.VMEM((8, 80), F32),
            pltpu.VMEM((8, 4), F32),
        ],
        compiler_params=pltpu.CompilerParams(vmem_limit_bytes=60 * MIB),
        cost_estimate=pl.CostEstimate(
            flops=cells * 576 * 768 * 6, bytes_accessed=12 * MIB, transcendentals=cells * 768
        ),
        name="heads",
    )(taps, target, spot, goal, stats, conv, bias, heat_w, heat_b, box_w, box_b)


MESH = pl.DeviceIdType.MESH


def rounded_up(value, step):
    return -(-value // step) * step


def place():
    return lax.axis_index("batch"), lax.axis_index("row"), lax.axis_index("col")


def extents():
    return lax.axis_size("batch"), lax.axis_size("row"), lax.axis_size("col")


def plane_partners():
    batch, row, col = place()
    batches, _, cols = extents()
    partners = []
    for over in range(batches):
        for along in range(cols):
            if over or along:
                partners.append(
                    (lax.rem(batch + over, batches), row, lax.rem(col + along, cols))
                )
    return partners


def row_partners():
    batch, row, col = place()
    rows = lax.axis_size("row")
    return [(batch, lax.rem(row + over, rows), col) for over in range(1, rows)]


def flat():
    batches, rows, cols = extents()
    return batches * rows * cols <= 8


def all_partners():
    batch, row, col = place()
    batches, rows, cols = extents()
    partners = []
    for over in range(batches):
        for up in range(rows):
            for along in range(cols):
                if over or up or along:
                    partners.append(
                        (
                            lax.rem(batch + over, batches),
                            lax.rem(row + up, rows),
                            lax.rem(col + along, cols),
                        )
                    )
    return partners


def greet():
    barrier = pltpu.get_barrier_semaphore()
    partners = all_partners() if flat() else plane_partners() + row_partners()
    for partner in partners:
        pl.semaphore_signal(barrier, inc=1, device_id=partner, device_id_type=MESH)
    batch, row, col = place()
    _, rows, cols = extents()
    expected = len(partners)
    for up in (-1, 1):
        for along in (-1, 1):
            fits = jnp.logical_and(row + up >= 0, row + up < rows)
            fits = jnp.logical_and(fits, jnp.logical_and(col + along >= 0, col + along < cols))
            expected = expected + fits.astype(jnp.int32)

            @pl.when(fits)
            def _(up=up, along=along):
                pl.semaphore_signal(
                    barrier,
                    inc=1,
                    device_id=(batch, row + up, col + along),
                    device_id_type=MESH,
                )

    pl.semaphore_wait(barrier, expected)


def remote(source, target, send, recv, device):
    return pltpu.make_async_remote_copy(
        src_ref=source,
        dst_ref=target,
        send_sem=send,
        recv_sem=recv,
        device_id=device,
        device_id_type=MESH,
    )


def start_all(copies):
    for copy in copies:
        copy.start()


def wait_all(copies):
    for copy in copies:
        copy.wait()


def slot_sum(slots):
    total = slots[0]
    for k in range(1, slots.shape[0]):
        total = total + slots[k]
    return total


class Total:
    def __init__(self, source, slots, mid, row_slots, sems):
        self.source, self.slots, self.mid = source, slots, mid
        self.row_slots, self.sems = row_slots, sems

    def send(self, source, slots, mine, partners, step):
        self.copies = [
            remote(
                source,
                slots.at[mine],
                self.sems.at[step, 0, k],
                self.sems.at[step, 1, k],
                partner,
            )
            for k, partner in enumerate(partners)
        ]
        start_all(self.copies)
        slots[mine] = source[...]

    def begin(self):
        batch, row, col = place()
        _, rows, cols = extents()
        if flat():
            mine, partners = (batch * rows + row) * cols + col, all_partners()
        else:
            mine, partners = batch * cols + col, plane_partners()
        self.send(self.source, self.slots, mine, partners, 0)

    def middle(self):
        if not flat():
            wait_all(self.copies)
            self.mid[...] = slot_sum(self.slots)
            self.send(self.mid, self.row_slots, place()[1], row_partners(), 1)

    def end(self):
        wait_all(self.copies)
        return slot_sum(self.slots if flat() else self.row_slots)


def total_scratch(lines):
    batches, rows, cols = extents()
    slots = batches * cols * (rows if flat() else 1)
    return [
        pltpu.VMEM((lines, 128), F32),
        pltpu.VMEM((slots, lines, 128), F32),
        pltpu.VMEM((lines, 128), F32),
        pltpu.VMEM((rows, lines, 128), F32),
        pltpu.SemaphoreType.DMA((2, 2, max(slots, rows) - 1)),
    ]


AROUND = ((-1, 0), (1, 0), (0, -1), (0, 1), (-1, -1), (-1, 1), (1, -1), (1, 1))


class Around:
    def __init__(self, pieces, slots, sems):
        batch, row, col = place()
        _, rows, cols = extents()

        def exists(up, along):
            fits = jnp.logical_and(row + up >= 0, row + up < rows)
            return jnp.logical_and(fits, jnp.logical_and(col + along >= 0, col + along < cols))

        self.sends = [exists(up, along) for up, along in AROUND]
        self.comes = [exists(-up, -along) for up, along in AROUND]
        self.copies = [
            remote(pieces[k], slots[k], sems.at[0, k], sems.at[1, k], (batch, row + up, col + along))
            for k, (up, along) in enumerate(AROUND)
        ]

    def start(self, which=range(8)):
        for k in which:
            pl.when(self.sends[k])(self.copies[k].start)

    def wait(self, which=range(8)):
        for k in which:
            pl.when(self.comes[k])(self.copies[k].wait_recv)
            pl.when(self.sends[k])(self.copies[k].wait_send)

    def each(self, use, which=range(8)):
        for k in which:
            pl.when(self.comes[k])(functools.partial(use, k))


def twice(values):
    return jnp.concatenate([values, values], axis=-1)


def lower_half(shape):
    return lax.broadcasted_iota(jnp.int32, shape, len(shape) - 1) < 64


def swapped(values):
    return pltpu.roll(values, 64, len(values.shape) - 1)


def widened(values):
    rows, cols = values.shape[0], values.shape[1]
    side = jnp.zeros((rows, 8, 128), F32)
    return jnp.concatenate([side, twice(values.astype(F32)), side], axis=1)


def tap_pairs(buffer, start, count, fill):
    low = lower_half((1, 128))
    first = jnp.where(low, buffer[pl.ds(start - 1, count), :], buffer[pl.ds(start, count), :])
    second = jnp.where(low, buffer[pl.ds(start + 1, count), :], fill)
    return jnp.concatenate([first, second], axis=1)


def silu_parts(values):
    logistic = 0.5 * jnp.tanh(0.5 * values) + 0.5
    return values * logistic, logistic


PAD = 16


def row_loop(total, step, body, init):
    return lax.fori_loop(0, total // step, lambda k, carry: body(k * step, carry), init)


def fold_sum(values):
    return jnp.sum(values.reshape(-1, 8, 128), axis=0)


def clear(buffer, start, rows, pitch, tops, bottoms, lefts, rights):
    _, row_at, col_at = place()
    count = rounded_up(rows, 8)

    def clear_rows(span):
        first, last = span
        size = (last - first) * pitch
        buffer[pl.ds(start + first * pitch, size), :] = jnp.zeros((size, 128), F32)

    def clear_columns(span):
        for column in range(*span):
            buffer[pl.ds(start + column, count, stride=pitch), :] = jnp.zeros((count, 128), F32)

    pl.when(row_at == 0)(lambda: clear_rows(tops))
    pl.when(row_at == lax.axis_size("row") - 1)(lambda: clear_rows(bottoms))
    pl.when(col_at == 0)(lambda: clear_columns(lefts))
    pl.when(col_at == lax.axis_size("col") - 1)(lambda: clear_columns(rights))


def stack_weight(target, source):
    for tap in range(3):
        target[256 * tap : 256 * tap + 192, :] = twice(source[tap].astype(F32)).astype(BF16)
        target[256 * tap + 192 : 256 * tap + 256, :] = jnp.zeros((64, 128), BF16)


def unpacked(packed, image, images):
    low = lower_half((1, 128))
    keep = low if image < images // 2 else jnp.logical_not(low)
    return jnp.where(keep, packed, swapped(packed))


def pack_columns(buffer, target, images, rows, pitch, first_row, first, depth):
    low = lower_half((1, 128))
    half = images // 2
    count = target.shape[1]
    for pair in range(half):
        for j in range(depth):
            parts = [
                buffer[
                    pl.ds(
                        PAD + (image * rows + first_row) * pitch + first + j, count, stride=pitch
                    ),
                    :,
                ]
                for image in (pair, pair + half)
            ]
            target[depth * pair + j] = jnp.where(low, parts[0], parts[1]).astype(target.dtype)


def pack_corner(buffer, target, images, rows, pitch, first_row, first, depth):
    low = lower_half((1, 128))
    half = images // 2
    count = target.shape[1] // 8
    for pair in range(half):
        pieces = []
        for row in range(count):
            if row < depth:
                starts = [
                    PAD + (image * rows + first_row + row) * pitch + first
                    for image in (pair, pair + half)
                ]
                pieces.append(
                    jnp.where(
                        low,
                        buffer[starts[0] : starts[0] + 8, :],
                        buffer[starts[1] : starts[1] + 8, :],
                    )
                )
            else:
                pieces.append(jnp.zeros((8, 128), F32))
        target[pair] = jnp.concatenate(pieces, axis=0).astype(target.dtype)


def unpack_columns(buffer, source, images, rows, pitch, first_row, first, depth, lines, add):
    half = images // 2
    count = rounded_up(lines, 8)
    valid = lax.broadcasted_iota(jnp.int32, (count, 128), 0) < lines
    for image in range(images):
        for j in range(depth):
            packed = source[depth * (image % half) + j].astype(F32)
            values = unpacked(packed, image, images)[:count]
            spots = pl.ds(
                PAD + (image * rows + first_row) * pitch + first + j, count, stride=pitch
            )
            if add:
                values = buffer[spots, :] + jnp.where(valid, values, 0.0)
            elif count > lines:
                values = jnp.where(valid, values, buffer[spots, :])
            buffer[spots, :] = values


def unpack_corner(buffer, source, images, rows, pitch, first_row, first, depth, add):
    half = images // 2
    valid = lax.broadcasted_iota(jnp.int32, (8, 128), 0) < depth
    for image in range(images):
        packed = unpacked(source[image % half].astype(F32), image, images)
        for row in range(depth):
            start = PAD + (image * rows + first_row + row) * pitch + first
            old = buffer[start : start + 8, :]
            values = packed[8 * row : 8 * row + 8]
            if add:
                values = old + jnp.where(valid, values, 0.0)
            else:
                values = jnp.where(valid, values, old)
            buffer[start : start + 8, :] = values


def rise_body(
    low_ref,
    skip_ref,
    target_ref,
    conv_one_ref,
    conv_two_ref,
    gain_one_ref,
    shift_one_ref,
    gain_two_ref,
    shift_two_ref,
    index_ref,
    count_ref,
    y_two_out,
    y_one_out,
    merged_out,
    low_out,
    stat_out,
    spot_out,
    tiles_out,
    low_in,
    skip_in,
    target_in,
    conv_one_in,
    conv_two_in,
    param_in,
    index_in,
    y_two_s,
    y_one_s,
    merged_s,
    low_s,
    low_x,
    skip_x,
    act_s,
    row_s,
    up_s,
    w_one,
    w_two,
    g_low,
    own_low,
    low_rows,
    skip_rows,
    low_send,
    low_recv,
    low_corner,
    skip_send,
    skip_recv,
    skip_corner,
    first_scratch,
    second_scratch,
    in_sems,
    out_sems,
    strip_sems,
):
    images, h, w, _ = low_ref.shape
    height, breadth = skip_ref.shape[1], skip_ref.shape[2]
    batch_at, row_at, col_at = place()
    batches, row_count, col_count = extents()
    pitch, wide = w + 16, breadth + 16
    low_r, y_one_r = h + 6, h + 4
    skip_r, y_two_r = height + 6, height + 4
    cells_low = float(images * batches * h * row_count * w * col_count)
    cells_high = 4.0 * cells_low

    loads = [
        pltpu.make_async_copy(source, target, in_sems.at[k])
        for k, (source, target) in enumerate(
            (
                (low_ref, low_in),
                (conv_one_ref, conv_one_in),
                (skip_ref, skip_in),
                (index_ref, index_in),
                (target_ref, target_in),
                (gain_one_ref, param_in.at[0]),
                (shift_one_ref, param_in.at[1]),
                (gain_two_ref, param_in.at[2]),
                (shift_two_ref, param_in.at[3]),
                (conv_two_ref, conv_two_in),
            )
        )
    ]
    for load in loads:
        load.start()
    greet()
    low_around = Around(
        [low_ref.at[:, 0:3], low_ref.at[:, h - 3 : h]]
        + [low_send.at[k] for k in range(2)]
        + [low_corner.at[0, k] for k in range(4)],
        [low_rows.at[0], low_rows.at[1]]
        + [low_recv.at[k] for k in range(2)]
        + [low_corner.at[1, k] for k in range(4)],
        strip_sems.at[0],
    )
    skip_around = Around(
        [skip_ref.at[:, 0:3], skip_ref.at[:, height - 3 : height]]
        + [skip_send.at[k] for k in range(2)]
        + [skip_corner.at[0, k] for k in range(4)],
        [skip_rows.at[0], skip_rows.at[1]]
        + [skip_recv.at[k] for k in range(2)]
        + [skip_corner.at[1, k] for k in range(4)],
        strip_sems.at[1],
    )
    low_around.start(range(2))

    def place_low(b, carry):
        start = PAD + b * low_r * pitch
        low_x[pl.ds(start, 3 * pitch), :] = jnp.zeros((3 * pitch, 128), F32)
        low_x[pl.ds(start + 3 * pitch, h * pitch), :] = widened(low_in[b]).reshape(h * pitch, 128)
        low_x[pl.ds(start + (h + 3) * pitch, 3 * pitch), :] = jnp.zeros((3 * pitch, 128), F32)
        return carry

    low_x[0:PAD, :] = jnp.zeros((PAD, 128), F32)
    tail = low_x.shape[0] - PAD - images * low_r * pitch
    low_x[PAD + images * low_r * pitch :, :] = jnp.zeros((tail, 128), F32)
    loads[0].wait()
    lax.fori_loop(0, images, place_low, 0)
    loads[1].wait()
    stack_weight(w_one, conv_one_in)

    def pack(buffer, sends, corners, rows, step, line, across):
        for side, first in enumerate((8, 5 + across)):
            pack_columns(buffer, sends.at[side], images, rows, line, 3, first, 3)
        for k, (up, along) in enumerate(AROUND[4:]):
            pack_corner(
                buffer,
                corners.at[0, k],
                images,
                rows,
                line,
                3 if up < 0 else step,
                8 if along < 0 else 5 + across,
                3,
            )

    def unpack(around, buffer, strips, columns, corners, rows, step, line, across):
        def use(k):
            up, along = AROUND[k]
            row = step + 3 if up < 0 else 0
            column = 8 + across if along < 0 else 5
            if k < 2:

                def body(b, carry):
                    start = PAD + (b * rows + row) * line
                    buffer[pl.ds(start, 3 * line), :] = widened(strips[k, b]).reshape(
                        3 * line, 128
                    )
                    return carry

                lax.fori_loop(0, images, body, 0)
            elif k < 4:
                unpack_columns(
                    buffer, columns.at[k - 2], images, rows, line, 3, column, 3, step, False
                )
            else:
                unpack_corner(
                    buffer, corners.at[1, k - 4], images, rows, line, row, column, 3, False
                )

        around.each(use)

    pack(low_x, low_send, low_corner, low_r, h, pitch, w)
    low_around.start(range(2, 8))
    skip_around.start(range(2))

    def place_skip(b, carry):
        start = PAD + b * skip_r * wide
        edge = jnp.zeros((3 * wide, 128), F32)
        skip_x[pl.ds(start, 3 * wide), :] = edge
        skip_x[pl.ds(start + 3 * wide, height * wide), :] = widened(skip_in[b]).reshape(
            height * wide, 128
        )
        skip_x[pl.ds(start + (height + 3) * wide, 3 * wide), :] = edge
        return carry

    skip_x[0:PAD, :] = jnp.zeros((PAD, 128), F32)
    skip_tail = skip_x.shape[0] - PAD - images * skip_r * wide
    skip_x[PAD + images * skip_r * wide :, :] = jnp.zeros((skip_tail, 128), F32)
    loads[2].wait()
    lax.fori_loop(0, images, place_skip, 0)
    pack(skip_x, skip_send, skip_corner, skip_r, height, wide, breadth)
    skip_around.start(range(2, 8))
    low_around.wait()
    unpack(low_around, low_x, low_rows, low_recv, low_corner, low_r, h, pitch, w)

    def conv_one(b, sums):
        pairs = tap_pairs(low_x, PAD + b * low_r * pitch, low_r * pitch, 0.0)
        own = pairs.reshape(low_r, pitch, 256)[2 : h + 4, 8 : 8 + w]
        low_s[b] = own.astype(BF16)
        lines = jnp.sum(own.astype(BF16).astype(F32), axis=1)
        tap_sums = [
            sums[2 + tap] + jnp.sum(lines[tap : tap + h], axis=0, keepdims=True)
            for tap in range(3)
        ]
        pairs = pairs.astype(BF16)
        count = y_one_r * pitch
        taps = jnp.concatenate([pairs[pitch * a : pitch * a + count] for a in range(3)], axis=1)
        value = dot(taps, w_one[...]).reshape(y_one_r, pitch, 128)
        y_one_s[b] = value
        own = value[2 : h + 2, 8 : 8 + w].reshape(h * w, 128)
        return (
            sums[0] + jnp.sum(own, axis=0, keepdims=True),
            sums[1] + jnp.sum(own * own, axis=0, keepdims=True),
            *tap_sums,
        )

    def count_ones(b, total):
        ones = (target_in[b].reshape(height * breadth, 80).astype(F32) == 1.0).astype(F32)
        return total + jnp.sum(ones, axis=0, keepdims=True)

    nothing = jnp.zeros((1, 128), F32)
    tap_none = jnp.zeros((1, 256), F32)
    sums = lax.fori_loop(0, images, conv_one, (nothing, nothing, tap_none, tap_none, tap_none))
    tap_sums = sums[2:]
    for k in (3, 4):
        loads[k].wait()
    ones = lax.fori_loop(0, images, count_ones, jnp.zeros((1, 80), F32))
    base = row_at * (height * breadth * col_count) + col_at * breadth
    slot = lax.broadcasted_iota(jnp.int32, (1, 128), 1)
    objects = 0
    spot_out[...] = jnp.full((8, 128), -(2**30), jnp.int32)
    for b in range(images):
        amount = count_ref[b]
        objects = objects + amount
        spot_out[b : b + 1, :] = jnp.where(
            slot < amount, index_in[b : b + 1, :] - base, -(2**30)
        )
    leading = jnp.logical_and(row_at == 0, col_at == 0).astype(F32)
    sum_src = first_scratch[0]
    sum_src[...] = jnp.zeros((8, 128), F32)
    sum_src[0:1, :] = sums[0]
    sum_src[1:2, :] = sums[1]
    sum_src[2:3, 0:80] = ones
    sum_src[3:4, :] = jnp.full((1, 128), objects.astype(F32) * leading)
    first_total = Total(*first_scratch)
    first_total.begin()
    stores = [
        pltpu.make_async_copy(y_one_s, y_one_out, out_sems.at[0, 0]),
        pltpu.make_async_copy(low_s, low_out, out_sems.at[0, 1]),
    ]
    for store in stores:
        store.start()

    loads[9].wait()
    stack_weight(w_two, conv_two_in)
    skip_around.wait()
    unpack(
        skip_around, skip_x, skip_rows, skip_recv, skip_corner, skip_r, height, wide, breadth
    )
    first_total.middle()
    for k in range(5, 9):
        loads[k].wait()
    totals = first_total.end()
    mean_one = totals[0:1] / cells_low
    scale_one = lax.rsqrt(totals[1:2] / cells_low - mean_one * mean_one + EPSILON)
    gain_one, shift_one = twice(param_in[0]), twice(param_in[1])
    gain_two, shift_two = twice(param_in[2]), twice(param_in[3])
    stat_out[...] = jnp.zeros((24, 128), F32)
    stat_out[0:1, :] = mean_one
    stat_out[1:2, :] = scale_one
    positives = jnp.sum(totals[2:3, 0:80], axis=1, keepdims=True)
    stat_out[4:5, :] = jnp.broadcast_to(1.0 / positives, (1, 128))
    stat_out[5:6, :] = 0.5 / totals[3:4]
    stat_out[6:7, :] = gain_one
    stat_out[7:8, :] = shift_one
    stat_out[8:9, :] = gain_two
    stat_out[9:10, :] = shift_two
    ends = (row_at > 0, row_at < row_count - 1, col_at > 0, col_at < col_count - 1)
    for k, inner in enumerate(ends):
        stat_out[10 + k : 11 + k, :] = jnp.full((1, 128), inner.astype(F32))

    def conv_two(b, sums):
        normed = (y_one_s[b] - mean_one) * scale_one
        value, _ = silu_parts(normed * gain_one + shift_one)
        act_s[0 : y_one_r * pitch, :] = value.astype(BF16).astype(F32).reshape(
            y_one_r * pitch, 128
        )
        clear(
            act_s, 0, y_one_r, pitch, (0, 2), (h + 2, h + 4), (6, 8), (8 + w, 10 + w)
        )
        act = act_s[0 : y_one_r * pitch, :].reshape(y_one_r, pitch, 128)
        odd = 0.75 * act[:-1] + 0.25 * act[1:]
        even = 0.75 * act[1:] + 0.25 * act[:-1]
        tall = jnp.stack([odd, even], axis=1).reshape(skip_r * pitch, 128)
        row_s[PAD : PAD + skip_r * pitch, :] = tall
        count = skip_r * pitch
        before = row_s[PAD - 1 : PAD - 1 + count, :]
        behind = row_s[PAD + 1 : PAD + 1 + count, :]
        up_s[pl.ds(0, count, stride=2), :] = 0.75 * tall + 0.25 * before
        up_s[pl.ds(1, count, stride=2), :] = 0.75 * tall + 0.25 * behind
        start = PAD + b * skip_r * wide
        whole = pl.ds(start, skip_r * wide)
        up = up_s[...].reshape(skip_r, 2 * pitch, 128)[:, 8 : 8 + wide]
        merged = up + skip_x[whole, :].reshape(skip_r, wide, 128)
        skip_x[whole, :] = merged.astype(BF16).astype(F32).reshape(skip_r * wide, 128)
        clear(
            skip_x,
            start,
            skip_r,
            wide,
            (0, 3),
            (height + 3, height + 6),
            (5, 8),
            (8 + breadth, 11 + breadth),
        )
        pairs = tap_pairs(skip_x, start, skip_r * wide, 0.0)
        merged_s[b] = pairs.reshape(skip_r, wide, 256)[2 : height + 4, 8 : 8 + breadth].astype(
            BF16
        )
        pltpu.make_async_copy(merged_s.at[b], merged_out.at[b], out_sems.at[1, b]).start()
        pairs = pairs.astype(BF16)
        count = y_two_r * wide
        taps = jnp.concatenate([pairs[wide * a : wide * a + count] for a in range(3)], axis=1)
        value = dot(taps, w_two[...]).reshape(y_two_r, wide, 128)
        y_two_s[b] = value
        pltpu.make_async_copy(y_two_s.at[b], y_two_out.at[b], out_sems.at[2, b]).start()
        own = value[2 : height + 2, 8 : 8 + breadth].reshape(height * breadth, 128)
        return (
            sums[0] + jnp.sum(own, axis=0, keepdims=True),
            sums[1] + jnp.sum(own * own, axis=0, keepdims=True),
        )

    row_s[0:PAD, :] = jnp.zeros((PAD, 128), F32)
    row_s[PAD + skip_r * pitch :, :] = jnp.zeros((PAD, 128), F32)
    sums = lax.fori_loop(0, images, conv_two, (nothing, nothing))
    sum_src = second_scratch[0]
    sum_src[...] = jnp.zeros((8, 128), F32)
    sum_src[0:1, :] = sums[0]
    sum_src[1:2, :] = sums[1]
    for tap in range(3):
        for part in range(2):
            line = 2 + 2 * tap + part
            sum_src[line : line + 1, :] = tap_sums[tap][:, 128 * part : 128 * part + 128]
    second_total = Total(*second_scratch)
    second_total.begin()
    g_low[...] = jnp.zeros_like(g_low)
    own_low[...] = jnp.zeros_like(own_low)

    def normed_taps(b, carry):
        normed = (y_one_s[b, 2 : h + 2] - mean_one) * scale_one
        own_low[2 * w : (h + 2) * w, :] = normed[:, 8 : 8 + w].reshape(h * w, 128)
        g_low[...] += product_of_parts(
            low_s[b].reshape((h + 2) * w, 256), shifted_taps(own_low, h, w)
        )
        return carry

    lax.fori_loop(0, images, normed_taps, 0)
    fold(tiles_out, 0, g_low)
    second_total.middle()
    totals = second_total.end()
    mean_two = totals[0:1] / cells_high
    scale_two = lax.rsqrt(totals[1:2] / cells_high - mean_two * mean_two + EPSILON)
    stat_out[2:3, :] = mean_two
    stat_out[3:4, :] = scale_two
    stat_out[16:22, :] = totals[2:8]

    for store in stores:
        store.wait()
    for b in range(images):
        pltpu.make_async_copy(merged_s.at[b], merged_out.at[b], out_sems.at[1, b]).wait()
        pltpu.make_async_copy(y_two_s.at[b], y_two_out.at[b], out_sems.at[2, b]).wait()


def rise(
    low_map,
    skip_map,
    target,
    conv_one,
    conv_two,
    gain_one,
    shift_one,
    gain_two,
    shift_two,
    index,
    count,
):
    images, h, w, _ = low_map.shape
    _, height, breadth, _ = skip_map.shape
    pitch, wide = w + 16, breadth + 16
    low_r, skip_r = h + 6, height + 6
    half = images // 2
    vmem = pl.BlockSpec(memory_space=pltpu.VMEM)
    hbm = pl.BlockSpec(memory_space=pl.ANY)
    kept = [
        jax.ShapeDtypeStruct((images, height + 4, wide, 128), F32),
        jax.ShapeDtypeStruct((images, h + 4, pitch, 128), F32),
        jax.ShapeDtypeStruct((images, height + 2, breadth, 256), BF16),
        jax.ShapeDtypeStruct((images, h + 2, w, 256), BF16),
    ]
    return pl.pallas_call(
        rise_body,
        in_specs=[hbm] * 10 + [pl.BlockSpec(memory_space=pltpu.SMEM)],
        out_specs=[hbm] * 4 + [vmem] * 3,
        out_shape=kept
        + [jax.ShapeDtypeStruct((24, 128), F32), jax.ShapeDtypeStruct((8, 128), jnp.int32)]
        + [jax.ShapeDtypeStruct((conv_tiles(36), 8, 128), F32)],
        scratch_shapes=[
            pltpu.VMEM(low_map.shape, BF16),
            pltpu.VMEM(skip_map.shape, BF16),
            pltpu.VMEM(target.shape, BF16),
            pltpu.VMEM((3, 192, 64), BF16),
            pltpu.VMEM((3, 192, 64), BF16),
            pltpu.VMEM((4, 1, 64), F32),
            pltpu.VMEM(index.shape, jnp.int32),
        ]
        + [pltpu.VMEM(array.shape, array.dtype) for array in kept]
        + [
            pltpu.VMEM((2 * PAD + (images * low_r + 8) * pitch, 128), F32),
            pltpu.VMEM((2 * PAD + (images * skip_r + 8) * wide, 128), F32),
            pltpu.VMEM((rounded_up(h + 4, 8) * pitch, 128), F32),
            pltpu.VMEM((2 * PAD + skip_r * pitch, 128), F32),
            pltpu.VMEM((2 * skip_r * pitch, 128), F32),
            pltpu.VMEM((768, 128), BF16),
            pltpu.VMEM((768, 128), BF16),
            pltpu.VMEM((256, 256), F32),
            pltpu.VMEM(((h + 4) * w, 128), F32),
            pltpu.VMEM((2, images, 3, w, 64), BF16),
            pltpu.VMEM((2, images, 3, breadth, 64), BF16),
            pltpu.VMEM((2, 3 * half, rounded_up(h, 16), 128), BF16),
            pltpu.VMEM((2, 3 * half, rounded_up(h, 16), 128), BF16),
            pltpu.VMEM((2, 4, half, 32, 128), BF16),
            pltpu.VMEM((2, 3 * half, rounded_up(height, 16), 128), BF16),
            pltpu.VMEM((2, 3 * half, rounded_up(height, 16), 128), BF16),
            pltpu.VMEM((2, 4, half, 32, 128), BF16),
            total_scratch(8),
            total_scratch(8),
            pltpu.SemaphoreType.DMA((10,)),
            pltpu.SemaphoreType.DMA((4, max(images, 2))),
            pltpu.SemaphoreType.DMA((2, 2, 8)),
        ],
        compiler_params=pltpu.CompilerParams(
            collective_id=1, has_side_effects=True, vmem_limit_bytes=60 * MIB
        ),
        name="rise",
    )(
        low_map,
        skip_map,
        target,
        conv_one,
        conv_two,
        gain_one,
        shift_one,
        gain_two,
        shift_two,
        index,
        count,
    )


def levels_of(tiles):
    batch, row, col = place()
    batches, rows, cols = extents()
    pairs = 2 if cols % 2 == 0 else 1
    outer = cols // pairs
    levels = []

    def add(count, mine, device_of):
        left = (levels[-1][3] if levels else tiles) // count
        partners = []
        for over in range(1, count):
            other = lax.rem(mine + over, count)
            partners.append((other, device_of(other)))
        levels.append((count, mine, partners, left))

    low = lax.rem(col, pairs)
    add(pairs, low, lambda k: (batch, row, col - low + k))
    add(
        outer * batches,
        lax.div(col, pairs) * batches + batch,
        lambda k: (lax.rem(k, batches), row, lax.div(k, batches) * pairs + low),
    )
    add(rows, row, lambda k: (batch, k, col))
    return levels


def level_sizes(tiles):
    batches, rows, cols = extents()
    pairs = 2 if cols % 2 == 0 else 1
    sizes = []
    for count in (pairs, cols // pairs * batches, rows):
        tiles = tiles // count
        sizes.append((count, tiles))
    return sizes


class Scatter:
    def __init__(self, source, mids, slots, sems):
        self.parts = [source, *mids]
        self.slots, self.sems = slots, sems
        self.levels = levels_of(source.shape[0])

    def begin(self, level):
        _, _, partners, left = self.levels[level]
        self.copies = [
            remote(
                self.parts[level].at[pl.ds(other * left, left)],
                self.slots[level].at[k],
                self.sems.at[level, 0, k],
                self.sems.at[level, 1, k],
                device,
            )
            for k, (other, device) in enumerate(partners)
        ]
        start_all(self.copies)

    def end(self, level):
        _, mine, partners, left = self.levels[level]
        wait_all(self.copies)
        total = self.parts[level][pl.ds(mine * left, left)].astype(F32)
        for k in range(len(partners)):
            total = total + self.slots[level][k].astype(F32)
        self.parts[level + 1][...] = total.astype(BF16)


class Gather:
    def __init__(self, full, sems):
        self.full, self.sems = full, sems
        self.levels = levels_of(full.shape[0])

    def span(self, level):
        base = 0
        for _, mine, _, left in self.levels[: level + 1]:
            base = base + mine * left
        return pl.ds(base, self.levels[level][3])

    def begin(self, level):
        part = self.full.at[self.span(level)]
        self.copies = [
            remote(part, part, self.sems.at[level, 0, k], self.sems.at[level, 1, k], device)
            for k, (_, device) in enumerate(self.levels[level][2])
        ]
        start_all(self.copies)

    def end(self):
        wait_all(self.copies)


def scatter_scratch(tiles):
    sizes = level_sizes(tiles)
    return (
        tuple(pltpu.VMEM((left, 16, 128), BF16) for _, left in sizes[:-1]),
        tuple(pltpu.VMEM((count - 1, left, 16, 128), BF16) for count, left in sizes),
        level_sems(),
    )


def level_sems():
    return pltpu.SemaphoreType.DMA((3, 2, max(count for count, _ in level_sizes(1)) - 1))


class PlaneReducer:
    def __init__(self, source, slots, mid, row_slots, full, sems):
        batch, row, col = place()
        batches, rows, cols = extents()
        self.source, self.slots, self.mid = source, slots, mid
        self.row_slots, self.full, self.sems = row_slots, full, sems
        self.share = mid.shape[0]
        self.mine = batch * cols + col
        self.row = row

    def begin(self):
        _, _, cols = extents()
        self.copies = []
        for k, (batch, row, col) in enumerate(plane_partners()):
            other = batch * cols + col
            part = self.source.at[pl.ds(other * self.share, self.share)]
            self.copies.append(
                remote(
                    part, self.slots.at[k], self.sems.at[0, 0, k], self.sems.at[0, 1, k],
                    (batch, row, col),
                )
            )
        start_all(self.copies)

    def middle(self):
        wait_all(self.copies)
        total = self.source[pl.ds(self.mine * self.share, self.share)]
        for k in range(self.slots.shape[0]):
            total = total + self.slots[k]
        self.mid[...] = total
        self.copies = [
            remote(
                self.mid, self.row_slots.at[self.row], self.sems.at[1, 0, k],
                self.sems.at[1, 1, k], partner,
            )
            for k, partner in enumerate(row_partners())
        ]
        start_all(self.copies)
        self.row_slots[self.row] = total

    def last(self):
        wait_all(self.copies)
        self.full[pl.ds(self.mine * self.share, self.share)] = slot_sum(self.row_slots)
        part = self.full.at[pl.ds(self.mine * self.share, self.share)]
        self.copies = [
            remote(part, part, self.sems.at[2, 0, k], self.sems.at[2, 1, k], partner)
            for k, partner in enumerate(plane_partners())
        ]
        start_all(self.copies)

    def end(self):
        wait_all(self.copies)


def plane_scratch(tiles):
    batches, rows, cols = extents()
    planes = batches * cols
    share = tiles // planes
    most = max(planes, rows) - 1
    return [
        pltpu.VMEM((tiles, 8, 128), F32),
        pltpu.VMEM((planes - 1, share, 8, 128), F32),
        pltpu.VMEM((share, 8, 128), F32),
        pltpu.VMEM((rows, share, 8, 128), F32),
        pltpu.SemaphoreType.DMA((3, 2, most)),
    ]


def conv_tiles(tiles):
    batches, _, cols = extents()
    planes = batches * cols
    return -(-tiles // planes) * planes


def fold(target, first, grads):
    low = lower_half((1, 128))
    last = grads[0:192, 128:256]
    target[first : first + 24] = grads[0:192, 0:128].reshape(24, 8, 128)
    target[first + 24 : first + 36] = jnp.where(low, last[0:96], swapped(last[96:192])).reshape(
        12, 8, 128
    )
    if target.shape[0] > first + 36:
        target[first + 36 :] = jnp.zeros((target.shape[0] - first - 36, 8, 128), F32)


def unfold(source, first):
    pairs = source[first : first + 24].reshape(192, 128)
    last = source[first + 24 : first + 36].reshape(96, 128)
    return [
        pairs[:, 0:64],
        swapped(pairs)[:, 0:64],
        jnp.concatenate([last[:, 0:64], swapped(last)[:, 0:64]], axis=0),
    ]


def shifted_taps(buffer, rows, line):
    count = (rows + 2) * line
    views = [buffer[(2 - tap) * line : (2 - tap) * line + count, :] for tap in range(3)]
    low = lower_half((1, 128))
    return jnp.concatenate(
        [jnp.where(low, views[0], views[1]), jnp.where(low, views[2], 0.0)], axis=1
    )


def product_of_parts(left, right):
    high = right.astype(BF16)
    rest = (right - high.astype(F32)).astype(BF16)
    return dot_left(left, high) + dot_left(left, rest)


def stack_back(target, source):
    for tap in range(3):
        for e in range(3):
            block = source[tap, 64 * e : 64 * e + 64, :].astype(F32)
            start = 256 * tap + 64 * e
            target[start : start + 64, :] = twice(block.T).astype(BF16)
        target[256 * tap + 192 : 256 * tap + 256, :] = jnp.zeros((64, 128), BF16)


def back_pairs(buffer, start, count):
    low = lower_half((1, 128))
    first = jnp.where(low, buffer[pl.ds(start + 1, count), :], buffer[pl.ds(start, count), :])
    second = jnp.where(low, buffer[pl.ds(start - 1, count), :], 0.0)
    return jnp.concatenate([first, second], axis=1).astype(BF16)


def slope_of(values):
    logistic = 0.5 * jnp.tanh(0.5 * values) + 0.5
    return logistic * (1.0 + values * (1.0 - logistic))


def fall_body(
    spread_ref,
    y_two_ref,
    stat_ref,
    load_ref,
    small_ref,
    tiles_ref,
    y_one_ref,
    merged_ref,
    low_ref,
    conv_ref,
    conv_one_ref,
    skip_out,
    zed_out,
    load_out,
    conv_out,
    conv_x_out,
    sums_out,
    last_out,
    weight_out,
    y_two_s,
    slope_s,
    y_one_s,
    merged_s,
    low_s,
    conv_s,
    load_s,
    skip_s,
    share_s,
    grad_x,
    zed_x,
    own_s,
    own_low_s,
    pair_s,
    narrow_s,
    w_two,
    g_two,
    g_one,
    total_s,
    strip_send,
    strip_recv,
    side_send,
    side_recv,
    corners,
    zed_send,
    zed_recv,
    edge_send,
    edge_recv,
    zed_corners,
    third_scratch,
    fourth_scratch,
    load_scratch,
    conv_x_scratch,
    conv_scratch,
    gather_sems,
    in_sems,
    map_sems,
    out_sems,
    strip_sems,
    zed_sems,
):
    images, rows, wide, _ = y_two_ref.shape
    height, breadth = rows - 4, wide - 16
    h, w = height // 2, breadth // 2
    pitch, ext = w + 16, height + 2
    zed_rows = h + 2
    half = images // 2
    _, row_at, col_at = place()
    batches, row_count, col_count = extents()
    cells_high = float(images * batches * height * row_count * breadth * col_count)
    low_half = lower_half((1, 128))
    mean_one, scale_one = stat_ref[0:1, :], stat_ref[1:2, :]
    mean_two, scale_two = stat_ref[2:3, :], stat_ref[3:4, :]
    gain_one, shift_one = stat_ref[6:7, :], stat_ref[7:8, :]
    gain_two, shift_two = stat_ref[8:9, :], stat_ref[9:10, :]
    top, bottom = stat_ref[10:11, :], stat_ref[11:12, :]
    left, right = stat_ref[12:13, :], stat_ref[13:14, :]

    def spread_load(b):
        start = PAD + (b * rows + 1) * wide
        return pltpu.make_async_copy(
            spread_ref.at[b], grad_x.at[pl.ds(start, ext * wide)], map_sems.at[0, b]
        )

    def y_two_load(b):
        return pltpu.make_async_copy(y_two_ref.at[b], y_two_s.at[b], map_sems.at[1, b])

    loads = [
        pltpu.make_async_copy(source, target, in_sems.at[k])
        for k, (source, target) in enumerate(
            (
                (load_ref, load_s),
                (tiles_ref, conv_x_scratch[0]),
                (conv_ref, conv_s.at[0]),
                (conv_one_ref, conv_s.at[1]),
                (merged_ref, merged_s),
                (y_one_ref, y_one_s),
                (low_ref, low_s),
            )
        )
    ]
    for b in range(images):
        spread_load(b).start()
    for b in range(images):
        y_two_load(b).start()
    for load in loads:
        load.start()
    grad_x[0:PAD, :] = jnp.zeros((PAD, 128), F32)
    tail = PAD + images * rows * wide
    grad_x[tail:, :] = jnp.zeros((grad_x.shape[0] - tail, 128), F32)
    for b in range(images):
        for line in (0, ext + 1):
            start = PAD + (b * rows + line) * wide
            grad_x[start : start + wide, :] = jnp.zeros((wide, 128), F32)
    greet()
    for b in range(images):
        spread_load(b).wait()
    for pair in range(half):
        for side, first in enumerate((1, ext - 2)):
            parts = []
            for image in (pair, pair + half):
                start = PAD + (image * rows + first) * wide
                parts.append(grad_x[start : start + 3 * wide, :])
            strip_send[side, pair] = jnp.where(low_half, parts[0], parts[1]).astype(BF16)
    around = Around(
        [strip_send.at[k] for k in range(2)]
        + [side_send.at[k] for k in range(2)]
        + [corners.at[0, k] for k in range(4)],
        [strip_recv.at[k] for k in range(2)]
        + [side_recv.at[k] for k in range(2)]
        + [corners.at[1, k] for k in range(4)],
        strip_sems,
    )
    around.start(range(2))
    for side, first in enumerate((7, 6 + breadth)):
        pack_columns(grad_x, side_send.at[side], images, rows, wide, 1, first, 3)
    for k, (up, along) in enumerate(AROUND[4:]):
        pack_corner(
            grad_x,
            corners.at[0, k],
            images,
            rows,
            wide,
            1 if up < 0 else height,
            7 if along < 0 else 6 + breadth,
            3,
        )
    around.start(range(2, 8))
    loads[0].wait()
    load_sum = Scatter(load_s, (*load_scratch[0], share_s), load_scratch[1], load_scratch[2])
    load_sum.begin(0)

    def begin(b, sums):
        y_two_load(b).wait()
        start = PAD + b * rows * wide
        clear(
            grad_x,
            start,
            rows,
            wide,
            (1, 2),
            (ext, ext + 1),
            (7, 8),
            (8 + breadth, 9 + breadth),
        )
        normed = (y_two_s[b] - mean_two) * scale_two
        slope = slope_of(normed * gain_two + shift_two)
        slope_s[b] = slope
        part = grad_x[pl.ds(start, rows * wide), :].reshape(rows, wide, 128)
        weighted = part * slope
        return sums[0] + fold_sum(weighted), sums[1] + fold_sum(weighted * normed)

    nothing = jnp.zeros((8, 128), F32)
    sums = lax.fori_loop(0, images, begin, (nothing, nothing))
    sum_src = third_scratch[0]
    sum_src[...] = jnp.zeros((16, 128), F32)
    sum_src[0:8, :] = small_ref[...]
    sum_src[8:9, :] = jnp.sum(sums[0], axis=0, keepdims=True)
    sum_src[9:10, :] = jnp.sum(sums[1], axis=0, keepdims=True)
    third_total = Total(*third_scratch)
    third_total.begin()
    load_sum.end(0)
    load_sum.begin(1)
    loads[2].wait()
    stack_back(w_two, conv_s.at[0])
    loads[3].wait()
    stack_back(weight_out, conv_s.at[1])
    g_two[...] = jnp.zeros_like(g_two)
    g_one[...] = jnp.zeros_like(g_one)
    own_s[...] = jnp.zeros_like(own_s)
    own_low_s[...] = jnp.zeros_like(own_low_s)
    narrow_s[...] = jnp.zeros_like(narrow_s)
    zed_x[...] = jnp.zeros_like(zed_x)
    third_total.middle()
    around.wait()

    def use(k):
        up, along = AROUND[k]
        row = height + 1 if up < 0 else 0
        column = 7 + breadth if along < 0 else 6
        if k < 2:
            for image in range(images):
                values = unpacked(strip_recv[k, image % half].astype(F32), image, images)
                start = PAD + (image * rows + row) * wide
                grad_x[start : start + 3 * wide, :] += values
        elif k < 4:
            unpack_columns(
                grad_x, side_recv.at[k - 2], images, rows, wide, 1, column, 3, ext, True
            )
        else:
            unpack_corner(
                grad_x, corners.at[1, k - 4], images, rows, wide, row, column, 3, True
            )

    around.each(use)

    loads[1].wait()
    conv_x_sum = PlaneReducer(*conv_x_scratch[:4], conv_x_out, conv_x_scratch[4])
    totals = third_total.end()
    sums_out[...] = totals
    conv_x_sum.begin()
    load_sum.end(1)
    load_sum.begin(2)
    factor_two = gain_two * scale_two
    shift_part, gain_part = totals[8:9] / cells_high, totals[9:10] / cells_high
    for k in (4, 5, 6):
        loads[k].wait()
    column = lax.broadcasted_iota(jnp.int32, (wide, 128), 0)
    keep = jnp.where(column < 8, left, 1.0)
    keep = jnp.where(column >= 8 + breadth, right, keep)

    def merge(b, sums):
        start = PAD + b * rows * wide
        whole = pl.ds(start, rows * wide)
        normed = (y_two_s[b] - mean_two) * scale_two
        grad_z = grad_x[whole, :].reshape(rows, wide, 128) * slope_s[b]
        grad_y = factor_two * (grad_z - shift_part - normed * gain_part)
        grad_y = (grad_y * keep).astype(BF16).astype(F32)
        grad_x[whole, :] = grad_y.reshape(rows * wide, 128)
        for line, flag in ((0, top), (ext, bottom)):
            span = pl.ds(start + line * wide, 2 * wide)
            grad_x[span, :] = grad_x[span, :] * flag
        own_s[2 * breadth : (height + 2) * breadth, :] = grad_y[
            2 : height + 2, 8 : 8 + breadth
        ].reshape(height * breadth, 128)
        source = merged_s[b].reshape(ext * breadth, 256)
        g_two[...] += dot_left(source, shifted_taps(own_s, height, breadth).astype(BF16))
        pair_s[...] = back_pairs(grad_x, start, rows * wide)
        count = ext * wide
        taps = jnp.concatenate(
            [pair_s[wide * (2 - a) : wide * (2 - a) + count, :] for a in range(3)], axis=1
        )
        merged_grad = dot(taps, w_two[...]).reshape(ext, wide, 128)
        skip_s[b] = merged_grad[1 : height + 1, 8 : 8 + breadth, 0:64]
        pltpu.make_async_copy(skip_s.at[b], skip_out.at[b], out_sems.at[0, b]).start()
        fine = (merged_grad * keep).astype(BF16).astype(F32).reshape(h + 1, 2, wide, 128)
        even, odd = fine[:, 0], fine[:, 1]
        even = jnp.concatenate([even[0:1] * top, even[1:]], axis=0)
        odd = jnp.concatenate([odd[:-1], odd[-1:] * bottom], axis=0)
        short = 0.75 * (odd[:-1] + even[1:]) + 0.25 * (even[:-1] + odd[1:])
        side = jnp.zeros((h, 8, 128), F32)
        count = h * 2 * pitch
        narrow_s[PAD : PAD + count, :] = jnp.concatenate([side, short, side], axis=1).reshape(
            count, 128
        )
        lines = [narrow_s[pl.ds(PAD + k, count // 2, stride=2), :] for k in (-1, 0, 1, 2)]
        act_grad = 0.75 * (lines[1] + lines[2]) + 0.25 * (lines[0] + lines[3])
        act_grad = act_grad.reshape(h, pitch, 128)
        normed = (y_one_s[b, 2 : h + 2] - mean_one) * scale_one
        slope = slope_of(normed * gain_one + shift_one)
        place_at = lax.broadcasted_iota(jnp.int32, (pitch, 128), 0)
        inner = jnp.logical_and(place_at >= 8, place_at < 8 + w)
        grad_z = jnp.where(inner, act_grad * slope, 0.0)
        spot = PAD + (b * zed_rows + 1) * pitch
        zed_x[pl.ds(spot, h * pitch), :] = grad_z.reshape(h * pitch, 128)
        own_low_s[2 * w : (h + 2) * w, :] = grad_z[:, 8 : 8 + w].reshape(h * w, 128)
        g_one[...] += product_of_parts(
            low_s[b].reshape((h + 2) * w, 256), shifted_taps(own_low_s, h, w)
        )
        return sums[0] + fold_sum(grad_z), sums[1] + fold_sum(grad_z * normed)

    sums = lax.fori_loop(0, half, merge, (nothing, nothing))
    gather = Gather(load_out, gather_sems)
    load_sum.end(2)
    load_out[gather.span(2)] = share_s[...]
    gather.begin(2)
    conv_x_sum.middle()
    sums = lax.fori_loop(half, images, merge, sums)
    last_src = fourth_scratch[0]
    last_src[...] = jnp.zeros((8, 128), F32)
    last_src[0:1, :] = jnp.sum(sums[0], axis=0, keepdims=True)
    last_src[1:2, :] = jnp.sum(sums[1], axis=0, keepdims=True)
    fourth_total = Total(*fourth_scratch)
    fourth_total.begin()
    gather.end()
    gather.begin(1)
    fold(conv_scratch[0], 0, g_two)
    fold(conv_scratch[0], 36, g_one)
    conv_sum = PlaneReducer(*conv_scratch[:4], conv_out, conv_scratch[4])
    conv_sum.begin()
    for pair in range(half):
        for side, line in enumerate((1, h)):
            parts = []
            for image in (pair, pair + half):
                start = PAD + (image * zed_rows + line) * pitch
                parts.append(zed_x[start : start + pitch, :])
            zed_send[side, pair] = jnp.where(low_half, parts[0], parts[1])
    for side, column in enumerate((8, 7 + w)):
        pack_columns(zed_x, edge_send.at[side], images, zed_rows, pitch, 1, column, 1)
    for k, (up, along) in enumerate(AROUND[4:]):
        pack_corner(
            zed_x,
            zed_corners.at[0, k],
            images,
            zed_rows,
            pitch,
            1 if up < 0 else h,
            8 if along < 0 else 7 + w,
            1,
        )
    zed_around = Around(
        [zed_send.at[k] for k in range(2)]
        + [edge_send.at[k] for k in range(2)]
        + [zed_corners.at[0, k] for k in range(4)],
        [zed_recv.at[k] for k in range(2)]
        + [edge_recv.at[k] for k in range(2)]
        + [zed_corners.at[1, k] for k in range(4)],
        zed_sems,
    )
    zed_around.start()
    fourth_total.middle()
    conv_x_sum.last()
    conv_sum.middle()
    zed_around.wait()

    def use_zed(k):
        up, along = AROUND[k]
        row = h + 1 if up < 0 else 0
        column = 8 + w if along < 0 else 7
        if k < 2:
            for image in range(images):
                start = PAD + (image * zed_rows + row) * pitch
                zed_x[start : start + pitch, :] = unpacked(
                    zed_recv[k, image % half], image, images
                )
        elif k < 4:
            unpack_columns(
                zed_x, edge_recv.at[k - 2], images, zed_rows, pitch, 1, column, 1, h, False
            )
        else:
            unpack_corner(
                zed_x, zed_corners.at[1, k - 4], images, zed_rows, pitch, row, column, 1, False
            )

    zed_around.each(use_zed)

    def zed_store(b):
        return pltpu.make_async_copy(
            zed_x.at[pl.ds(PAD + b * zed_rows * pitch, zed_rows * pitch)],
            zed_out.at[b],
            out_sems.at[1, b],
        )

    for b in range(images):
        zed_store(b).start()
    last_out[...] = fourth_total.end()
    conv_sum.last()
    gather.end()
    gather.begin(0)
    conv_x_sum.end()
    conv_sum.end()
    gather.end()
    for b in range(images):
        zed_store(b).wait()
        pltpu.make_async_copy(skip_s.at[b], skip_out.at[b], out_sems.at[0, b]).wait()


def fall(
    spread, y_two, stats, load, small, tiles_x, y_one, merged, low, conv_two, conv_one
):
    images, rows, wide, _ = y_two.shape
    height, breadth = rows - 4, wide - 16
    h, w = height // 2, breadth // 2
    pitch, ext, zed_rows = w + 16, height + 2, h + 2
    half = images // 2
    tiles, parts_x, parts = load.shape[0], tiles_x.shape[0], conv_tiles(72)
    vmem = pl.BlockSpec(memory_space=pltpu.VMEM)
    hbm = pl.BlockSpec(memory_space=pl.ANY)
    lines, low_lines = rounded_up(ext, 16), rounded_up(h, 8)
    return pl.pallas_call(
        fall_body,
        in_specs=[hbm] * 2 + [vmem, hbm, vmem] + [hbm] * 6,
        out_specs=[hbm] * 2 + [vmem] * 6,
        out_shape=[
            jax.ShapeDtypeStruct((images, height, breadth, 64), F32),
            jax.ShapeDtypeStruct((images, zed_rows * pitch, 128), F32),
            jax.ShapeDtypeStruct((tiles, 16, 128), BF16),
            jax.ShapeDtypeStruct((parts, 8, 128), F32),
            jax.ShapeDtypeStruct((parts_x, 8, 128), F32),
            jax.ShapeDtypeStruct((16, 128), F32),
            jax.ShapeDtypeStruct((8, 128), F32),
            jax.ShapeDtypeStruct((768, 128), BF16),
        ],
        scratch_shapes=[
            pltpu.VMEM(y_two.shape, F32),
            pltpu.VMEM(y_two.shape, F32),
            pltpu.VMEM(y_one.shape, F32),
            pltpu.VMEM(merged.shape, BF16),
            pltpu.VMEM(low.shape, BF16),
            pltpu.VMEM((2, 3, 192, 64), BF16),
            pltpu.VMEM(load.shape, BF16),
            pltpu.VMEM((images, height, breadth, 64), F32),
            pltpu.VMEM((level_sizes(tiles)[-1][1], 16, 128), BF16),
            pltpu.VMEM((2 * PAD + (images * rows + lines - ext) * wide, 128), F32),
            pltpu.VMEM((2 * PAD + (images * zed_rows + 8) * pitch, 128), F32),
            pltpu.VMEM(((height + 4) * breadth, 128), F32),
            pltpu.VMEM(((h + 4) * w, 128), F32),
            pltpu.VMEM((rows * wide, 256), BF16),
            pltpu.VMEM((2 * PAD + h * 2 * pitch, 128), F32),
            pltpu.VMEM((768, 128), BF16),
            pltpu.VMEM((256, 256), F32),
            pltpu.VMEM((256, 256), F32),
            pltpu.VMEM((2, 8, 128), F32),
            pltpu.VMEM((2, half, 3 * wide, 128), BF16),
            pltpu.VMEM((2, half, 3 * wide, 128), BF16),
            pltpu.VMEM((2, 3 * half, lines, 128), BF16),
            pltpu.VMEM((2, 3 * half, lines, 128), BF16),
            pltpu.VMEM((2, 4, half, 32, 128), BF16),
            pltpu.VMEM((2, half, pitch, 128), F32),
            pltpu.VMEM((2, half, pitch, 128), F32),
            pltpu.VMEM((2, half, low_lines, 128), F32),
            pltpu.VMEM((2, half, low_lines, 128), F32),
            pltpu.VMEM((2, 4, half, 8, 128), F32),
            total_scratch(16),
            total_scratch(8),
            scatter_scratch(tiles),
            plane_scratch(parts_x),
            plane_scratch(parts),
            level_sems(),
            pltpu.SemaphoreType.DMA((7,)),
            pltpu.SemaphoreType.DMA((2, images)),
            pltpu.SemaphoreType.DMA((2, images)),
            pltpu.SemaphoreType.DMA((2, 8)),
            pltpu.SemaphoreType.DMA((2, 8)),
        ],
        compiler_params=pltpu.CompilerParams(
            collective_id=2, has_side_effects=True, vmem_limit_bytes=60 * MIB
        ),
        name="fall",
    )(spread, y_two, stats, load, small, tiles_x, y_one, merged, low, conv_two, conv_one)


def finish_body(
    cells_low,
    load_ref,
    rest_ref,
    conv_ref,
    conv_x_ref,
    sums_ref,
    last_ref,
    stat_ref,
    zed_ref,
    y_one_ref,
    weight_ref,
    skip_ref,
    conv_one_out,
    gain_one_out,
    shift_one_out,
    conv_two_out,
    gain_two_out,
    shift_two_out,
    head_out,
    head_b_out,
    heat_w_out,
    heat_b_out,
    box_w_out,
    box_b_out,
    low_out,
    skip_out,
    zed_x,
):
    step = pl.program_id(0)
    each, h, w, _ = low_out.shape
    pitch = w + 16
    rows = h + 2
    factor = stat_ref[6:7, :] * stat_ref[1:2, :]
    shift_low, gain_low = last_ref[0:1, :] / cells_low, last_ref[1:2, :] / cells_low
    skip_out[...] = skip_ref[...]
    for column in range(head_out.shape[3] // 128):
        block = load_ref[36 * column : 36 * column + 36].astype(F32)
        head_out[:, :, :, 128 * column : 128 * column + 128] = block.reshape(3, 3, 64, 128)

    @pl.when(step == 0)
    def _():
        zed_x[0:PAD, :] = jnp.zeros((PAD, 128), F32)
        zed_x[PAD + rows * pitch :, :] = jnp.zeros((PAD, 128), F32)
        spread = stat_ref[16:24, :].T
        ones = unfold(conv_ref, 36)
        normed = unfold(conv_x_ref, 0)
        for tap, part in enumerate(unfold(conv_ref, 0)):
            conv_two_out[tap] = part.reshape(3, 64, 64)
            count = jnp.concatenate(
                [spread[:, 2 * tap : 2 * tap + 1], spread[0:64, 2 * tap + 1 : 2 * tap + 2]], axis=0
            )
            value = ones[tap] - count * shift_low[:, 0:64] - normed[tap] * gain_low[:, 0:64]
            conv_one_out[tap] = (value * factor[:, 0:64]).reshape(3, 64, 64)
        for column in range(6):
            span = slice(128 * column, 128 * column + 128)
            head_b_out[span] = sums_ref[column : column + 1, :].reshape(128)
        for part in range(2):
            span = slice(128 * part, 128 * part + 128)
            heat_w_out[:, span] = rest_ref[5 * part : 5 * part + 5].astype(F32).reshape(80, 128)
            for box in range(2):
                block = rest_ref[10 + 2 * box + part].astype(F32)
                box_w_out[box, :, span] = block[2 * box : 2 * box + 2, :]
            box_b_out[part : part + 1, :] = sums_ref[7:8, 2 * part : 2 * part + 2]
        heat_b_out[...] = sums_ref[6:7, 0:80]
        shift_two_out[...] = sums_ref[8:9, 0:64]
        gain_two_out[...] = sums_ref[9:10, 0:64]
        shift_one_out[...] = last_ref[0:1, 0:64]
        gain_one_out[...] = last_ref[1:2, 0:64]

    for b in range(each):
        normed = (y_one_ref[b, 1 : h + 3] - stat_ref[0:1, :]) * stat_ref[1:2, :]
        grad_z = zed_ref[b].reshape(rows, pitch, 128)
        grad_y = factor * (grad_z - shift_low - normed * gain_low)
        column = lax.broadcasted_iota(jnp.int32, (pitch, 128), 0)
        keep = jnp.where(column < 8, stat_ref[12:13, :], 1.0)
        keep = jnp.where(column >= 8 + w, stat_ref[13:14, :], keep)
        grad_y = (grad_y * keep).astype(BF16).astype(F32)
        zed_x[PAD : PAD + rows * pitch, :] = grad_y.reshape(rows * pitch, 128)
        for line, row in ((0, 10), (rows - 1, 11)):
            span = slice(PAD + line * pitch, PAD + (line + 1) * pitch)
            zed_x[span, :] = zed_x[span, :] * stat_ref[row : row + 1, :]
        pairs = back_pairs(zed_x, PAD, rows * pitch)
        count = h * pitch
        taps = jnp.concatenate(
            [pairs[pitch * (2 - a) : pitch * (2 - a) + count] for a in range(3)], axis=1
        )
        grad = dot(taps, weight_ref[...]).reshape(h, pitch, 128)
        low_out[b] = grad[:, 8 : 8 + w, 0:64]


def finish(load, conv, conv_x, sums, last, stats, zed, y_one, weight, skip):
    images, y_rows, pitch, _ = y_one.shape
    h, w = y_rows - 4, pitch - 16
    batches, row_count, col_count = extents()
    cells = float(images * batches * h * row_count * w * col_count)
    span = zed.shape[1]
    steps = 2
    each = images // steps
    shapes = [
        (3, 3, 64, 64),
        (1, 64),
        (1, 64),
        (3, 3, 64, 64),
        (1, 64),
        (1, 64),
        (3, 3, 64, 768),
        (768,),
        (80, 256),
        (1, 80),
        (2, 2, 256),
        (2, 2),
        (images, h, w, 64),
        skip.shape,
    ]
    whole = lambda shape: pl.BlockSpec(shape, lambda c: (0,) * len(shape))
    part = lambda shape: pl.BlockSpec(shape, lambda c: (c,) + (0,) * (len(shape) - 1))
    out_specs = [whole(shape) for shape in shapes]
    out_specs[6] = pl.BlockSpec((3, 3, 64, 768 // steps), lambda c: (0, 0, 0, c))
    out_specs[12] = part((each, h, w, 64))
    out_specs[13] = part((each,) + skip.shape[1:])
    return pl.pallas_call(
        functools.partial(finish_body, cells),
        grid=(steps,),
        in_specs=[
            part((216 // steps, 16, 128)),
            pl.BlockSpec((36, 16, 128), lambda c: (6, 0, 0)),
        ]
        + [whole(array.shape) for array in (conv, conv_x, sums, last, stats)]
        + [
            part((each, span, 128)),
            part((each, y_rows, pitch, 128)),
            whole(weight.shape),
            part((each,) + skip.shape[1:]),
        ],
        out_specs=out_specs,
        out_shape=[jax.ShapeDtypeStruct(shape, F32) for shape in shapes],
        scratch_shapes=[
            pltpu.VMEM((2 * PAD + span, 128), F32),
        ],
        compiler_params=pltpu.CompilerParams(vmem_limit_bytes=60 * MIB),
        name="finish",
    )(load, load, conv, conv_x, sums, last, stats, zed, y_one, weight, skip)


def local(
    low_map,
    skip_map,
    conv_first,
    gain_first,
    shift_first,
    conv_second,
    gain_second,
    shift_second,
    head_conv,
    head_bias,
    heat_weight,
    heat_bias,
    box_weight,
    box_bias,
    heat_target,
    box_target,
    obj_index,
    obj_count,
):
    batches, rows, cols = extents()
    devices = batches * rows * cols
    conv_one = conv_first.reshape(3, 192, 64)
    conv_two = conv_second.reshape(3, 192, 64)
    y_two, y_one, merged, low, stats, spot, tiles_x = rise(
        low_map,
        skip_map,
        heat_target,
        conv_one,
        conv_two,
        gain_first.reshape(1, 64),
        shift_first.reshape(1, 64),
        gain_second.reshape(1, 64),
        shift_second.reshape(1, 64),
        obj_index,
        obj_count,
    )
    heat_map, box_map, spread, load, small = heads(
        y_two,
        heat_target,
        spot,
        box_target.transpose(0, 2, 1),
        stats,
        head_conv.reshape(3, 192, 768),
        head_bias,
        heat_weight.T,
        heat_bias.reshape(1, 80),
        box_weight.transpose(0, 2, 1),
        box_bias,
        devices,
    )
    images, ext, wide, _ = spread.shape
    grad_skip, zed, load, conv, conv_x, sums, last, weight = fall(
        spread.reshape(images, ext * wide, 128),
        y_two,
        stats,
        load,
        small,
        tiles_x,
        y_one,
        merged,
        low,
        conv_two,
        conv_one,
    )
    grads = finish(load, conv, conv_x, sums, last, stats, zed, y_one, weight, grad_skip)
    return (
        heat_map,
        box_map.transpose(0, 1, 3, 2),
        grads[12],
        grads[13],
        grads[0],
        grads[1].reshape(64),
        grads[2].reshape(64),
        grads[3],
        grads[4].reshape(64),
        grads[5].reshape(64),
        grads[6],
        grads[7],
        grads[8].T,
        grads[9].reshape(80),
        grads[10].transpose(0, 2, 1),
        grads[11],
    )


def solution(mesh):
    tile = P("batch", "row", "col", None)
    return jax.shard_map(
        local,
        mesh=mesh,
        in_specs=(tile, tile)
        + (P(),) * 12
        + (tile, P("batch", None, None), P("batch", None), P("batch")),
        out_specs=(tile,) * 4 + (P(),) * 12,
        check_vma=False,
    )
```

time: 618 us -> 117 us (0.19); the launches traced: 607 us -> 117 us
  blocking collectives: 168 us -> 0 us
  waiting for transfers between devices: 148 us -> 0 us
  Pallas kernels: 0 us -> 116 us
  matrix products: 88.9 us -> 0 us
  starting transfers between devices: 67.2 us -> 0 us
  local copies, waits for them, and re-layouts: 65.8 us -> 0 us
  other arithmetic: 51.5 us -> 0 us
  between operations: 17.5 us -> 0.83 us
    psum x4 -> x0, blocking collectives: 168 us -> none  [the longest x1 43.1 us: local(): lax.psum((jnp.sum(grad_z_two, axis=reduce_axes), jnp.sum(grad_z_two * nor...]
    psum x1 -> x0, waiting for transfers between devices: 127 us -> none  [local(): lax.psum((conv_one_grad, conv_two_grad, head_w_grad, head_b_grad, heat_w_...]
    pallas_call x0 -> x4, Pallas kernels: none -> 116 us  [the longest x1 46 us: fall(): pl.pallas_call(fall_body, in_specs=[hbm] * 2 + [vmem, hbm, vmem] + [hbm]...]
    dot_general x44 -> x0, matrix products: 88.9 us -> none  [the longest x27 40.4 us: transpose_conv(): jnp.dot(window, kernel[row_tap, col_tap].T, preferred_element_type=jnp.fl...]
    ppermute x28 -> x0, starting transfers between devices: 67.2 us -> none  [the longest x14 49.1 us: extended(): lax.ppermute(lax.slice_in_dim(block, block.shape[dim] - width, None, axis...]
    concatenate x6 -> x0, local copies, waits for them, and re-layouts: 31.5 us -> none  [the longest x4 31.4 us: patches(): return jnp.concatenate(pieces, axis=-1)]
    slice x18 -> x0, local copies, waits for them, and re-layouts: 22 us -> none  [the longest x4 8.41 us: patches(): padded[:, row_tap:row_tap + height, col_tap:col_tap + breadth, :]]
    ppermute x28 -> x0, waiting for transfers between devices: 21.4 us -> none  [the longest x14 17.8 us: extended(): lax.ppermute(lax.slice_in_dim(block, 0, width, axis=dim), axis, backward)]
  transfers between devices with their start and end apart: 29 -> 0, of which waited for: 11 -> 0; matrix products, arithmetic and copies ran while one was open for 5% -> 0% of each run, Pallas kernels for 0% -> 0%
where the time goes in v1:
time: 117 us
  Pallas kernels  116 us (99%)
    pallas_call x1, Pallas kernels, fall(): pl.pallas_call(fall_body, in_specs=[hbm] * 2 + [vmem, hbm, vmem] + [hbm]...  46 us
    pallas_call x1, Pallas kernels, rise(): pl.pallas_call(rise_body, in_specs=[hbm] * 10 + [pl.BlockSpec(memory_spac...  34.7 us
    pallas_call x1, Pallas kernels, heads(): pl.pallas_call(functools.partial(heads_body, chunks, breadth * lax.axis_s...  29.8 us
    pallas_call x1, Pallas kernels, finish(): pl.pallas_call(functools.partial(finish_body, cells), grid=(steps,), in_s...  5.22 us

profile of v1, /device:TPU:0, one launch (start us, length us, event | category | flops | bytes accessed | tf_op | source)
XLA Modules:
  0.0 116.5 jit_solution(4842913555059363154)
XLA Ops:
  0.6 34.7 %rise.1 = (f32[4,36,48,128]{3,2,1,0:T(8,128)}, f32[4,20,32,128]{3,2,1,0:T(8,128)}, bf16[4,34,32,256]{3,2,1,0:T(8,128)(2,1)}, bf16[4,18,16,256]{3,2,1,0:T(8,128)(...) custom-call(bf16[4,16,16,64]{3,2,1,0:T(8,128)(2,1)} %low_ref.1, ...), custom_call_target="tpu_custom_call" | custom-call | tf_op jit(solution)/shard_map/rise/pallas_call | solution.py:1028
  35.4 29.8 %heads.1 = (f32[4,32,32,80]{3,2,1,0:T(8,128)}, f32[4,32,4,32]{3,2,1,0:T(4,128)}, f32[4,34,48,128]{3,2,1,0:T(8,128)}, bf16[256,16,128]{2,1,0:T(8,128)(2,1)}, f32[8,128]{1,0:T(8,128)}) custom-call(f32[4,36,48,128]{3,2,1,0:T(8,128)} %get-tuple-element.50.y_two_ref, bf16[4,32,32,80]{3,2,1,0:T(8,128)(2,1)} %target_ref.3, s32[8,128]{1,0:T(8,128)} %get-tuple-element.51.spot_ref, ...), custom_call_target="tpu_custom_call" | custom-call | flops 10871635968 | bytes 12582912 | tf_op jit(solution)/shard_map/heads/pallas_call | solution.py:246
  65.2 46.0 %fall.1 = (f32[4,32,32,64]{3,2,1,0:T(8,128)}, f32[4,576,128]{2,1,0:T(8,128)}, bf16[256,16,128]{2,1,0:T(8,128)(2,1)}, f32[72,8,128]{2,1,0:T(8,128)}, f32[40,8,128...) custom-call(f32[4,1632,128]{2,1,0:T(8,128)} %bitcast.20, ...), custom_call_target="tpu_custom_call" | custom-call | tf_op jit(solution)/shard_map/fall/pallas_call | solution.py:1709
  111.1 5.2 %finish.1 = (f32[3,3,64,64]{3,2,1,0:T(8,128)}, f32[1,64]{1,0:T(1,128)}, f32[1,64]{1,0:T(1,128)}, f32[3,3,64,64]{3,2,1,0:T(8,128)}, f32[1,64]{1,0:T(1,128)}, /*in...) custom-call(bf16[256,16,128]{2,1,0:T(8,128)(2,1)} %get-tuple-element, ...), custom_call_target="tpu_custom_call" | custom-call | tf_op jit(solution)/shard_map/finish/pallas_call | solution.py:1893

commit v2 on v1

--- a/solution.py
+++ b/solution.py
@@ -39,7 +39,6 @@
 
 
 def heads_body(
-    chunks,
     map_side,
     y_two_ref,
     target_ref,
@@ -62,7 +61,6 @@
     kernel_s,
     back_s,
     box_s,
-    goal_s,
     wide_s,
     grad_s,
     heat_grad_s,
@@ -70,13 +68,13 @@
     heat_sum_s,
     box_sum_s,
 ):
-    image = pl.program_id(0)
-    chunk = pl.program_id(1)
-    rows, breadth = target_ref.shape[1], target_ref.shape[2]
-    cells = rows * breadth
+    step = pl.program_id(0)
+    each, height, breadth, _ = target_ref.shape
+    image_cells = height * breadth
+    cells = each * image_cells
     units = 256
 
-    @pl.when(jnp.logical_and(image == 0, chunk == 0))
+    @pl.when(step == 0)
     def _():
         for tap in range(3):
             kernel_s[tap, 0:192, :] = (0.5 * conv_ref[tap].astype(F32)).astype(BF16)
@@ -103,29 +101,25 @@
         box_grad_s[...] = jnp.zeros_like(box_grad_s)
         heat_sum_s[...] = jnp.zeros_like(heat_sum_s)
         box_sum_s[...] = jnp.zeros_like(box_sum_s)
-
-    @pl.when(chunk == 0)
-    def _():
         wide_s[...] = jnp.zeros_like(wide_s)
-        ext, wide = taps_ref.shape[0], breadth + 16
-        normed = (y_two_ref[0, 1 : ext + 1] - stat_ref[2:3, :]) * stat_ref[3:4, :]
+
+    ext, wide = height + 2, breadth + 16
+    column = lax.broadcasted_iota(jnp.int32, (wide, 128), 0)
+    keep = jnp.where(column < 8, stat_ref[12:13, :], 1.0)
+    keep = jnp.where(column >= 8 + breadth, stat_ref[13:14, :], keep)
+    feat_s[0:PAD, :] = jnp.zeros((PAD, 128), F32)
+    feat_s[PAD + ext * wide :, :] = jnp.zeros((PAD, 128), F32)
+    for image in range(each):
+        normed = (y_two_ref[image, 1 : ext + 1] - stat_ref[2:3, :]) * stat_ref[3:4, :]
         feature, _ = silu_parts(normed * stat_ref[8:9, :] + stat_ref[9:10, :])
-        column = lax.broadcasted_iota(jnp.int32, (wide, 128), 0)
-        keep = jnp.where(column < 8, stat_ref[12:13, :], 1.0)
-        keep = jnp.where(column >= 8 + breadth, stat_ref[13:14, :], keep)
-        feat_s[0:PAD, :] = jnp.zeros((PAD, 128), F32)
         feat_s[PAD : PAD + ext * wide, :] = (feature * keep).reshape(ext * wide, 128)
-        feat_s[PAD + ext * wide :, :] = jnp.zeros((PAD, 128), F32)
         for line, row in ((PAD, 10), (PAD + (ext - 1) * wide, 11)):
             feat_s[line : line + wide, :] = feat_s[line : line + wide, :] * stat_ref[row : row + 1]
         pairs = tap_pairs(feat_s, PAD, ext * wide, 1.0)
-        taps_ref[...] = pairs.reshape(ext, wide, 256)[:, 8 : 8 + breadth].astype(BF16)
-        for place, part in enumerate(three_parts(goal_ref[0])):
-            goal_s[place] = part
-
-    first = chunk * rows
+        taps_ref[image] = pairs.reshape(ext, wide, 256)[:, 8 : 8 + breadth].astype(BF16)
+
     taps = jnp.concatenate(
-        [taps_ref[pl.ds(first + tap, rows)].reshape(cells, 256) for tap in range(3)], axis=1
+        [taps_ref[:, tap : tap + height].reshape(cells, 256) for tap in range(3)], axis=1
     )
     active, slope = [], []
     for block in range(3):
@@ -143,8 +137,8 @@
     small = decay * large
     above = logit >= 0.0
     chance = jnp.where(above, large, small)
-    heat_out[0] = chance.reshape(rows, breadth, 80)
-    target = target_ref[0].reshape(cells, 80).astype(F32)
+    heat_out[...] = chance.reshape(each, height, breadth, 80)
+    target = target_ref[...].reshape(cells, 80).astype(F32)
     positive = target == 1.0
     side = jnp.where(positive, jnp.where(above, small, large), chance)
     value = jnp.where(positive, -logit, logit)
@@ -158,14 +152,21 @@
 
     box_bias = jnp.concatenate([box_b_ref[0:1, :], box_b_ref[1:2, :]], axis=1)
     boxes = dot_keep(active[1], box_s[0]) + dot_keep(active[2], box_s[1]) + box_bias
-    box_out[0] = jnp.swapaxes(boxes.reshape(rows, breadth, 4), 1, 2)
-    shape = (rows, breadth, 128)
-    cell = (first + lax.broadcasted_iota(jnp.int32, shape, 0)) * map_side
-    cell = (cell + lax.broadcasted_iota(jnp.int32, shape, 1)).reshape(cells, 128)
-    chosen = (cell == spot_ref[pl.ds(image, 1), :]).astype(F32).astype(BF16)
-    goals = dot_keep(chosen, goal_s[0]) + dot_keep(chosen, goal_s[1])
-    goals = goals + dot_keep(chosen, goal_s[2])
-    hit = dot(chosen, jnp.ones((128, 4), BF16))
+    turned = jnp.swapaxes(boxes.reshape(each * height, breadth, 4), 1, 2)
+    box_out[...] = turned.reshape(each, height, 4, breadth)
+    shape = (height, breadth, 128)
+    cell = lax.broadcasted_iota(jnp.int32, shape, 0) * map_side
+    cell = (cell + lax.broadcasted_iota(jnp.int32, shape, 1)).reshape(image_cells, 128)
+    goals, hits = [], []
+    for image in range(each):
+        spots = spot_ref[pl.ds(step * each + image, 1), :]
+        chosen = (cell == spots).astype(F32).astype(BF16)
+        goal = jnp.zeros((image_cells, 4), F32)
+        for part in three_parts(goal_ref[image]):
+            goal = goal + dot_keep(chosen, part)
+        goals.append(goal)
+        hits.append(dot(chosen, jnp.ones((128, 4), BF16)))
+    goals, hit = jnp.concatenate(goals, axis=0), jnp.concatenate(hits, axis=0)
     miss = boxes - goals
     lane = lax.broadcasted_iota(jnp.int32, (1, 4), 1)
     factor = jnp.where(lane < 2, 0.1, 1.0) * stat_ref[5:6, 0:4]
@@ -189,27 +190,23 @@
     spread = []
     for tap in range(3):
         part = dot(grad_hidden, back_s[:, 256 * tap : 256 * tap + 256])
-        spread.append(part.reshape(rows, breadth, 256))
+        spread.append(part.reshape(each, height, breadth, 256))
     inner = slice(16, 16 + breadth)
-    wide_s[pl.ds(first, 1), inner, :] += spread[0][0:1]
-    wide_s[pl.ds(first + 1, 1), inner, :] += spread[0][1:2] + spread[1][0:1]
-    wide_s[pl.ds(first + 2, rows - 2), inner, :] = (
-        spread[0][2:] + spread[1][1:-1] + spread[2][:-2]
-    )
-    wide_s[pl.ds(first + rows, 1), inner, :] = spread[1][-1:] + spread[2][-2:-1]
-    wide_s[pl.ds(first + rows + 1, 1), inner, :] = spread[2][-1:]
+    for image in range(each):
+        first, second, third = [part[image] for part in spread]
+        wide_s[0:1, inner, :] = first[0:1]
+        wide_s[1:2, inner, :] = first[1:2] + second[0:1]
+        wide_s[2:height, inner, :] = first[2:] + second[1:-1] + third[:-2]
+        wide_s[height : height + 1, inner, :] = second[-1:] + third[-2:-1]
+        wide_s[height + 1 :, inner, :] = third[-1:]
+        centre = swapped(wide_s[:, 8 : 8 + wide, 0:128])
+        total = wide_s[:, 9 : 9 + wide, 0:128] + centre + wide_s[:, 7 : 7 + wide, 128:256]
+        lanes = lax.broadcasted_iota(jnp.int32, total.shape, 2)
+        spread_out[image] = jnp.where(lanes < 64, total, swapped(total))
     for tap in range(3):
         grad_s[tap] += dot_left(taps[:, 256 * tap : 256 * tap + 256], grad_hidden)
 
-    @pl.when(chunk == chunks - 1)
-    def _():
-        reach = breadth + 16
-        centre = pltpu.roll(wide_s[:, 8 : 8 + reach, 0:128], 64, 2)
-        total = wide_s[:, 9 : 9 + reach, 0:128] + centre + wide_s[:, 7 : 7 + reach, 128:256]
-        lanes = lax.broadcasted_iota(jnp.int32, total.shape, 2)
-        spread_out[0] = jnp.where(lanes < 64, total, pltpu.roll(total, 64, 2))
-
-    @pl.when(jnp.logical_and(image == pl.num_programs(0) - 1, chunk == chunks - 1))
+    @pl.when(step == pl.num_programs(0) - 1)
     def _():
         for column in range(6):
             span = slice(128 * column, 128 * column + 128)
@@ -238,19 +235,19 @@
     taps, target, spot, goal, stats, conv, bias, heat_w, heat_b, box_w, box_b, devices
 ):
     images, height, breadth, classes = target.shape
-    rows = height
-    chunks = height // rows
+    each = 1
     tiles = tile_count(devices)
-    whole = lambda *shape: pl.BlockSpec(shape, lambda b, c: (0,) * len(shape))
+    whole = lambda *shape: pl.BlockSpec(shape, lambda b: (0,) * len(shape))
+    part = lambda *shape: pl.BlockSpec((each,) + shape, lambda b: (b,) + (0,) * len(shape))
     cells = images * height * breadth
     return pl.pallas_call(
-        functools.partial(heads_body, chunks, breadth * lax.axis_size("col")),
-        grid=(images, chunks),
+        functools.partial(heads_body, breadth * lax.axis_size("col")),
+        grid=(images // each,),
         in_specs=[
-            pl.BlockSpec((1, height + 4, breadth + 16, 128), lambda b, c: (b, 0, 0, 0)),
-            pl.BlockSpec((1, rows, breadth, classes), lambda b, c: (b, c, 0, 0)),
+            part(height + 4, breadth + 16, 128),
+            part(height, breadth, classes),
             whole(8, 128),
-            pl.BlockSpec((1, 4, 128), lambda b, c: (b, 0, 0)),
+            part(4, 128),
             whole(24, 128),
             whole(3, 192, 768),
             whole(768),
@@ -260,9 +257,9 @@
             whole(2, 2),
         ],
         out_specs=[
-            pl.BlockSpec((1, rows, breadth, classes), lambda b, c: (b, c, 0, 0)),
-            pl.BlockSpec((1, rows, 4, breadth), lambda b, c: (b, c, 0, 0)),
-            pl.BlockSpec((1, height + 2, breadth + 16, 128), lambda b, c: (b, 0, 0, 0)),
+            part(height, breadth, classes),
+            part(height, 4, breadth),
+            part(height + 2, breadth + 16, 128),
             whole(tiles, 16, 128),
             whole(8, 128),
         ],
@@ -275,11 +272,10 @@
         ],
         scratch_shapes=[
             pltpu.VMEM((2 * PAD + (height + 2) * (breadth + 16), 128), F32),
-            pltpu.VMEM((height + 2, breadth, 256), BF16),
+            pltpu.VMEM((each, height + 2, breadth, 256), BF16),
             pltpu.VMEM((3, 256, 768), BF16),
             pltpu.VMEM((768, 768), BF16),
             pltpu.VMEM((2, 4, 256), BF16),
-            pltpu.VMEM((3, 4, 128), BF16),
             pltpu.VMEM((height + 2, breadth + 32, 256), F32),
             pltpu.VMEM((3, 256, 768), F32),
             pltpu.VMEM((80, 256), F32),
@@ -375,7 +371,11 @@
                     device_id_type=MESH,
                 )
 
-    pl.semaphore_wait(barrier, expected)
+    return expected
+
+
+def greeted(expected):
+    pl.semaphore_wait(pltpu.get_barrier_semaphore(), expected)
 
 
 def remote(source, target, send, recv, device):
@@ -718,9 +718,9 @@
             )
         )
     ]
+    expected = greet()
     for load in loads:
         load.start()
-    greet()
     low_around = Around(
         [low_ref.at[:, 0:3], low_ref.at[:, h - 3 : h]]
         + [low_send.at[k] for k in range(2)]
@@ -739,7 +739,6 @@
         + [skip_corner.at[1, k] for k in range(4)],
         strip_sems.at[1],
     )
-    low_around.start(range(2))
 
     def place_low(b, carry):
         start = PAD + b * low_r * pitch
@@ -753,8 +752,6 @@
     low_x[PAD + images * low_r * pitch :, :] = jnp.zeros((tail, 128), F32)
     loads[0].wait()
     lax.fori_loop(0, images, place_low, 0)
-    loads[1].wait()
-    stack_weight(w_one, conv_one_in)
 
     def pack(buffer, sends, corners, rows, step, line, across):
         for side, first in enumerate((8, 5 + across)):
@@ -798,7 +795,8 @@
         around.each(use)
 
     pack(low_x, low_send, low_corner, low_r, h, pitch, w)
-    low_around.start(range(2, 8))
+    greeted(expected)
+    low_around.start()
     skip_around.start(range(2))
 
     def place_skip(b, carry):
@@ -818,6 +816,8 @@
     lax.fori_loop(0, images, place_skip, 0)
     pack(skip_x, skip_send, skip_corner, skip_r, height, wide, breadth)
     skip_around.start(range(2, 8))
+    loads[1].wait()
+    stack_weight(w_one, conv_one_in)
     low_around.wait()
     unpack(low_around, low_x, low_rows, low_recv, low_corner, low_r, h, pitch, w)
 
@@ -983,6 +983,7 @@
         return carry
 
     lax.fori_loop(0, images, normed_taps, 0)
+    tiles_out[36:] = jnp.zeros((tiles_out.shape[0] - 36, 8, 128), F32)
     fold(tiles_out, 0, g_low)
     second_total.middle()
     totals = second_total.end()
@@ -1127,9 +1128,9 @@
         self.slots, self.sems = slots, sems
         self.levels = levels_of(source.shape[0])
 
-    def begin(self, level):
+    def copies(self, level):
         _, _, partners, left = self.levels[level]
-        self.copies = [
+        return [
             remote(
                 self.parts[level].at[pl.ds(other * left, left)],
                 self.slots[level].at[k],
@@ -1139,11 +1140,13 @@
             )
             for k, (other, device) in enumerate(partners)
         ]
-        start_all(self.copies)
+
+    def begin(self, level):
+        start_all(self.copies(level))
 
     def end(self, level):
         _, mine, partners, left = self.levels[level]
-        wait_all(self.copies)
+        wait_all(self.copies(level))
         total = self.parts[level][pl.ds(mine * left, left)].astype(F32)
         for k in range(len(partners)):
             total = total + self.slots[level][k].astype(F32)
@@ -1161,16 +1164,18 @@
             base = base + mine * left
         return pl.ds(base, self.levels[level][3])
 
-    def begin(self, level):
+    def copies(self, level):
         part = self.full.at[self.span(level)]
-        self.copies = [
+        return [
             remote(part, part, self.sems.at[level, 0, k], self.sems.at[level, 1, k], device)
             for k, (_, device) in enumerate(self.levels[level][2])
         ]
-        start_all(self.copies)
-
-    def end(self):
-        wait_all(self.copies)
+
+    def begin(self, level):
+        start_all(self.copies(level))
+
+    def end(self, level):
+        wait_all(self.copies(level))
 
 
 def scatter_scratch(tiles):
@@ -1196,48 +1201,61 @@
         self.mine = batch * cols + col
         self.row = row
 
-    def begin(self):
+    def first_copies(self):
         _, _, cols = extents()
-        self.copies = []
+        copies = []
         for k, (batch, row, col) in enumerate(plane_partners()):
             other = batch * cols + col
             part = self.source.at[pl.ds(other * self.share, self.share)]
-            self.copies.append(
+            copies.append(
                 remote(
-                    part, self.slots.at[k], self.sems.at[0, 0, k], self.sems.at[0, 1, k],
+                    part,
+                    self.slots.at[k],
+                    self.sems.at[0, 0, k],
+                    self.sems.at[0, 1, k],
                     (batch, row, col),
                 )
             )
-        start_all(self.copies)
+        return copies
+
+    def middle_copies(self):
+        return [
+            remote(
+                self.mid,
+                self.row_slots.at[self.row],
+                self.sems.at[1, 0, k],
+                self.sems.at[1, 1, k],
+                partner,
+            )
+            for k, partner in enumerate(row_partners())
+        ]
+
+    def last_copies(self):
+        part = self.full.at[pl.ds(self.mine * self.share, self.share)]
+        return [
+            remote(part, part, self.sems.at[2, 0, k], self.sems.at[2, 1, k], partner)
+            for k, partner in enumerate(plane_partners())
+        ]
+
+    def begin(self):
+        start_all(self.first_copies())
 
     def middle(self):
-        wait_all(self.copies)
+        wait_all(self.first_copies())
         total = self.source[pl.ds(self.mine * self.share, self.share)]
         for k in range(self.slots.shape[0]):
             total = total + self.slots[k]
         self.mid[...] = total
-        self.copies = [
-            remote(
-                self.mid, self.row_slots.at[self.row], self.sems.at[1, 0, k],
-                self.sems.at[1, 1, k], partner,
-            )
-            for k, partner in enumerate(row_partners())
-        ]
-        start_all(self.copies)
+        start_all(self.middle_copies())
         self.row_slots[self.row] = total
 
     def last(self):
-        wait_all(self.copies)
+        wait_all(self.middle_copies())
         self.full[pl.ds(self.mine * self.share, self.share)] = slot_sum(self.row_slots)
-        part = self.full.at[pl.ds(self.mine * self.share, self.share)]
-        self.copies = [
-            remote(part, part, self.sems.at[2, 0, k], self.sems.at[2, 1, k], partner)
-            for k, partner in enumerate(plane_partners())
-        ]
-        start_all(self.copies)
+        start_all(self.last_copies())
 
     def end(self):
-        wait_all(self.copies)
+        wait_all(self.last_copies())
 
 
 def plane_scratch(tiles):
@@ -1267,8 +1285,6 @@
     target[first + 24 : first + 36] = jnp.where(low, last[0:96], swapped(last[96:192])).reshape(
         12, 8, 128
     )
-    if target.shape[0] > first + 36:
-        target[first + 36 :] = jnp.zeros((target.shape[0] - first - 36, 8, 128), F32)
 
 
 def unfold(source, first):
@@ -1335,7 +1351,6 @@
     conv_out,
     conv_x_out,
     sums_out,
-    last_out,
     weight_out,
     y_two_s,
     slope_s,
@@ -1355,7 +1370,6 @@
     w_two,
     g_two,
     g_one,
-    total_s,
     strip_send,
     strip_recv,
     side_send,
@@ -1367,7 +1381,6 @@
     edge_recv,
     zed_corners,
     third_scratch,
-    fourth_scratch,
     load_scratch,
     conv_x_scratch,
     conv_scratch,
@@ -1418,6 +1431,7 @@
             )
         )
     ]
+    expected = greet()
     for b in range(images):
         spread_load(b).start()
     for b in range(images):
@@ -1431,9 +1445,9 @@
         for line in (0, ext + 1):
             start = PAD + (b * rows + line) * wide
             grad_x[start : start + wide, :] = jnp.zeros((wide, 128), F32)
-    greet()
     for b in range(images):
         spread_load(b).wait()
+
     for pair in range(half):
         for side, first in enumerate((1, ext - 2)):
             parts = []
@@ -1450,7 +1464,6 @@
         + [corners.at[1, k] for k in range(4)],
         strip_sems,
     )
-    around.start(range(2))
     for side, first in enumerate((7, 6 + breadth)):
         pack_columns(grad_x, side_send.at[side], images, rows, wide, 1, first, 3)
     for k, (up, along) in enumerate(AROUND[4:]):
@@ -1464,7 +1477,8 @@
             7 if along < 0 else 6 + breadth,
             3,
         )
-    around.start(range(2, 8))
+    greeted(expected)
+    around.start()
     loads[0].wait()
     load_sum = Scatter(load_s, (*load_scratch[0], share_s), load_scratch[1], load_scratch[2])
     load_sum.begin(0)
@@ -1538,8 +1552,6 @@
     totals = third_total.end()
     sums_out[...] = totals
     conv_x_sum.begin()
-    load_sum.end(1)
-    load_sum.begin(2)
     factor_two = gain_two * scale_two
     shift_part, gain_part = totals[8:9] / cells_high, totals[9:10] / cells_high
     for k in (4, 5, 6):
@@ -1598,23 +1610,40 @@
         )
         return sums[0] + fold_sum(grad_z), sums[1] + fold_sum(grad_z * normed)
 
-    sums = lax.fori_loop(0, half, merge, (nothing, nothing))
     gather = Gather(load_out, gather_sems)
-    load_sum.end(2)
-    load_out[gather.span(2)] = share_s[...]
-    gather.begin(2)
-    conv_x_sum.middle()
-    sums = lax.fori_loop(half, images, merge, sums)
-    last_src = fourth_scratch[0]
-    last_src[...] = jnp.zeros((8, 128), F32)
-    last_src[0:1, :] = jnp.sum(sums[0], axis=0, keepdims=True)
-    last_src[1:2, :] = jnp.sum(sums[1], axis=0, keepdims=True)
-    fourth_total = Total(*fourth_scratch)
-    fourth_total.begin()
-    gather.end()
-    gather.begin(1)
+
+    def merge_and_move(b, sums):
+        sums = merge(b, sums)
+
+        @pl.when(b == 0)
+        def _():
+            load_sum.end(1)
+            load_sum.begin(2)
+
+        @pl.when(b == 1)
+        def _():
+            conv_x_sum.middle()
+            load_sum.end(2)
+            load_out[gather.span(2)] = share_s[...]
+            gather.begin(2)
+
+        @pl.when(b == 2)
+        def _():
+            gather.end(2)
+            gather.begin(1)
+
+        @pl.when(b == 3)
+        def _():
+            conv_x_sum.last()
+
+        return sums
+
+    sums = lax.fori_loop(0, images, merge_and_move, (nothing, nothing))
+    fold(conv_scratch[0], 36, g_one)
+    conv_scratch[0][72:] = jnp.zeros((conv_out.shape[0] - 72, 8, 128), F32)
+    for k in range(2):
+        conv_scratch[0][72, k : k + 1, :] = jnp.sum(sums[k], axis=0, keepdims=True)
     fold(conv_scratch[0], 0, g_two)
-    fold(conv_scratch[0], 36, g_one)
     conv_sum = PlaneReducer(*conv_scratch[:4], conv_out, conv_scratch[4])
     conv_sum.begin()
     for pair in range(half):
@@ -1647,9 +1676,9 @@
         zed_sems,
     )
     zed_around.start()
-    fourth_total.middle()
-    conv_x_sum.last()
     conv_sum.middle()
+    gather.end(1)
+    gather.begin(0)
     zed_around.wait()
 
     def use_zed(k):
@@ -1682,13 +1711,10 @@
 
     for b in range(images):
         zed_store(b).start()
-    last_out[...] = fourth_total.end()
     conv_sum.last()
-    gather.end()
-    gather.begin(0)
     conv_x_sum.end()
     conv_sum.end()
-    gather.end()
+    gather.end(0)
     for b in range(images):
         zed_store(b).wait()
         pltpu.make_async_copy(skip_s.at[b], skip_out.at[b], out_sems.at[0, b]).wait()
@@ -1702,14 +1728,14 @@
     h, w = height // 2, breadth // 2
     pitch, ext, zed_rows = w + 16, height + 2, h + 2
     half = images // 2
-    tiles, parts_x, parts = load.shape[0], tiles_x.shape[0], conv_tiles(72)
+    tiles, parts_x, parts = load.shape[0], tiles_x.shape[0], conv_tiles(73)
     vmem = pl.BlockSpec(memory_space=pltpu.VMEM)
     hbm = pl.BlockSpec(memory_space=pl.ANY)
     lines, low_lines = rounded_up(ext, 16), rounded_up(h, 8)
     return pl.pallas_call(
         fall_body,
         in_specs=[hbm] * 2 + [vmem, hbm, vmem] + [hbm] * 6,
-        out_specs=[hbm] * 2 + [vmem] * 6,
+        out_specs=[hbm] * 2 + [vmem] * 5,
         out_shape=[
             jax.ShapeDtypeStruct((images, height, breadth, 64), F32),
             jax.ShapeDtypeStruct((images, zed_rows * pitch, 128), F32),
@@ -1717,7 +1743,6 @@
             jax.ShapeDtypeStruct((parts, 8, 128), F32),
             jax.ShapeDtypeStruct((parts_x, 8, 128), F32),
             jax.ShapeDtypeStruct((16, 128), F32),
-            jax.ShapeDtypeStruct((8, 128), F32),
             jax.ShapeDtypeStruct((768, 128), BF16),
         ],
         scratch_shapes=[
@@ -1739,7 +1764,6 @@
             pltpu.VMEM((768, 128), BF16),
             pltpu.VMEM((256, 256), F32),
             pltpu.VMEM((256, 256), F32),
-            pltpu.VMEM((2, 8, 128), F32),
             pltpu.VMEM((2, half, 3 * wide, 128), BF16),
             pltpu.VMEM((2, half, 3 * wide, 128), BF16),
             pltpu.VMEM((2, 3 * half, lines, 128), BF16),
@@ -1751,7 +1775,6 @@
             pltpu.VMEM((2, half, low_lines, 128), F32),
             pltpu.VMEM((2, 4, half, 8, 128), F32),
             total_scratch(16),
-            total_scratch(8),
             scatter_scratch(tiles),
             plane_scratch(parts_x),
             plane_scratch(parts),
@@ -1776,7 +1799,6 @@
     conv_ref,
     conv_x_ref,
     sums_ref,
-    last_ref,
     stat_ref,
     zed_ref,
     y_one_ref,
@@ -1803,7 +1825,7 @@
     pitch = w + 16
     rows = h + 2
     factor = stat_ref[6:7, :] * stat_ref[1:2, :]
-    shift_low, gain_low = last_ref[0:1, :] / cells_low, last_ref[1:2, :] / cells_low
+    shift_low, gain_low = conv_ref[72, 0:1, :] / cells_low, conv_ref[72, 1:2, :] / cells_low
     skip_out[...] = skip_ref[...]
     for column in range(head_out.shape[3] // 128):
         block = load_ref[36 * column : 36 * column + 36].astype(F32)
@@ -1836,8 +1858,8 @@
         heat_b_out[...] = sums_ref[6:7, 0:80]
         shift_two_out[...] = sums_ref[8:9, 0:64]
         gain_two_out[...] = sums_ref[9:10, 0:64]
-        shift_one_out[...] = last_ref[0:1, 0:64]
-        gain_one_out[...] = last_ref[1:2, 0:64]
+        shift_one_out[...] = conv_ref[72, 0:1, 0:64]
+        gain_one_out[...] = conv_ref[72, 1:2, 0:64]
 
     for b in range(each):
         normed = (y_one_ref[b, 1 : h + 3] - stat_ref[0:1, :]) * stat_ref[1:2, :]
@@ -1860,7 +1882,7 @@
         low_out[b] = grad[:, 8 : 8 + w, 0:64]
 
 
-def finish(load, conv, conv_x, sums, last, stats, zed, y_one, weight, skip):
+def finish(load, conv, conv_x, sums, stats, zed, y_one, weight, skip):
     images, y_rows, pitch, _ = y_one.shape
     h, w = y_rows - 4, pitch - 16
     batches, row_count, col_count = extents()
@@ -1897,7 +1919,7 @@
             part((216 // steps, 16, 128)),
             pl.BlockSpec((36, 16, 128), lambda c: (6, 0, 0)),
         ]
-        + [whole(array.shape) for array in (conv, conv_x, sums, last, stats)]
+        + [whole(array.shape) for array in (conv, conv_x, sums, stats)]
         + [
             part((each, span, 128)),
             part((each, y_rows, pitch, 128)),
@@ -1911,7 +1933,7 @@
         ],
         compiler_params=pltpu.CompilerParams(vmem_limit_bytes=60 * MIB),
         name="finish",
-    )(load, load, conv, conv_x, sums, last, stats, zed, y_one, weight, skip)
+    )(load, load, conv, conv_x, sums, stats, zed, y_one, weight, skip)
 
 
 def local(
@@ -1966,7 +1988,7 @@
         devices,
     )
     images, ext, wide, _ = spread.shape
-    grad_skip, zed, load, conv, conv_x, sums, last, weight = fall(
+    grad_skip, zed, load, conv, conv_x, sums, weight = fall(
         spread.reshape(images, ext * wide, 128),
         y_two,
         stats,
@@ -1979,7 +2001,7 @@
         conv_two,
         conv_one,
     )
-    grads = finish(load, conv, conv_x, sums, last, stats, zed, y_one, weight, grad_skip)
+    grads = finish(load, conv, conv_x, sums, stats, zed, y_one, weight, grad_skip)
     return (
         heat_map,
         box_map.transpose(0, 1, 3, 2),

time: 117 us -> 119 us (1.017)
  Pallas kernels: 116 us -> 118 us
    pallas_call x1, Pallas kernels: 46 us -> 48.6 us  [fall(): pl.pallas_call(fall_body, in_specs=[hbm] * 2 + [vmem, hbm, vmem] + [hbm]...]
where the time goes in v2:
time: 119 us
  Pallas kernels  118 us (99%)
    pallas_call x1, Pallas kernels, fall(): pl.pallas_call(fall_body, in_specs=[hbm] * 2 + [vmem, hbm, vmem] + [hbm]...  48.6 us
    pallas_call x1, Pallas kernels, rise(): pl.pallas_call(rise_body, in_specs=[hbm] * 10 + [pl.BlockSpec(memory_spac...  34.7 us
    pallas_call x1, Pallas kernels, heads(): pl.pallas_call(functools.partial(heads_body, breadth * lax.axis_size('col...  29.8 us
    pallas_call x1, Pallas kernels, finish(): pl.pallas_call(functools.partial(finish_body, cells), grid=(steps,), in_s...  5.21 us

profile of v2, /device:TPU:0, one launch (start us, length us, event | category | flops | bytes accessed | tf_op | source)
XLA Modules:
  0.0 119.1 jit_solution(16671412201234435407)
XLA Ops:
  0.6 34.7 %rise.1 = (f32[4,36,48,128]{3,2,1,0:T(8,128)}, f32[4,20,32,128]{3,2,1,0:T(8,128)}, bf16[4,34,32,256]{3,2,1,0:T(8,128)(2,1)}, bf16[4,18,16,256]{3,2,1,0:T(8,128)(...) custom-call(bf16[4,16,16,64]{3,2,1,0:T(8,128)(2,1)} %low_ref.1, ...), custom_call_target="tpu_custom_call" | custom-call | tf_op jit(solution)/shard_map/rise/pallas_call | solution.py:1029
  35.4 29.8 %heads.1 = (f32[4,32,32,80]{3,2,1,0:T(8,128)}, f32[4,32,4,32]{3,2,1,0:T(4,128)}, f32[4,34,48,128]{3,2,1,0:T(8,128)}, bf16[256,16,128]{2,1,0:T(8,128)(2,1)}, f32[8,128]{1,0:T(8,128)}) custom-call(f32[4,36,48,128]{3,2,1,0:T(8,128)} %get-tuple-element.49.y_two_ref, bf16[4,32,32,80]{3,2,1,0:T(8,128)(2,1)} %target_ref.3, s32[8,128]{1,0:T(8,128)} %get-tuple-element.50.spot_ref, ...), custom_call_target="tpu_custom_call" | custom-call | flops 10871635968 | bytes 12582912 | tf_op jit(solution)/shard_map/heads/pallas_call | solution.py:243
  65.1 48.6 %fall.1 = (f32[4,32,32,64]{3,2,1,0:T(8,128)}, f32[4,576,128]{2,1,0:T(8,128)}, bf16[256,16,128]{2,1,0:T(8,128)(2,1)}, f32[80,8,128]{2,1,0:T(8,128)}, f32[40,8,128...) custom-call(f32[4,1632,128]{2,1,0:T(8,128)} %bitcast.20, f32[4,36,48,128]{3,2,1,0:T(8,128)} %get-tuple-element.49.y_two_ref, ...), custom_call_target="tpu_custom_call" | custom-call | tf_op jit(solution)/shard_map/fall/pallas_call | solution.py:1735
  113.7 5.2 %finish.1 = (f32[3,3,64,64]{3,2,1,0:T(8,128)}, f32[1,64]{1,0:T(1,128)}, f32[1,64]{1,0:T(1,128)}, f32[3,3,64,64]{3,2,1,0:T(8,128)}, f32[1,64]{1,0:T(1,128)}, /*in...) custom-call(bf16[256,16,128]{2,1,0:T(8,128)(2,1)} %get-tuple-element, ...), custom_call_target="tpu_custom_call" | custom-call | tf_op jit(solution)/shard_map/finish/pallas_call | solution.py:1915

commit v3 on v2

--- a/solution.py
+++ b/solution.py
@@ -122,7 +122,8 @@
         [taps_ref[:, tap : tap + height].reshape(cells, 256) for tap in range(3)], axis=1
     )
     active, slope = [], []
-    for block in range(3):
+
+    def forward(block):
         weight = kernel_s[:, :, block * units : (block + 1) * units].reshape(768, units)
         hidden = dot(taps, weight)
         turn = jnp.tanh(hidden)
@@ -131,6 +132,7 @@
         active.append(product.astype(BF16))
         slope.append(above + product * (1.0 - turn))
 
+    forward(0)
     logit = dot_keep(active[0], heat_w_ref[...]) + heat_b_ref[...]
     decay = jnp.exp(-jnp.abs(logit))
     large = 1.0 / (1.0 + decay)
@@ -149,6 +151,11 @@
     weighting = jnp.where(positive, -1.0, gap * gap) * stat_ref[4:5, 0:80]
     logit_grad = weighting * slant
     logit_low = logit_grad.astype(BF16)
+    heat_sum_s[...] += jnp.sum(logit_low.astype(F32).reshape(cells // 8, 8, 80), axis=0)
+    heat_grad_s[...] += dot_left(logit_low, active[0])
+    hidden_low = [(dot(logit_low, heat_w_ref[...]) * slope[0]).astype(BF16)]
+    forward(1)
+    forward(2)
 
     box_bias = jnp.concatenate([box_b_ref[0:1, :], box_b_ref[1:2, :]], axis=1)
     boxes = dot_keep(active[1], box_s[0]) + dot_keep(active[2], box_s[1]) + box_bias
@@ -161,11 +168,13 @@
     for image in range(each):
         spots = spot_ref[pl.ds(step * each + image, 1), :]
         chosen = (cell == spots).astype(F32).astype(BF16)
-        goal = jnp.zeros((image_cells, 4), F32)
-        for part in three_parts(goal_ref[image]):
-            goal = goal + dot_keep(chosen, part)
-        goals.append(goal)
-        hits.append(dot(chosen, jnp.ones((128, 4), BF16)))
+        high, mid, least = three_parts(goal_ref[image])
+        ends = jnp.concatenate([least.astype(F32), jnp.ones((4, 128), F32)], axis=0).astype(BF16)
+        twofold = jnp.concatenate([chosen, chosen], axis=1)
+        goal = dot_keep(twofold, jnp.concatenate([high, mid], axis=1))
+        both = dot_keep(chosen, ends)
+        goals.append(goal + both[:, 0:4])
+        hits.append(both[:, 4:8])
     goals, hit = jnp.concatenate(goals, axis=0), jnp.concatenate(hits, axis=0)
     miss = boxes - goals
     lane = lax.broadcasted_iota(jnp.int32, (1, 4), 1)
@@ -173,20 +182,14 @@
     box_grad = hit * factor * miss * lax.rsqrt(miss * miss + 1.0)
     box_low = box_grad.astype(BF16)
 
-    heat_sum_s[...] += jnp.sum(logit_low.astype(F32).reshape(cells // 8, 8, 80), axis=0)
     box_sum_s[...] += jnp.sum(box_low.astype(F32).reshape(cells // 8, 8, 4), axis=0)
-    heat_grad_s[...] += dot_left(logit_low, active[0])
     for part in range(2):
         box_grad_s[part] += dot_left(box_low, active[1 + part])
 
-    back = [
-        dot(logit_low, heat_w_ref[...]),
-        dot(box_low, box_s[0]),
-        dot(box_low, box_s[1]),
-    ]
-    grad_hidden = jnp.concatenate(
-        [(back[block] * slope[block]).astype(BF16) for block in range(3)], axis=1
-    )
+    for part in range(2):
+        back = dot(box_low, box_s[part])
+        hidden_low.append((back * slope[1 + part]).astype(BF16))
+    grad_hidden = jnp.concatenate(hidden_low, axis=1)
     spread = []
     for tap in range(3):
         part = dot(grad_hidden, back_s[:, 256 * tap : 256 * tap + 256])
@@ -1128,9 +1131,9 @@
         self.slots, self.sems = slots, sems
         self.levels = levels_of(source.shape[0])
 
-    def copies(self, level):
+    def begin(self, level):
         _, _, partners, left = self.levels[level]
-        return [
+        self.copies = [
             remote(
                 self.parts[level].at[pl.ds(other * left, left)],
                 self.slots[level].at[k],
@@ -1140,13 +1143,11 @@
             )
             for k, (other, device) in enumerate(partners)
         ]
-
-    def begin(self, level):
-        start_all(self.copies(level))
+        start_all(self.copies)
 
     def end(self, level):
         _, mine, partners, left = self.levels[level]
-        wait_all(self.copies(level))
+        wait_all(self.copies)
         total = self.parts[level][pl.ds(mine * left, left)].astype(F32)
         for k in range(len(partners)):
             total = total + self.slots[level][k].astype(F32)
@@ -1164,18 +1165,16 @@
             base = base + mine * left
         return pl.ds(base, self.levels[level][3])
 
-    def copies(self, level):
+    def begin(self, level):
         part = self.full.at[self.span(level)]
-        return [
+        self.copies = [
             remote(part, part, self.sems.at[level, 0, k], self.sems.at[level, 1, k], device)
             for k, (_, device) in enumerate(self.levels[level][2])
         ]
-
-    def begin(self, level):
-        start_all(self.copies(level))
-
-    def end(self, level):
-        wait_all(self.copies(level))
+        start_all(self.copies)
+
+    def end(self):
+        wait_all(self.copies)
 
 
 def scatter_scratch(tiles):
@@ -1201,61 +1200,48 @@
         self.mine = batch * cols + col
         self.row = row
 
-    def first_copies(self):
+    def begin(self):
         _, _, cols = extents()
-        copies = []
+        self.copies = []
         for k, (batch, row, col) in enumerate(plane_partners()):
             other = batch * cols + col
             part = self.source.at[pl.ds(other * self.share, self.share)]
-            copies.append(
+            self.copies.append(
                 remote(
-                    part,
-                    self.slots.at[k],
-                    self.sems.at[0, 0, k],
-                    self.sems.at[0, 1, k],
+                    part, self.slots.at[k], self.sems.at[0, 0, k], self.sems.at[0, 1, k],
                     (batch, row, col),
                 )
             )
-        return copies
-
-    def middle_copies(self):
-        return [
-            remote(
-                self.mid,
-                self.row_slots.at[self.row],
-                self.sems.at[1, 0, k],
-                self.sems.at[1, 1, k],
-                partner,
-            )
-            for k, partner in enumerate(row_partners())
-        ]
-
-    def last_copies(self):
-        part = self.full.at[pl.ds(self.mine * self.share, self.share)]
-        return [
-            remote(part, part, self.sems.at[2, 0, k], self.sems.at[2, 1, k], partner)
-            for k, partner in enumerate(plane_partners())
-        ]
-
-    def begin(self):
-        start_all(self.first_copies())
+        start_all(self.copies)
 
     def middle(self):
-        wait_all(self.first_copies())
+        wait_all(self.copies)
         total = self.source[pl.ds(self.mine * self.share, self.share)]
         for k in range(self.slots.shape[0]):
             total = total + self.slots[k]
         self.mid[...] = total
-        start_all(self.middle_copies())
+        self.copies = [
+            remote(
+                self.mid, self.row_slots.at[self.row], self.sems.at[1, 0, k],
+                self.sems.at[1, 1, k], partner,
+            )
+            for k, partner in enumerate(row_partners())
+        ]
+        start_all(self.copies)
         self.row_slots[self.row] = total
 
     def last(self):
-        wait_all(self.middle_copies())
+        wait_all(self.copies)
         self.full[pl.ds(self.mine * self.share, self.share)] = slot_sum(self.row_slots)
-        start_all(self.last_copies())
+        part = self.full.at[pl.ds(self.mine * self.share, self.share)]
+        self.copies = [
+            remote(part, part, self.sems.at[2, 0, k], self.sems.at[2, 1, k], partner)
+            for k, partner in enumerate(plane_partners())
+        ]
+        start_all(self.copies)
 
     def end(self):
-        wait_all(self.last_copies())
+        wait_all(self.copies)
 
 
 def plane_scratch(tiles):
@@ -1431,7 +1417,6 @@
             )
         )
     ]
-    expected = greet()
     for b in range(images):
         spread_load(b).start()
     for b in range(images):
@@ -1445,9 +1430,9 @@
         for line in (0, ext + 1):
             start = PAD + (b * rows + line) * wide
             grad_x[start : start + wide, :] = jnp.zeros((wide, 128), F32)
+    greeted(greet())
     for b in range(images):
         spread_load(b).wait()
-
     for pair in range(half):
         for side, first in enumerate((1, ext - 2)):
             parts = []
@@ -1464,6 +1449,7 @@
         + [corners.at[1, k] for k in range(4)],
         strip_sems,
     )
+    around.start(range(2))
     for side, first in enumerate((7, 6 + breadth)):
         pack_columns(grad_x, side_send.at[side], images, rows, wide, 1, first, 3)
     for k, (up, along) in enumerate(AROUND[4:]):
@@ -1477,8 +1463,7 @@
             7 if along < 0 else 6 + breadth,
             3,
         )
-    greeted(expected)
-    around.start()
+    around.start(range(2, 8))
     loads[0].wait()
     load_sum = Scatter(load_s, (*load_scratch[0], share_s), load_scratch[1], load_scratch[2])
     load_sum.begin(0)
@@ -1552,6 +1537,8 @@
     totals = third_total.end()
     sums_out[...] = totals
     conv_x_sum.begin()
+    load_sum.end(1)
+    load_sum.begin(2)
     factor_two = gain_two * scale_two
     shift_part, gain_part = totals[8:9] / cells_high, totals[9:10] / cells_high
     for k in (4, 5, 6):
@@ -1610,40 +1597,20 @@
         )
         return sums[0] + fold_sum(grad_z), sums[1] + fold_sum(grad_z * normed)
 
+    sums = lax.fori_loop(0, half, merge, (nothing, nothing))
     gather = Gather(load_out, gather_sems)
-
-    def merge_and_move(b, sums):
-        sums = merge(b, sums)
-
-        @pl.when(b == 0)
-        def _():
-            load_sum.end(1)
-            load_sum.begin(2)
-
-        @pl.when(b == 1)
-        def _():
-            conv_x_sum.middle()
-            load_sum.end(2)
-            load_out[gather.span(2)] = share_s[...]
-            gather.begin(2)
-
-        @pl.when(b == 2)
-        def _():
-            gather.end(2)
-            gather.begin(1)
-
-        @pl.when(b == 3)
-        def _():
-            conv_x_sum.last()
-
-        return sums
-
-    sums = lax.fori_loop(0, images, merge_and_move, (nothing, nothing))
+    load_sum.end(2)
+    load_out[gather.span(2)] = share_s[...]
+    gather.begin(2)
+    conv_x_sum.middle()
+    sums = lax.fori_loop(half, images, merge, sums)
+    gather.end()
+    gather.begin(1)
+    fold(conv_scratch[0], 0, g_two)
     fold(conv_scratch[0], 36, g_one)
     conv_scratch[0][72:] = jnp.zeros((conv_out.shape[0] - 72, 8, 128), F32)
     for k in range(2):
         conv_scratch[0][72, k : k + 1, :] = jnp.sum(sums[k], axis=0, keepdims=True)
-    fold(conv_scratch[0], 0, g_two)
     conv_sum = PlaneReducer(*conv_scratch[:4], conv_out, conv_scratch[4])
     conv_sum.begin()
     for pair in range(half):
@@ -1676,9 +1643,8 @@
         zed_sems,
     )
     zed_around.start()
+    conv_x_sum.last()
     conv_sum.middle()
-    gather.end(1)
-    gather.begin(0)
     zed_around.wait()
 
     def use_zed(k):
@@ -1712,9 +1678,11 @@
     for b in range(images):
         zed_store(b).start()
     conv_sum.last()
+    gather.end()
+    gather.begin(0)
     conv_x_sum.end()
     conv_sum.end()
-    gather.end(0)
+    gather.end()
     for b in range(images):
         zed_store(b).wait()
         pltpu.make_async_copy(skip_s.at[b], skip_out.at[b], out_sems.at[0, b]).wait()

time: 119 us -> 120 us (level)
    pallas_call x1, Pallas kernels: 29.8 us -> 32.7 us  [heads(): pl.pallas_call(functools.partial(heads_body, breadth * lax.axis_size('col...]
    pallas_call x1, Pallas kernels: 48.6 us -> 46 us  [fall(): pl.pallas_call(fall_body, in_specs=[hbm] * 2 + [vmem, hbm, vmem] + [hbm]...]
where the time goes in v3:
time: 120 us; the launch traced here: 119 us
  Pallas kernels  119 us (99%)
    pallas_call x1, Pallas kernels, fall(): pl.pallas_call(fall_body, in_specs=[hbm] * 2 + [vmem, hbm, vmem] + [hbm]...  46 us
    pallas_call x1, Pallas kernels, rise(): pl.pallas_call(rise_body, in_specs=[hbm] * 10 + [pl.BlockSpec(memory_spac...  34.7 us
    pallas_call x1, Pallas kernels, heads(): pl.pallas_call(functools.partial(heads_body, breadth * lax.axis_size('col...  32.7 us
    pallas_call x1, Pallas kernels, finish(): pl.pallas_call(functools.partial(finish_body, cells), grid=(steps,), in_s...  5.21 us

profile of v3, /device:TPU:0, one launch (start us, length us, event | category | flops | bytes accessed | tf_op | source)
XLA Modules:
  0.0 119.4 jit_solution(7848862416456366582)
XLA Ops:
  0.6 34.7 %rise.1 = (f32[4,36,48,128]{3,2,1,0:T(8,128)}, f32[4,20,32,128]{3,2,1,0:T(8,128)}, bf16[4,34,32,256]{3,2,1,0:T(8,128)(2,1)}, bf16[4,18,16,256]{3,2,1,0:T(8,128)(...) custom-call(bf16[4,16,16,64]{3,2,1,0:T(8,128)(2,1)} %low_ref.1, ...), custom_call_target="tpu_custom_call" | custom-call | tf_op jit(solution)/shard_map/rise/pallas_call | solution.py:1032
  35.4 32.7 %heads.1 = (f32[4,32,32,80]{3,2,1,0:T(8,128)}, f32[4,32,4,32]{3,2,1,0:T(4,128)}, f32[4,34,48,128]{3,2,1,0:T(8,128)}, bf16[256,16,128]{2,1,0:T(8,128)(2,1)}, f32[8,128]{1,0:T(8,128)}) custom-call(f32[4,36,48,128]{3,2,1,0:T(8,128)} %get-tuple-element.49.y_two_ref, bf16[4,32,32,80]{3,2,1,0:T(8,128)(2,1)} %target_ref.3, s32[8,128]{1,0:T(8,128)} %get-tuple-element.50.spot_ref, ...), custom_call_target="tpu_custom_call" | custom-call | flops 10871635968 | bytes 12582912 | tf_op jit(solution)/shard_map/heads/pallas_call | solution.py:246
  68.1 46.0 %fall.1 = (f32[4,32,32,64]{3,2,1,0:T(8,128)}, f32[4,576,128]{2,1,0:T(8,128)}, bf16[256,16,128]{2,1,0:T(8,128)(2,1)}, f32[80,8,128]{2,1,0:T(8,128)}, f32[40,8,128...) custom-call(f32[4,1632,128]{2,1,0:T(8,128)} %bitcast.20, f32[4,36,48,128]{3,2,1,0:T(8,128)} %get-tuple-element.49.y_two_ref, ...), custom_call_target="tpu_custom_call" | custom-call | tf_op jit(solution)/shard_map/fall/pallas_call | solution.py:1703
  114.1 5.2 %finish.1 = (f32[3,3,64,64]{3,2,1,0:T(8,128)}, f32[1,64]{1,0:T(1,128)}, f32[1,64]{1,0:T(1,128)}, f32[3,3,64,64]{3,2,1,0:T(8,128)}, f32[1,64]{1,0:T(1,128)}, /*in...) custom-call(bf16[256,16,128]{2,1,0:T(8,128)(2,1)} %get-tuple-element, ...), custom_call_target="tpu_custom_call" | custom-call | tf_op jit(solution)/shard_map/finish/pallas_call | solution.py:1883

commit v4 on v1

--- a/solution.py
+++ b/solution.py
@@ -46,8 +46,8 @@
     spot_ref,
     goal_ref,
     stat_ref,
-    conv_ref,
-    bias_ref,
+    kernel_s,
+    back_s,
     heat_w_ref,
     heat_b_ref,
     box_w_ref,
@@ -59,8 +59,6 @@
     small_out,
     feat_s,
     taps_ref,
-    kernel_s,
-    back_s,
     box_s,
     goal_s,
     wide_s,
@@ -78,21 +76,6 @@
 
     @pl.when(jnp.logical_and(image == 0, chunk == 0))
     def _():
-        for tap in range(3):
-            kernel_s[tap, 0:192, :] = (0.5 * conv_ref[tap].astype(F32)).astype(BF16)
-            kernel_s[tap, 192:256, :] = jnp.zeros((64, 768), BF16)
-        parts = three_parts(0.5 * bias_ref[...].reshape(1, 768))
-        which = lax.broadcasted_iota(jnp.int32, (16, 768), 0)
-        filled = jnp.zeros((16, 768), F32)
-        for place in range(3):
-            filled = jnp.where(which == place, parts[place].astype(F32), filled)
-        kernel_s[1, 192:208, :] = filled.astype(BF16)
-        for tap in range(3):
-            for block in range(3):
-                span = slice(256 * block, 256 * block + 256)
-                back_s[span, 256 * tap : 256 * tap + 256] = (
-                    kernel_s[tap, :, span].astype(F32).T.astype(BF16)
-                )
         empty = jnp.zeros((2, 256), F32)
         for part in range(2):
             pieces = [empty, empty]
@@ -235,7 +218,7 @@
 
 
 def heads(
-    taps, target, spot, goal, stats, conv, bias, heat_w, heat_b, box_w, box_b, devices
+    taps, target, spot, goal, stats, kernel, back, heat_w, heat_b, box_w, box_b, devices
 ):
     images, height, breadth, classes = target.shape
     rows = height
@@ -252,8 +235,8 @@
             whole(8, 128),
             pl.BlockSpec((1, 4, 128), lambda b, c: (b, 0, 0)),
             whole(24, 128),
-            whole(3, 192, 768),
-            whole(768),
+            whole(3, 256, 768),
+            whole(768, 768),
             whole(80, 256),
             whole(1, 80),
             whole(2, 2, 256),
@@ -276,8 +259,6 @@
         scratch_shapes=[
             pltpu.VMEM((2 * PAD + (height + 2) * (breadth + 16), 128), F32),
             pltpu.VMEM((height + 2, breadth, 256), BF16),
-            pltpu.VMEM((3, 256, 768), BF16),
-            pltpu.VMEM((768, 768), BF16),
             pltpu.VMEM((2, 4, 256), BF16),
             pltpu.VMEM((3, 4, 128), BF16),
             pltpu.VMEM((height + 2, breadth + 32, 256), F32),
@@ -292,7 +273,7 @@
             flops=cells * 576 * 768 * 6, bytes_accessed=12 * MIB, transcendentals=cells * 768
         ),
         name="heads",
-    )(taps, target, spot, goal, stats, conv, bias, heat_w, heat_b, box_w, box_b)
+    )(taps, target, spot, goal, stats, kernel, back, heat_w, heat_b, box_w, box_b)
 
 
 MESH = pl.DeviceIdType.MESH
@@ -375,7 +356,11 @@
                     device_id_type=MESH,
                 )
 
-    pl.semaphore_wait(barrier, expected)
+    return expected
+
+
+def greeted(expected):
+    pl.semaphore_wait(pltpu.get_barrier_semaphore(), expected)
 
 
 def remote(source, target, send, recv, device):
@@ -649,11 +634,15 @@
     gain_two_ref,
     shift_two_ref,
     index_ref,
+    head_ref,
+    bias_ref,
     count_ref,
     y_two_out,
     y_one_out,
     merged_out,
     low_out,
+    kernel_out,
+    back_out,
     stat_out,
     spot_out,
     tiles_out,
@@ -664,10 +653,14 @@
     conv_two_in,
     param_in,
     index_in,
+    head_in,
+    bias_in,
     y_two_s,
     y_one_s,
     merged_s,
     low_s,
+    kernel_s,
+    back_s,
     low_x,
     skip_x,
     act_s,
@@ -715,12 +708,14 @@
                 (gain_two_ref, param_in.at[2]),
                 (shift_two_ref, param_in.at[3]),
                 (conv_two_ref, conv_two_in),
+                (head_ref, head_in),
+                (bias_ref, bias_in),
             )
         )
     ]
+    expected = greet()
     for load in loads:
         load.start()
-    greet()
     low_around = Around(
         [low_ref.at[:, 0:3], low_ref.at[:, h - 3 : h]]
         + [low_send.at[k] for k in range(2)]
@@ -739,7 +734,6 @@
         + [skip_corner.at[1, k] for k in range(4)],
         strip_sems.at[1],
     )
-    low_around.start(range(2))
 
     def place_low(b, carry):
         start = PAD + b * low_r * pitch
@@ -753,8 +747,6 @@
     low_x[PAD + images * low_r * pitch :, :] = jnp.zeros((tail, 128), F32)
     loads[0].wait()
     lax.fori_loop(0, images, place_low, 0)
-    loads[1].wait()
-    stack_weight(w_one, conv_one_in)
 
     def pack(buffer, sends, corners, rows, step, line, across):
         for side, first in enumerate((8, 5 + across)):
@@ -798,7 +790,8 @@
         around.each(use)
 
     pack(low_x, low_send, low_corner, low_r, h, pitch, w)
-    low_around.start(range(2, 8))
+    greeted(expected)
+    low_around.start()
     skip_around.start(range(2))
 
     def place_skip(b, carry):
@@ -818,18 +811,13 @@
     lax.fori_loop(0, images, place_skip, 0)
     pack(skip_x, skip_send, skip_corner, skip_r, height, wide, breadth)
     skip_around.start(range(2, 8))
+    loads[1].wait()
+    stack_weight(w_one, conv_one_in)
     low_around.wait()
     unpack(low_around, low_x, low_rows, low_recv, low_corner, low_r, h, pitch, w)
 
     def conv_one(b, sums):
         pairs = tap_pairs(low_x, PAD + b * low_r * pitch, low_r * pitch, 0.0)
-        own = pairs.reshape(low_r, pitch, 256)[2 : h + 4, 8 : 8 + w]
-        low_s[b] = own.astype(BF16)
-        lines = jnp.sum(own.astype(BF16).astype(F32), axis=1)
-        tap_sums = [
-            sums[2 + tap] + jnp.sum(lines[tap : tap + h], axis=0, keepdims=True)
-            for tap in range(3)
-        ]
         pairs = pairs.astype(BF16)
         count = y_one_r * pitch
         taps = jnp.concatenate([pairs[pitch * a : pitch * a + count] for a in range(3)], axis=1)
@@ -839,17 +827,42 @@
         return (
             sums[0] + jnp.sum(own, axis=0, keepdims=True),
             sums[1] + jnp.sum(own * own, axis=0, keepdims=True),
-            *tap_sums,
         )
+
+    def own_taps(b, sums):
+        pairs = tap_pairs(low_x, PAD + (b * low_r + 2) * pitch, (h + 2) * pitch, 0.0)
+        own = pairs.reshape(h + 2, pitch, 256)[:, 8 : 8 + w].astype(BF16)
+        low_s[b] = own
+        lines = jnp.sum(own.astype(F32), axis=1)
+        return [
+            sums[tap] + jnp.sum(lines[tap : tap + h], axis=0, keepdims=True) for tap in range(3)
+        ]
 
     def count_ones(b, total):
         ones = (target_in[b].reshape(height * breadth, 80).astype(F32) == 1.0).astype(F32)
         return total + jnp.sum(ones, axis=0, keepdims=True)
 
     nothing = jnp.zeros((1, 128), F32)
-    tap_none = jnp.zeros((1, 256), F32)
-    sums = lax.fori_loop(0, images, conv_one, (nothing, nothing, tap_none, tap_none, tap_none))
-    tap_sums = sums[2:]
+    sums = lax.fori_loop(0, images, conv_one, (nothing, nothing))
+    sum_src = first_scratch[0]
+    sum_src[...] = jnp.zeros((8, 128), F32)
+    sum_src[0:1, :] = sums[0]
+    sum_src[1:2, :] = sums[1]
+    first_total = Total(*first_scratch)
+    first_total.begin()
+    stores = [
+        pltpu.make_async_copy(y_one_s, y_one_out, out_sems.at[0, 0]),
+        pltpu.make_async_copy(low_s, low_out, out_sems.at[0, 1]),
+    ]
+    stores[0].start()
+
+    loads[9].wait()
+    stack_weight(w_two, conv_two_in)
+    skip_around.wait()
+    unpack(
+        skip_around, skip_x, skip_rows, skip_recv, skip_corner, skip_r, height, wide, breadth
+    )
+    first_total.middle()
     for k in (3, 4):
         loads[k].wait()
     ones = lax.fori_loop(0, images, count_ones, jnp.zeros((1, 80), F32))
@@ -864,28 +877,9 @@
             slot < amount, index_in[b : b + 1, :] - base, -(2**30)
         )
     leading = jnp.logical_and(row_at == 0, col_at == 0).astype(F32)
-    sum_src = first_scratch[0]
-    sum_src[...] = jnp.zeros((8, 128), F32)
-    sum_src[0:1, :] = sums[0]
-    sum_src[1:2, :] = sums[1]
-    sum_src[2:3, 0:80] = ones
-    sum_src[3:4, :] = jnp.full((1, 128), objects.astype(F32) * leading)
-    first_total = Total(*first_scratch)
-    first_total.begin()
-    stores = [
-        pltpu.make_async_copy(y_one_s, y_one_out, out_sems.at[0, 0]),
-        pltpu.make_async_copy(low_s, low_out, out_sems.at[0, 1]),
-    ]
-    for store in stores:
-        store.start()
-
-    loads[9].wait()
-    stack_weight(w_two, conv_two_in)
-    skip_around.wait()
-    unpack(
-        skip_around, skip_x, skip_rows, skip_recv, skip_corner, skip_r, height, wide, breadth
-    )
-    first_total.middle()
+    tap_none = jnp.zeros((1, 256), F32)
+    tap_sums = lax.fori_loop(0, images, own_taps, [tap_none] * 3)
+    stores[1].start()
     for k in range(5, 9):
         loads[k].wait()
     totals = first_total.end()
@@ -896,9 +890,6 @@
     stat_out[...] = jnp.zeros((24, 128), F32)
     stat_out[0:1, :] = mean_one
     stat_out[1:2, :] = scale_one
-    positives = jnp.sum(totals[2:3, 0:80], axis=1, keepdims=True)
-    stat_out[4:5, :] = jnp.broadcast_to(1.0 / positives, (1, 128))
-    stat_out[5:6, :] = 0.5 / totals[3:4]
     stat_out[6:7, :] = gain_one
     stat_out[7:8, :] = shift_one
     stat_out[8:9, :] = gain_two
@@ -962,7 +953,9 @@
     row_s[PAD + skip_r * pitch :, :] = jnp.zeros((PAD, 128), F32)
     sums = lax.fori_loop(0, images, conv_two, (nothing, nothing))
     sum_src = second_scratch[0]
-    sum_src[...] = jnp.zeros((8, 128), F32)
+    sum_src[...] = jnp.zeros((16, 128), F32)
+    sum_src[8:9, 0:80] = ones
+    sum_src[9:10, :] = jnp.full((1, 128), objects.astype(F32) * leading)
     sum_src[0:1, :] = sums[0]
     sum_src[1:2, :] = sums[1]
     for tap in range(3):
@@ -983,14 +976,41 @@
         return carry
 
     lax.fori_loop(0, images, normed_taps, 0)
+    tiles_out[36:] = jnp.zeros((tiles_out.shape[0] - 36, 8, 128), F32)
     fold(tiles_out, 0, g_low)
     second_total.middle()
+    for k in (10, 11):
+        loads[k].wait()
+    for tap in range(3):
+        kernel_s[tap, 0:192, :] = (0.5 * head_in[tap].astype(F32)).astype(BF16)
+        kernel_s[tap, 192:256, :] = jnp.zeros((64, 768), BF16)
+    parts = three_parts(0.5 * bias_in[...].reshape(1, 768))
+    which = lax.broadcasted_iota(jnp.int32, (16, 768), 0)
+    filled = jnp.zeros((16, 768), F32)
+    for place_at in range(3):
+        filled = jnp.where(which == place_at, parts[place_at].astype(F32), filled)
+    kernel_s[1, 192:208, :] = filled.astype(BF16)
+    for tap in range(3):
+        for block in range(3):
+            span = slice(256 * block, 256 * block + 256)
+            back_s[span, 256 * tap : 256 * tap + 256] = (
+                kernel_s[tap, :, span].astype(F32).T.astype(BF16)
+            )
+    stores += [
+        pltpu.make_async_copy(kernel_s, kernel_out, out_sems.at[0, 2]),
+        pltpu.make_async_copy(back_s, back_out, out_sems.at[0, 3]),
+    ]
+    for store in stores[2:]:
+        store.start()
     totals = second_total.end()
     mean_two = totals[0:1] / cells_high
     scale_two = lax.rsqrt(totals[1:2] / cells_high - mean_two * mean_two + EPSILON)
     stat_out[2:3, :] = mean_two
     stat_out[3:4, :] = scale_two
     stat_out[16:22, :] = totals[2:8]
+    positives = jnp.sum(totals[8:9, 0:80], axis=1, keepdims=True)
+    stat_out[4:5, :] = jnp.broadcast_to(1.0 / positives, (1, 128))
+    stat_out[5:6, :] = 0.5 / totals[9:10]
 
     for store in stores:
         store.wait()
@@ -1010,6 +1030,8 @@
     gain_two,
     shift_two,
     index,
+    head,
+    bias,
     count,
 ):
     images, h, w, _ = low_map.shape
@@ -1024,11 +1046,13 @@
         jax.ShapeDtypeStruct((images, h + 4, pitch, 128), F32),
         jax.ShapeDtypeStruct((images, height + 2, breadth, 256), BF16),
         jax.ShapeDtypeStruct((images, h + 2, w, 256), BF16),
+        jax.ShapeDtypeStruct((3, 256, 768), BF16),
+        jax.ShapeDtypeStruct((768, 768), BF16),
     ]
     return pl.pallas_call(
         rise_body,
-        in_specs=[hbm] * 10 + [pl.BlockSpec(memory_space=pltpu.SMEM)],
-        out_specs=[hbm] * 4 + [vmem] * 3,
+        in_specs=[hbm] * 12 + [pl.BlockSpec(memory_space=pltpu.SMEM)],
+        out_specs=[hbm] * 6 + [vmem] * 3,
         out_shape=kept
         + [jax.ShapeDtypeStruct((24, 128), F32), jax.ShapeDtypeStruct((8, 128), jnp.int32)]
         + [jax.ShapeDtypeStruct((conv_tiles(36), 8, 128), F32)],
@@ -1040,6 +1064,8 @@
             pltpu.VMEM((3, 192, 64), BF16),
             pltpu.VMEM((4, 1, 64), F32),
             pltpu.VMEM(index.shape, jnp.int32),
+            pltpu.VMEM((3, 192, 768), BF16),
+            pltpu.VMEM((768,), F32),
         ]
         + [pltpu.VMEM(array.shape, array.dtype) for array in kept]
         + [
@@ -1061,9 +1087,9 @@
             pltpu.VMEM((2, 3 * half, rounded_up(height, 16), 128), BF16),
             pltpu.VMEM((2, 4, half, 32, 128), BF16),
             total_scratch(8),
-            total_scratch(8),
-            pltpu.SemaphoreType.DMA((10,)),
-            pltpu.SemaphoreType.DMA((4, max(images, 2))),
+            total_scratch(16),
+            pltpu.SemaphoreType.DMA((12,)),
+            pltpu.SemaphoreType.DMA((4, max(images, 4))),
             pltpu.SemaphoreType.DMA((2, 2, 8)),
         ],
         compiler_params=pltpu.CompilerParams(
@@ -1081,6 +1107,8 @@
         gain_two,
         shift_two,
         index,
+        head,
+        bias,
         count,
     )
 
@@ -1267,8 +1295,6 @@
     target[first + 24 : first + 36] = jnp.where(low, last[0:96], swapped(last[96:192])).reshape(
         12, 8, 128
     )
-    if target.shape[0] > first + 36:
-        target[first + 36 :] = jnp.zeros((target.shape[0] - first - 36, 8, 128), F32)
 
 
 def unfold(source, first):
@@ -1431,7 +1457,7 @@
         for line in (0, ext + 1):
             start = PAD + (b * rows + line) * wide
             grad_x[start : start + wide, :] = jnp.zeros((wide, 128), F32)
-    greet()
+    greeted(greet())
     for b in range(images):
         spread_load(b).wait()
     for pair in range(half):
@@ -1615,6 +1641,8 @@
     gather.begin(1)
     fold(conv_scratch[0], 0, g_two)
     fold(conv_scratch[0], 36, g_one)
+    if conv_out.shape[0] > 72:
+        conv_scratch[0][72:] = jnp.zeros((conv_out.shape[0] - 72, 8, 128), F32)
     conv_sum = PlaneReducer(*conv_scratch[:4], conv_out, conv_scratch[4])
     conv_sum.begin()
     for pair in range(half):
@@ -1938,7 +1966,7 @@
     devices = batches * rows * cols
     conv_one = conv_first.reshape(3, 192, 64)
     conv_two = conv_second.reshape(3, 192, 64)
-    y_two, y_one, merged, low, stats, spot, tiles_x = rise(
+    y_two, y_one, merged, low, kernel, back, stats, spot, tiles_x = rise(
         low_map,
         skip_map,
         heat_target,
@@ -1949,6 +1977,8 @@
         gain_second.reshape(1, 64),
         shift_second.reshape(1, 64),
         obj_index,
+        head_conv.reshape(3, 192, 768),
+        head_bias,
         obj_count,
     )
     heat_map, box_map, spread, load, small = heads(
@@ -1957,8 +1987,8 @@
         spot,
         box_target.transpose(0, 2, 1),
         stats,
-        head_conv.reshape(3, 192, 768),
-        head_bias,
+        kernel,
+        back,
         heat_weight.T,
         heat_bias.reshape(1, 80),
         box_weight.transpose(0, 2, 1),

time: 117 us -> 116 us (level)
  no operation moved by 1% of the time
where the time goes in v4:
time: 116 us
  Pallas kernels  115 us (99%)
    pallas_call x1, Pallas kernels, fall(): pl.pallas_call(fall_body, in_specs=[hbm] * 2 + [vmem, hbm, vmem] + [hbm]...  45.5 us
    pallas_call x1, Pallas kernels, rise(): pl.pallas_call(rise_body, in_specs=[hbm] * 12 + [pl.BlockSpec(memory_spac...  34.1 us
    pallas_call x1, Pallas kernels, heads(): pl.pallas_call(functools.partial(heads_body, chunks, breadth * lax.axis_s...  29.9 us
    pallas_call x1, Pallas kernels, finish(): pl.pallas_call(functools.partial(finish_body, cells), grid=(steps,), in_s...  5.22 us

profile of v4, /device:TPU:0, one launch (start us, length us, event | category | flops | bytes accessed | tf_op | source)
XLA Modules:
  0.0 115.5 jit_solution(8618097855357723929)
XLA Ops:
  0.6 34.1 %rise.1 = (f32[4,36,48,128]{3,2,1,0:T(8,128)}, f32[4,20,32,128]{3,2,1,0:T(8,128)}, bf16[4,34,32,256]{3,2,1,0:T(8,128)(2,1)}, bf16[4,18,16,256]{3,2,1,0:T(8,128)(...) custom-call(bf16[4,16,16,64]{3,2,1,0:T(8,128)(2,1)} %low_ref.1, ...), custom_call_target="tpu_custom_call" | custom-call | tf_op jit(solution)/shard_map/rise/pallas_call | solution.py:1052
  34.8 29.9 %heads.1 = (f32[4,32,32,80]{3,2,1,0:T(8,128)}, f32[4,32,4,32]{3,2,1,0:T(4,128)}, f32[4,34,48,128]{3,2,1,0:T(8,128)}, bf16[256,16,128]{2,1,0:T(8,128)(2,1)}, f32[8,128]{1,0:T(8,128)}) custom-call(f32[4,36,48,128]{3,2,1,0:T(8,128)} %get-tuple-element.52.y_two_ref, bf16[4,32,32,80]{3,2,1,0:T(8,128)(2,1)} %target_ref.3, s32[8,128]{1,0:T(8,128)} %get-tuple-element.53.spot_ref, ...), custom_call_target="tpu_custom_call" | custom-call | flops 10871635968 | bytes 12582912 | tf_op jit(solution)/shard_map/heads/pallas_call | solution.py:229
  64.6 45.5 %fall.1 = (f32[4,32,32,64]{3,2,1,0:T(8,128)}, f32[4,576,128]{2,1,0:T(8,128)}, bf16[256,16,128]{2,1,0:T(8,128)(2,1)}, f32[72,8,128]{2,1,0:T(8,128)}, f32[40,8,128...) custom-call(f32[4,1632,128]{2,1,0:T(8,128)} %bitcast.20, ...), custom_call_target="tpu_custom_call" | custom-call | tf_op jit(solution)/shard_map/fall/pallas_call | solution.py:1737
  110.1 5.2 %finish.1 = (f32[3,3,64,64]{3,2,1,0:T(8,128)}, f32[1,64]{1,0:T(1,128)}, f32[1,64]{1,0:T(1,128)}, f32[3,3,64,64]{3,2,1,0:T(8,128)}, f32[1,64]{1,0:T(1,128)}, /*in...) custom-call(bf16[256,16,128]{2,1,0:T(8,128)(2,1)} %get-tuple-element, ...), custom_call_target="tpu_custom_call" | custom-call | tf_op jit(solution)/shard_map/finish/pallas_call | solution.py:1921

commit v5 on v4

--- a/solution.py
+++ b/solution.py
@@ -106,44 +106,28 @@
         for place, part in enumerate(three_parts(goal_ref[0])):
             goal_s[place] = part
 
-    first = chunk * rows
     taps = jnp.concatenate(
-        [taps_ref[pl.ds(first + tap, rows)].reshape(cells, 256) for tap in range(3)], axis=1
+        [taps_ref[tap : tap + rows].reshape(cells, 256) for tap in range(3)], axis=1
     )
-    active, slope = [], []
-    for block in range(3):
+    active, slope = {}, {}
+
+    def forward(block):
         weight = kernel_s[:, :, block * units : (block + 1) * units].reshape(768, units)
         hidden = dot(taps, weight)
         turn = jnp.tanh(hidden)
         above = 1.0 + turn
         product = hidden * above
-        active.append(product.astype(BF16))
-        slope.append(above + product * (1.0 - turn))
-
-    logit = dot_keep(active[0], heat_w_ref[...]) + heat_b_ref[...]
-    decay = jnp.exp(-jnp.abs(logit))
-    large = 1.0 / (1.0 + decay)
-    small = decay * large
-    above = logit >= 0.0
-    chance = jnp.where(above, large, small)
-    heat_out[0] = chance.reshape(rows, breadth, 80)
-    target = target_ref[0].reshape(cells, 80).astype(F32)
-    positive = target == 1.0
-    side = jnp.where(positive, jnp.where(above, small, large), chance)
-    value = jnp.where(positive, -logit, logit)
-    soft = jnp.maximum(value, 0.0) + jnp.log(1.0 + decay)
-    slant = side * side * (2.0 * (1.0 - side) * soft + side)
-    gap = 1.0 - target
-    gap = gap * gap
-    weighting = jnp.where(positive, -1.0, gap * gap) * stat_ref[4:5, 0:80]
-    logit_grad = weighting * slant
-    logit_low = logit_grad.astype(BF16)
-
+        active[block] = product.astype(BF16)
+        slope[block] = above + product * (1.0 - turn)
+
+    forward(1)
+    forward(2)
     box_bias = jnp.concatenate([box_b_ref[0:1, :], box_b_ref[1:2, :]], axis=1)
     boxes = dot_keep(active[1], box_s[0]) + dot_keep(active[2], box_s[1]) + box_bias
+    forward(0)
     box_out[0] = jnp.swapaxes(boxes.reshape(rows, breadth, 4), 1, 2)
     shape = (rows, breadth, 128)
-    cell = (first + lax.broadcasted_iota(jnp.int32, shape, 0)) * map_side
+    cell = lax.broadcasted_iota(jnp.int32, shape, 0) * map_side
     cell = (cell + lax.broadcasted_iota(jnp.int32, shape, 1)).reshape(cells, 128)
     chosen = (cell == spot_ref[pl.ds(image, 1), :]).astype(F32).astype(BF16)
     goals = dot_keep(chosen, goal_s[0]) + dot_keep(chosen, goal_s[1])
@@ -152,45 +136,68 @@
     miss = boxes - goals
     lane = lax.broadcasted_iota(jnp.int32, (1, 4), 1)
     factor = jnp.where(lane < 2, 0.1, 1.0) * stat_ref[5:6, 0:4]
-    box_grad = hit * factor * miss * lax.rsqrt(miss * miss + 1.0)
-    box_low = box_grad.astype(BF16)
-
-    heat_sum_s[...] += jnp.sum(logit_low.astype(F32).reshape(cells // 8, 8, 80), axis=0)
+    box_low = (hit * factor * miss * lax.rsqrt(miss * miss + 1.0)).astype(BF16)
     box_sum_s[...] += jnp.sum(box_low.astype(F32).reshape(cells // 8, 8, 4), axis=0)
-    heat_grad_s[...] += dot_left(logit_low, active[0])
+    hidden_low = {}
     for part in range(2):
         box_grad_s[part] += dot_left(box_low, active[1 + part])
-
-    back = [
-        dot(logit_low, heat_w_ref[...]),
-        dot(box_low, box_s[0]),
-        dot(box_low, box_s[1]),
-    ]
-    grad_hidden = jnp.concatenate(
-        [(back[block] * slope[block]).astype(BF16) for block in range(3)], axis=1
-    )
+        back = dot(box_low, box_s[part])
+        hidden_low[1 + part] = (back * slope[1 + part]).astype(BF16)
+    boxes_low = jnp.concatenate([hidden_low[1], hidden_low[2]], axis=1)
+    logits = dot_keep(active[0], heat_w_ref[...]) + heat_b_ref[...]
+    piece_rows = rows // 4
+    piece_cells = piece_rows * breadth
+
+    def focal(piece):
+        lines = slice(piece_rows * piece, piece_rows * piece + piece_rows)
+        logit = logits[piece_cells * piece : piece_cells * piece + piece_cells]
+        decay = jnp.exp(-jnp.abs(logit))
+        large = 1.0 / (1.0 + decay)
+        small = decay * large
+        above = logit >= 0.0
+        chance = jnp.where(above, large, small)
+        heat_out[0, lines] = chance.reshape(piece_rows, breadth, 80)
+        target = target_ref[0, lines].reshape(piece_cells, 80).astype(F32)
+        positive = target == 1.0
+        side = jnp.where(positive, jnp.where(above, small, large), chance)
+        value = jnp.where(positive, -logit, logit)
+        soft = jnp.maximum(value, 0.0) + jnp.log(1.0 + decay)
+        slant = side * side * (2.0 * (1.0 - side) * soft + side)
+        gap = 1.0 - target
+        gap = gap * gap
+        weighting = jnp.where(positive, -1.0, gap * gap) * stat_ref[4:5, 0:80]
+        return (weighting * slant).astype(BF16)
+
+    turned = [taps[:, 256 * tap : 256 * tap + 256].T for tap in range(3)]
+    pieces = []
+    for tap in range(3):
+        grad_s[tap, :, 256:768] += dot(turned[tap], boxes_low)
+        if tap < 2:
+            pieces += [focal(2 * tap), focal(2 * tap + 1)]
+    logit_low = jnp.concatenate(pieces, axis=0)
+    heat_sum_s[...] += jnp.sum(logit_low.astype(F32).reshape(cells // 8, 8, 80), axis=0)
+    heat_grad_s[...] += dot_left(logit_low, active[0])
+    hidden_low[0] = (dot(logit_low, heat_w_ref[...]) * slope[0]).astype(BF16)
+    grad_hidden = jnp.concatenate([hidden_low[0], boxes_low], axis=1)
     spread = []
     for tap in range(3):
         part = dot(grad_hidden, back_s[:, 256 * tap : 256 * tap + 256])
         spread.append(part.reshape(rows, breadth, 256))
     inner = slice(16, 16 + breadth)
-    wide_s[pl.ds(first, 1), inner, :] += spread[0][0:1]
-    wide_s[pl.ds(first + 1, 1), inner, :] += spread[0][1:2] + spread[1][0:1]
-    wide_s[pl.ds(first + 2, rows - 2), inner, :] = (
-        spread[0][2:] + spread[1][1:-1] + spread[2][:-2]
-    )
-    wide_s[pl.ds(first + rows, 1), inner, :] = spread[1][-1:] + spread[2][-2:-1]
-    wide_s[pl.ds(first + rows + 1, 1), inner, :] = spread[2][-1:]
+    wide_s[0:1, inner, :] = spread[0][0:1]
+    wide_s[1:2, inner, :] = spread[0][1:2] + spread[1][0:1]
+    wide_s[2:rows, inner, :] = spread[0][2:] + spread[1][1:-1] + spread[2][:-2]
+    wide_s[rows : rows + 1, inner, :] = spread[1][-1:] + spread[2][-2:-1]
+    wide_s[rows + 1 : rows + 2, inner, :] = spread[2][-1:]
+    reach, ends = breadth + 16, [(rows + 2) * k // 3 for k in range(4)]
     for tap in range(3):
-        grad_s[tap] += dot_left(taps[:, 256 * tap : 256 * tap + 256], grad_hidden)
-
-    @pl.when(chunk == chunks - 1)
-    def _():
-        reach = breadth + 16
-        centre = pltpu.roll(wide_s[:, 8 : 8 + reach, 0:128], 64, 2)
-        total = wide_s[:, 9 : 9 + reach, 0:128] + centre + wide_s[:, 7 : 7 + reach, 128:256]
+        grad_s[tap, :, 0:256] += dot(turned[tap], hidden_low[0])
+        lines = slice(ends[tap], ends[tap + 1])
+        centre = pltpu.roll(wide_s[lines, 8 : 8 + reach, 0:128], 64, 2)
+        total = wide_s[lines, 9 : 9 + reach, 0:128] + centre
+        total = total + wide_s[lines, 7 : 7 + reach, 128:256]
         lanes = lax.broadcasted_iota(jnp.int32, total.shape, 2)
-        spread_out[0] = jnp.where(lanes < 64, total, pltpu.roll(total, 64, 2))
+        spread_out[0, lines] = jnp.where(lanes < 64, total, pltpu.roll(total, 64, 2))
 
     @pl.when(jnp.logical_and(image == pl.num_programs(0) - 1, chunk == chunks - 1))
     def _():

time: 116 us -> 120 us (1.034)
  Pallas kernels: 115 us -> 119 us
    pallas_call x1, Pallas kernels: 29.9 us -> 33.9 us  [heads(): pl.pallas_call(functools.partial(heads_body, chunks, breadth * lax.axis_s...]
where the time goes in v5:
time: 120 us
  Pallas kernels  119 us (99%)
    pallas_call x1, Pallas kernels, fall(): pl.pallas_call(fall_body, in_specs=[hbm] * 2 + [vmem, hbm, vmem] + [hbm]...  45.5 us
    pallas_call x1, Pallas kernels, rise(): pl.pallas_call(rise_body, in_specs=[hbm] * 12 + [pl.BlockSpec(memory_spac...  34.1 us
    pallas_call x1, Pallas kernels, heads(): pl.pallas_call(functools.partial(heads_body, chunks, breadth * lax.axis_s...  33.9 us
    pallas_call x1, Pallas kernels, finish(): pl.pallas_call(functools.partial(finish_body, cells), grid=(steps,), in_s...  5.22 us

profile of v5, /device:TPU:0, one launch (start us, length us, event | category | flops | bytes accessed | tf_op | source)
XLA Modules:
  0.0 119.6 jit_solution(11719550073235870480)
XLA Ops:
  0.6 34.1 %rise.1 = (f32[4,36,48,128]{3,2,1,0:T(8,128)}, f32[4,20,32,128]{3,2,1,0:T(8,128)}, bf16[4,34,32,256]{3,2,1,0:T(8,128)(2,1)}, bf16[4,18,16,256]{3,2,1,0:T(8,128)(...) custom-call(bf16[4,16,16,64]{3,2,1,0:T(8,128)(2,1)} %low_ref.1, ...), custom_call_target="tpu_custom_call" | custom-call | tf_op jit(solution)/shard_map/rise/pallas_call | solution.py:1059
  34.8 33.9 %heads.1 = (f32[4,32,32,80]{3,2,1,0:T(8,128)}, f32[4,32,4,32]{3,2,1,0:T(4,128)}, f32[4,34,48,128]{3,2,1,0:T(8,128)}, bf16[256,16,128]{2,1,0:T(8,128)(2,1)}, f32[8,128]{1,0:T(8,128)}) custom-call(f32[4,36,48,128]{3,2,1,0:T(8,128)} %get-tuple-element.52.y_two_ref, bf16[4,32,32,80]{3,2,1,0:T(8,128)(2,1)} %target_ref.3, s32[8,128]{1,0:T(8,128)} %get-tuple-element.53.spot_ref, ...), custom_call_target="tpu_custom_call" | custom-call | flops 10871635968 | bytes 12582912 | tf_op jit(solution)/shard_map/heads/pallas_call | solution.py:236
  68.7 45.5 %fall.1 = (f32[4,32,32,64]{3,2,1,0:T(8,128)}, f32[4,576,128]{2,1,0:T(8,128)}, bf16[256,16,128]{2,1,0:T(8,128)(2,1)}, f32[72,8,128]{2,1,0:T(8,128)}, f32[40,8,128...) custom-call(f32[4,1632,128]{2,1,0:T(8,128)} %bitcast.20, ...), custom_call_target="tpu_custom_call" | custom-call | tf_op jit(solution)/shard_map/fall/pallas_call | solution.py:1744
  114.2 5.2 %finish.1 = (f32[3,3,64,64]{3,2,1,0:T(8,128)}, f32[1,64]{1,0:T(1,128)}, f32[1,64]{1,0:T(1,128)}, f32[3,3,64,64]{3,2,1,0:T(8,128)}, f32[1,64]{1,0:T(1,128)}, /*in...) custom-call(bf16[256,16,128]{2,1,0:T(8,128)(2,1)} %get-tuple-element, ...), custom_call_target="tpu_custom_call" | custom-call | tf_op jit(solution)/shard_map/finish/pallas_call | solution.py:1928

commit v6 on v4

--- a/solution.py
+++ b/solution.py
@@ -146,9 +146,11 @@
     cell = (first + lax.broadcasted_iota(jnp.int32, shape, 0)) * map_side
     cell = (cell + lax.broadcasted_iota(jnp.int32, shape, 1)).reshape(cells, 128)
     chosen = (cell == spot_ref[pl.ds(image, 1), :]).astype(F32).astype(BF16)
-    goals = dot_keep(chosen, goal_s[0]) + dot_keep(chosen, goal_s[1])
-    goals = goals + dot_keep(chosen, goal_s[2])
-    hit = dot(chosen, jnp.ones((128, 4), BF16))
+    twofold = jnp.concatenate([chosen, chosen], axis=1)
+    goals = dot_keep(twofold, jnp.concatenate([goal_s[0], goal_s[1]], axis=1))
+    ends = jnp.concatenate([goal_s[2].astype(F32), jnp.ones((4, 128), F32)], axis=0)
+    both = dot_keep(chosen, ends.astype(BF16))
+    goals, hit = goals + both[:, 0:4], both[:, 4:8]
     miss = boxes - goals
     lane = lax.broadcasted_iota(jnp.int32, (1, 4), 1)
     factor = jnp.where(lane < 2, 0.1, 1.0) * stat_ref[5:6, 0:4]

time: 116 us -> 117 us (level)
  no operation moved by 1% of the time
where the time goes in v6:
time: 117 us
  Pallas kernels  116 us (99%)
    pallas_call x1, Pallas kernels, fall(): pl.pallas_call(fall_body, in_specs=[hbm] * 2 + [vmem, hbm, vmem] + [hbm]...  45.5 us
    pallas_call x1, Pallas kernels, rise(): pl.pallas_call(rise_body, in_specs=[hbm] * 12 + [pl.BlockSpec(memory_spac...  34.1 us
    pallas_call x1, Pallas kernels, heads(): pl.pallas_call(functools.partial(heads_body, chunks, breadth * lax.axis_s...  30.9 us
    pallas_call x1, Pallas kernels, finish(): pl.pallas_call(functools.partial(finish_body, cells), grid=(steps,), in_s...  5.22 us

profile of v6, /device:TPU:0, one launch (start us, length us, event | category | flops | bytes accessed | tf_op | source)
XLA Modules:
  0.0 116.6 jit_solution(2213191283529425463)
XLA Ops:
  0.6 34.1 %rise.1 = (f32[4,36,48,128]{3,2,1,0:T(8,128)}, f32[4,20,32,128]{3,2,1,0:T(8,128)}, bf16[4,34,32,256]{3,2,1,0:T(8,128)(2,1)}, bf16[4,18,16,256]{3,2,1,0:T(8,128)(...) custom-call(bf16[4,16,16,64]{3,2,1,0:T(8,128)(2,1)} %low_ref.1, ...), custom_call_target="tpu_custom_call" | custom-call | tf_op jit(solution)/shard_map/rise/pallas_call | solution.py:1054
  34.8 30.9 %heads.1 = (f32[4,32,32,80]{3,2,1,0:T(8,128)}, f32[4,32,4,32]{3,2,1,0:T(4,128)}, f32[4,34,48,128]{3,2,1,0:T(8,128)}, bf16[256,16,128]{2,1,0:T(8,128)(2,1)}, f32[8,128]{1,0:T(8,128)}) custom-call(f32[4,36,48,128]{3,2,1,0:T(8,128)} %get-tuple-element.52.y_two_ref, bf16[4,32,32,80]{3,2,1,0:T(8,128)(2,1)} %target_ref.3, s32[8,128]{1,0:T(8,128)} %get-tuple-element.53.spot_ref, ...), custom_call_target="tpu_custom_call" | custom-call | flops 10871635968 | bytes 12582912 | tf_op jit(solution)/shard_map/heads/pallas_call | solution.py:231
  65.7 45.5 %fall.1 = (f32[4,32,32,64]{3,2,1,0:T(8,128)}, f32[4,576,128]{2,1,0:T(8,128)}, bf16[256,16,128]{2,1,0:T(8,128)(2,1)}, f32[72,8,128]{2,1,0:T(8,128)}, f32[40,8,128...) custom-call(f32[4,1632,128]{2,1,0:T(8,128)} %bitcast.20, ...), custom_call_target="tpu_custom_call" | custom-call | tf_op jit(solution)/shard_map/fall/pallas_call | solution.py:1739
  111.2 5.2 %finish.1 = (f32[3,3,64,64]{3,2,1,0:T(8,128)}, f32[1,64]{1,0:T(1,128)}, f32[1,64]{1,0:T(1,128)}, f32[3,3,64,64]{3,2,1,0:T(8,128)}, f32[1,64]{1,0:T(1,128)}, /*in...) custom-call(bf16[256,16,128]{2,1,0:T(8,128)(2,1)} %get-tuple-element, ...), custom_call_target="tpu_custom_call" | custom-call | tf_op jit(solution)/shard_map/finish/pallas_call | solution.py:1923
